TPU v7x, 32 devices: a whole 2x2x4 slice. The times are simulated.
32 devices in a mesh: dp: 16 (over z, y, x), tensor: 2 (over core).
Axes of the slice: x: 2, y: 2, z: 4, core: 2. Of those that a mesh axis runs over, the one named last changes fastest.
Arguments:
- inputs: bfloat16 [4096, 2560], P(('dp', 'tensor')), may hold values from -6 to 6
- gain_mix: bfloat16 [2560], P('dp'), may hold values from 0.099609375 to 1.8984375
- gain_mlp: bfloat16 [2560], P('dp'), may hold values from 0.099609375 to 1.8984375
- branch_x: bfloat16 [2560, 2560], P('dp', 'tensor'), may hold values from -0.125 to 0.125
- branch_y: bfloat16 [2560, 2560], P('dp', 'tensor'), may hold values from -0.125 to 0.125
- conv_taps: bfloat16 [4, 2560], P(None, ('tensor', 'dp')), may hold values from -3 to 3
- conv_bias: bfloat16 [2560], P(('tensor', 'dp')), may hold values from -3 to 3
- gate_a: bfloat16 [10, 256, 256], P('tensor', 'dp'), may hold values from -0.375 to 0.375
- bias_a: bfloat16 [2560], P(('tensor', 'dp')), may hold values from -4 to 4
- gate_in: bfloat16 [10, 256, 256], P('tensor', 'dp'), may hold values from -0.375 to 0.375
- bias_in: bfloat16 [2560], P(('tensor', 'dp')), may hold values from -4 to 4
- decay_param: bfloat16 [2560], P(('tensor', 'dp')), may hold values from -9 to -4.5
- out_proj: bfloat16 [2560, 2560], P('tensor', 'dp'), may hold values from -0.5 to 0.5
- ffn_gate: bfloat16 [2560, 7680], P('dp', 'tensor'), may hold values from -0.125 to 0.125
- ffn_up: bfloat16 [2560, 7680], P('dp', 'tensor'), may hold values from -0.125 to 0.125
- ffn_down: bfloat16 [7680, 2560], P('tensor', 'dp'), may hold values from -0.125 to 0.125
- cotangent: bfloat16 [4096, 2560], P(('dp', 'tensor')), may hold values from -6 to 6
Outputs:
- result: bfloat16 [4096, 2560], P(('dp', 'tensor'))
- grad_inputs: float32 [4096, 2560], P(('dp', 'tensor'))
- grad_gain_mix: float32 [2560], P(('dp', 'tensor'))
- grad_gain_mlp: float32 [2560], P(('dp', 'tensor'))
- grad_branch_x: float32 [2560, 2560], P('dp', 'tensor')
- grad_branch_y: float32 [2560, 2560], P('dp', 'tensor')
- grad_conv_taps: float32 [4, 2560], P(None, ('tensor', 'dp'))
- grad_conv_bias: float32 [2560], P(('tensor', 'dp'))
- grad_gate_a: float32 [10, 256, 256], P('tensor', 'dp')
- grad_bias_a: float32 [2560], P(('tensor', 'dp'))
- grad_gate_in: float32 [10, 256, 256], P('tensor', 'dp')
- grad_bias_in: float32 [2560], P(('tensor', 'dp'))
- grad_decay_param: float32 [2560], P(('tensor', 'dp'))
- grad_out_proj: float32 [2560, 2560], P('tensor', 'dp')
- grad_ffn_gate: float32 [2560, 7680], P('dp', 'tensor')
- grad_ffn_up: float32 [2560, 7680], P('dp', 'tensor')
- grad_ffn_down: float32 [7680, 2560], P('tensor', 'dp')
All inputs are finite; a program needn't handle non-finite values.
Results may differ from a plain program's by a relative error of at most 0.009.
Values may be sent and summed in bfloat16 or wider, within the bound.
No kernel may reach another device: no remote copies, remote signals or barrier semaphores. Data moves between devices by JAX's collectives and lax.ppermute only.
A program may use at most 384 MiB of HBM per device.

v0:
```python
import jax
import jax.numpy as jnp
from jax import lax
from jax.sharding import PartitionSpec as P

EPSILON = 1e-06


def scale_norm(values, gain):
    return values * lax.rsqrt(jnp.mean(values * values, axis=-1, keepdims=True) + EPSILON) * gain


def convolve(values, taps, bias):
    width = taps.shape[0]
    length = values.shape[0]
    padded = jnp.pad(values, ((width - 1, 0), (0, 0)))
    total = jnp.zeros_like(values) + bias
    for shift_by in range(width):
        total = (
            total + taps[shift_by] * padded[width - 1 - shift_by : width - 1 - shift_by + length]
        )
    return total


def lru_terms(pre_a, pre_i, decay_param, conv_out):
    rate = jax.nn.sigmoid(pre_a)
    entry = jax.nn.sigmoid(pre_i)
    log_decay = -8.0 * jax.nn.softplus(decay_param) * rate
    decay = jnp.exp(log_decay)
    driven = jnp.sqrt(-jnp.expm1(2.0 * log_decay)) * (entry * conv_out)
    return (decay, driven)


def combine(earlier, later):
    return (earlier[0] * later[0], later[0] * earlier[1] + later[1])


def linear_scan(decay, driven):
    return lax.associative_scan(combine, (decay, driven), axis=0)[1]


def contract_last(left, right):
    return lax.dot_general(
        left, right, (((1,), (1,)), ((), ())), preferred_element_type=jnp.float32
    )


def contract_first(left, right):
    return lax.dot_general(
        left, right, (((0,), (0,)), ((), ())), preferred_element_type=jnp.float32
    )


def fetch_mixer(
    gain_mix,
    gain_mlp,
    branch_x,
    branch_y,
    conv_taps,
    conv_bias,
    gate_a,
    bias_a,
    gate_in,
    bias_in,
    decay_param,
    out_proj,
):
    return (
        lax.all_gather(gain_mix, "dp", axis=0, tiled=True),
        lax.all_gather(gain_mlp, "dp", axis=0, tiled=True),
        lax.all_gather(branch_x, "dp", axis=0, tiled=True),
        lax.all_gather(branch_y, "dp", axis=0, tiled=True),
        lax.all_gather(conv_taps, "dp", axis=1, tiled=True),
        lax.all_gather(conv_bias, "dp", axis=0, tiled=True),
        lax.all_gather(gate_a, "dp", axis=1, tiled=True),
        lax.all_gather(bias_a, "dp", axis=0, tiled=True),
        lax.all_gather(gate_in, "dp", axis=1, tiled=True),
        lax.all_gather(bias_in, "dp", axis=0, tiled=True),
        lax.all_gather(decay_param, "dp", axis=0, tiled=True),
        lax.all_gather(out_proj, "dp", axis=1, tiled=True),
    )


def fetch_ffn(ffn_gate, ffn_up, ffn_down):
    return (
        lax.all_gather(ffn_gate, "dp", axis=0, tiled=True),
        lax.all_gather(ffn_up, "dp", axis=0, tiled=True),
        lax.all_gather(ffn_down, "dp", axis=1, tiled=True),
    )


def local(
    inputs,
    gain_mix,
    gain_mlp,
    branch_x,
    branch_y,
    conv_taps,
    conv_bias,
    gate_a,
    bias_a,
    gate_in,
    bias_in,
    decay_param,
    out_proj,
    ffn_gate,
    ffn_up,
    ffn_down,
    cotangent,
):
    fetched = fetch_mixer(
        gain_mix,
        gain_mlp,
        branch_x,
        branch_y,
        conv_taps,
        conv_bias,
        gate_a,
        bias_a,
        gate_in,
        bias_in,
        decay_param,
        out_proj,
    )
    (
        full_gain_mix,
        full_gain_mlp,
        full_branch_x,
        full_branch_y,
        full_taps,
        full_conv_bias,
        full_gate_a,
        full_bias_a,
        full_gate_in,
        full_bias_in,
        full_decay,
        full_out_proj,
    ) = fetched
    rows = inputs.astype(jnp.float32)
    normed_rows, norm_pull = jax.vjp(scale_norm, rows, full_gain_mix.astype(jnp.float32))
    normed = lax.all_gather(normed_rows.astype(jnp.bfloat16), "tensor", axis=0, tiled=True)
    pre_x = jnp.dot(normed, full_branch_x, preferred_element_type=jnp.float32)
    pre_y = jnp.dot(normed, full_branch_y, preferred_element_type=jnp.float32)
    gated_y, gelu_pull = jax.vjp(jax.nn.gelu, pre_y)
    conv_out, conv_pull = jax.vjp(
        convolve, pre_x, full_taps.astype(jnp.float32), full_conv_bias.astype(jnp.float32)
    )
    length = conv_out.shape[0]
    channels = conv_out.shape[1]
    heads = full_gate_a.shape[0]
    block = full_gate_a.shape[2]
    rounded = conv_out.astype(jnp.bfloat16).reshape(length, heads, block)
    pre_a = jnp.einsum(
        "thd,hde->the", rounded, full_gate_a, preferred_element_type=jnp.float32
    ).reshape(length, channels) + full_bias_a.astype(jnp.float32)
    pre_i = jnp.einsum(
        "thd,hde->the", rounded, full_gate_in, preferred_element_type=jnp.float32
    ).reshape(length, channels) + full_bias_in.astype(jnp.float32)
    (decay, driven), lru_pull = jax.vjp(
        lru_terms, pre_a, pre_i, full_decay.astype(jnp.float32), conv_out
    )
    states = linear_scan(decay, driven)
    mixed = (states * gated_y).astype(jnp.bfloat16)
    branch_out = lax.psum_scatter(
        jnp.dot(mixed, full_out_proj, preferred_element_type=jnp.float32),
        "tensor",
        scatter_dimension=0,
        tiled=True,
    )
    resid = rows + branch_out
    normed_two_rows, norm_two_pull = jax.vjp(scale_norm, resid, full_gain_mlp.astype(jnp.float32))
    normed_two = lax.all_gather(normed_two_rows.astype(jnp.bfloat16), "tensor", axis=0, tiled=True)
    full_ffn_gate, full_ffn_up, full_ffn_down = fetch_ffn(ffn_gate, ffn_up, ffn_down)
    gate_pre = jnp.dot(normed_two, full_ffn_gate, preferred_element_type=jnp.float32)
    up_pre = jnp.dot(normed_two, full_ffn_up, preferred_element_type=jnp.float32)
    gate_act, gate_pull = jax.vjp(jax.nn.gelu, gate_pre)
    hidden = (gate_act * up_pre).astype(jnp.bfloat16)
    ffn_out = lax.psum_scatter(
        jnp.dot(hidden, full_ffn_down, preferred_element_type=jnp.float32),
        "tensor",
        scatter_dimension=0,
        tiled=True,
    )
    result = (resid + ffn_out).astype(jnp.bfloat16)
    upstream = lax.all_gather(cotangent, "tensor", axis=0, tiled=True)
    full_ffn_gate, full_ffn_up, full_ffn_down = fetch_ffn(ffn_gate, ffn_up, ffn_down)
    grad_hidden = contract_last(upstream, full_ffn_down)
    grad_down = contract_first(hidden, upstream)
    grad_gate_pre = gate_pull(grad_hidden * up_pre)[0].astype(jnp.bfloat16)
    grad_up_pre = (grad_hidden * gate_act).astype(jnp.bfloat16)
    grad_gate_weight = contract_first(normed_two, grad_gate_pre)
    grad_up_weight = contract_first(normed_two, grad_up_pre)
    ffn_grads = (
        lax.psum_scatter(grad_gate_weight, "dp", scatter_dimension=0, tiled=True),
        lax.psum_scatter(grad_up_weight, "dp", scatter_dimension=0, tiled=True),
        lax.psum_scatter(grad_down, "dp", scatter_dimension=1, tiled=True),
    )
    grad_normed_two = lax.psum_scatter(
        contract_last(grad_gate_pre, full_ffn_gate) + contract_last(grad_up_pre, full_ffn_up),
        "tensor",
        scatter_dimension=0,
        tiled=True,
    )
    grad_resid_norm, grad_gain_two = norm_two_pull(grad_normed_two)
    grad_resid = cotangent.astype(jnp.float32) + grad_resid_norm
    back_rows = lax.all_gather(grad_resid.astype(jnp.bfloat16), "tensor", axis=0, tiled=True)
    fetched = fetch_mixer(
        gain_mix,
        gain_mlp,
        branch_x,
        branch_y,
        conv_taps,
        conv_bias,
        gate_a,
        bias_a,
        gate_in,
        bias_in,
        decay_param,
        out_proj,
    )
    full_branch_x = fetched[2]
    full_branch_y = fetched[3]
    full_gate_a = fetched[6]
    full_gate_in = fetched[8]
    full_out_proj = fetched[11]
    grad_mixed = contract_last(back_rows, full_out_proj)
    grad_out_weight = contract_first(mixed, back_rows)
    grad_states = grad_mixed * gated_y
    grad_pre_y = gelu_pull(grad_mixed * states)[0].astype(jnp.bfloat16)
    next_decay = jnp.concatenate([decay[1:], jnp.zeros_like(decay[:1])], axis=0)
    grad_driven = jnp.flip(linear_scan(jnp.flip(next_decay, 0), jnp.flip(grad_states, 0)), 0)
    prior_states = jnp.concatenate([jnp.zeros_like(states[:1]), states[:-1]], axis=0)
    grad_decay = grad_driven * prior_states
    grad_pre_a, grad_pre_i, grad_decay_raw, grad_conv_direct = lru_pull((grad_decay, grad_driven))
    rounded_grad_a = grad_pre_a.astype(jnp.bfloat16)
    rounded_grad_i = grad_pre_i.astype(jnp.bfloat16)
    blocks_grad_a = rounded_grad_a.reshape(length, heads, block)
    blocks_grad_i = rounded_grad_i.reshape(length, heads, block)
    grad_rounded = jnp.einsum(
        "the,hde->thd", blocks_grad_a, full_gate_a, preferred_element_type=jnp.float32
    ) + jnp.einsum("the,hde->thd", blocks_grad_i, full_gate_in, preferred_element_type=jnp.float32)
    grad_gate_a_weight = jnp.einsum(
        "thd,the->hde", rounded, blocks_grad_a, preferred_element_type=jnp.float32
    )
    grad_gate_in_weight = jnp.einsum(
        "thd,the->hde", rounded, blocks_grad_i, preferred_element_type=jnp.float32
    )
    grad_bias_a_vec = jnp.sum(rounded_grad_a.astype(jnp.float32), axis=0)
    grad_bias_in_vec = jnp.sum(rounded_grad_i.astype(jnp.float32), axis=0)
    grad_conv = grad_conv_direct + grad_rounded.reshape(length, channels)
    grad_pre_x, grad_taps, grad_conv_bias_vec = conv_pull(grad_conv)
    grad_pre_x = grad_pre_x.astype(jnp.bfloat16)
    grad_x_weight = contract_first(normed, grad_pre_x)
    grad_y_weight = contract_first(normed, grad_pre_y)
    mixer_grads = (
        lax.psum_scatter(grad_x_weight, "dp", scatter_dimension=0, tiled=True),
        lax.psum_scatter(grad_y_weight, "dp", scatter_dimension=0, tiled=True),
        lax.psum_scatter(grad_taps, "dp", scatter_dimension=1, tiled=True),
        lax.psum_scatter(grad_conv_bias_vec, "dp", scatter_dimension=0, tiled=True),
        lax.psum_scatter(grad_gate_a_weight, "dp", scatter_dimension=1, tiled=True),
        lax.psum_scatter(grad_bias_a_vec, "dp", scatter_dimension=0, tiled=True),
        lax.psum_scatter(grad_gate_in_weight, "dp", scatter_dimension=1, tiled=True),
        lax.psum_scatter(grad_bias_in_vec, "dp", scatter_dimension=0, tiled=True),
        lax.psum_scatter(grad_decay_raw, "dp", scatter_dimension=0, tiled=True),
        lax.psum_scatter(grad_out_weight, "dp", scatter_dimension=1, tiled=True),
    )
    grad_normed = lax.psum_scatter(
        contract_last(grad_pre_x, full_branch_x) + contract_last(grad_pre_y, full_branch_y),
        "tensor",
        scatter_dimension=0,
        tiled=True,
    )
    grad_rows, grad_gain_one = norm_pull(grad_normed)
    grad_inputs = grad_resid + grad_rows
    gain_grads = (
        lax.psum_scatter(grad_gain_one, ("dp", "tensor"), scatter_dimension=0, tiled=True),
        lax.psum_scatter(grad_gain_two, ("dp", "tensor"), scatter_dimension=0, tiled=True),
    )
    return (
        result,
        grad_inputs,
        gain_grads[0],
        gain_grads[1],
        mixer_grads[0],
        mixer_grads[1],
        mixer_grads[2],
        mixer_grads[3],
        mixer_grads[4],
        mixer_grads[5],
        mixer_grads[6],
        mixer_grads[7],
        mixer_grads[8],
        mixer_grads[9],
        ffn_grads[0],
        ffn_grads[1],
        ffn_grads[2],
    )


def solution(mesh):
    in_specs = (
        P(("dp", "tensor"), None),
        P("dp"),
        P("dp"),
        P("dp", "tensor"),
        P("dp", "tensor"),
        P(None, ("tensor", "dp")),
        P(("tensor", "dp")),
        P("tensor", "dp", None),
        P(("tensor", "dp")),
        P("tensor", "dp", None),
        P(("tensor", "dp")),
        P(("tensor", "dp")),
        P("tensor", "dp"),
        P("dp", "tensor"),
        P("dp", "tensor"),
        P("tensor", "dp"),
        P(("dp", "tensor"), None),
    )
    out_specs = (
        P(("dp", "tensor"), None),
        P(("dp", "tensor"), None),
        P(("dp", "tensor")),
        P(("dp", "tensor")),
        P("dp", "tensor"),
        P("dp", "tensor"),
        P(None, ("tensor", "dp")),
        P(("tensor", "dp")),
        P("tensor", "dp", None),
        P(("tensor", "dp")),
        P("tensor", "dp", None),
        P(("tensor", "dp")),
        P(("tensor", "dp")),
        P("tensor", "dp"),
        P("dp", "tensor"),
        P("dp", "tensor"),
        P("tensor", "dp"),
    )
    return jax.shard_map(local, mesh=mesh, in_specs=in_specs, out_specs=out_specs, check_vma=False)
```

profile of v0, /device:TPU:0, one launch (start us, length us, event | category | flops | bytes accessed | tf_op | source)
XLA Modules:
  0.0 4107.4 jit_solution(13589128066195491140)
XLA Ops:
  16.3 78.5 %all-reduce.57 = (bf16[1280]{0:T(1024)(128)(2,1)S(1)}, bf16[2560]{0:T(1024)(128)(2,1)S(1)}, bf16[1280]{0:T(1024)(128)(2,1)S(1)}, bf16[1280]{0:T(1024)(128)(2,1)S...) all-reduce(bf16[1280]{0:T(1024)(128)(2,1)S(1)} %dynamic-update-slic, ...), channel_id=1, replica_groups=mesh['dp'=16,'tensor'=2] {'dp'}, use_global_device_ids=true, to_apply=%add.43 | all-reduce | flops 10240 | bytes 40960
  99.2 35.6 all-gather
  135.0 47.1 %all_gather.71 = bf16[5,256,256]{2,1,0:T(8,128)(2,1)S(1)} all-gather(bf16[5,16,256]{2,1,0:T(8,128)(2,1)S(1)} %copy-done.51), channel_id=1, replica_groups=mesh['dp'=16,'tensor'=2] {'dp'}, dimensions={1}, use_global_device_ids=true | all-gather | bytes 696320 | tf_op jit(solution)/shard_map/all_gather | solution.py:75
  182.1 43.3 %all_gather.73 = bf16[5,256,256]{2,1,0:T(8,128)(2,1)S(1)} all-gather(bf16[5,16,256]{2,1,0:T(8,128)(2,1)S(1)} %copy-done.52), channel_id=1, replica_groups=mesh['dp'=16,'tensor'=2] {'dp'}, dimensions={1}, use_global_device_ids=true | all-gather | bytes 696320 | tf_op jit(solution)/shard_map/all_gather | solution.py:77
  225.4 5.6 fusion.80
  239.4 4.2 multiply_exponential_fusion
  243.7 4.7 slice.428
  252.0 4.3 slice.480
  279.3 3.0 pad.148
  282.3 2.9 pad.149
  285.2 29.6 all-gather.16.cloned.1.call-done
  314.8 7.1 multiply_convert_fusion.3
  321.8 90.4 %all-gather.18.cloned.1.call-done = bf16[1280,2560]{0,1:T(8,128)(2,1)} async-done(((bf16[1280,160]{0,1:T(8,128)(2,1)}), bf16[1280,2560]{0,1:T(8,128)(2,1)}) %all-gather.18.cloned.1.call-update) | async-done | bytes 6553616 | tf_op jit(solution)/shard_map/all_gather | solution.py:80
  412.3 6.2 fusion.83
  418.6 8.5 reduce-scatter.16.cloned.1.call-done
  432.8 8.0 all-gather.20.cloned.1.call-done
  440.8 223.3 %all-gather.24.cloned.1.call-done = bf16[2560,3840]{1,0:T(8,128)(2,1)} async-done(((bf16[160,3840]{1,0:T(8,128)(2,1)}), bf16[2560,3840]{1,0:T(8,128)(2,1)}) %all-gather.24.cloned.1.call-update) | async-done | bytes 19660816 | tf_op jit(solution)/shard_map/all_gather | solution.py:87
  664.1 14.1 fusion.85
  678.1 206.3 %all-gather.22.cloned.1.call-done = bf16[2560,3840]{1,0:T(8,128)(2,1)} async-done(((bf16[160,3840]{1,0:T(8,128)(2,1)}), bf16[2560,3840]{1,0:T(8,128)(2,1)}) %all-gather.22.cloned.1.call-update) | async-done | bytes 19660816 | tf_op jit(solution)/shard_map/all_gather | solution.py:86
  884.4 13.8 fusion.84
  898.2 218.6 %all-gather.26.cloned.1.call-done = bf16[3840,2560]{0,1:T(8,128)(2,1)} async-done(((bf16[3840,160]{0,1:T(8,128)(2,1)}), bf16[3840,2560]{0,1:T(8,128)(2,1)}) %all-gather.26.cloned.1.call-update) | async-done | bytes 19660816 | tf_op jit(solution)/shard_map/all_gather | solution.py:88
  1116.8 14.9 multiply_convert_fusion
  1131.7 10.8 fusion.87
  1142.5 11.8 convolution_add_fusion
  1154.4 8.5 reduce-scatter.20.cloned.1.call-done
  1162.9 2.4 multiply_reduce_fusion.5
  1168.3 2.2 slice.492
  1171.1 2.2 slice.483
  1173.2 5.9 slice.493
  1179.2 6.0 slice.484
  1185.2 3.2 slice.486
  1188.4 2.5 slice_add_fusion
  1191.0 7.3 fusion.17
  1198.8 2.2 slice.489
  1203.1 6.0 slice.488
  1209.1 3.4 slice.490
  1226.2 3.3 slice.546
  1234.1 4.9 pad.165
  1239.0 2.5 add.433
  1241.6 11.0 rev.6
  1252.6 5.4 convert_reduce_fusion
  1259.1 2.6 convert_reduce_fusion.1
  1261.7 2.2 copy.77
  1266.9 2.8 copy.81
  1269.7 6.9 multiply_reduce_fusion.4
  1278.7 5.0 fusion.88
  1283.7 3.4 convolution_add_fusion.1
  1287.2 11.0 fusion.86
  1304.8 6.6 fusion.93
  1312.8 6.6 fusion.90
  1319.4 6.7 fusion.89
  1328.1 15.3 fusion.95
  1345.0 15.9 fusion.94
  1363.0 16.5 fusion.96
  1380.4 77.2 %all-reduce.56 = (f32[1280]{0:T(1024)S(1)}, f32[1280]{0:T(1024)S(1)}, f32[1280]{0:T(1024)S(1)}, f32[1280]{0:T(1024)S(1)}) all-reduce(f32[1280]{0:T(1024)S(1)} %get-tuple-element.25, f32[1280]{0:T(1024)S(1)} %get-tuple-element.46, f32[1280]{0:T(1024)S(1)} %get-tuple-element.44, ...), channel_id=11, replica_groups=mesh['dp'=16,'tensor'=2] {'dp'}, use_global_device_ids=true, to_apply=%region_20.21.clone | all-reduce | flops 5120 | bytes 40960
  1463.3 38.0 all-reduce.55
  1502.6 4.3 fusion.23
  1506.9 32.2 reduce-scatter.30.cloned.1.call-done
  1539.1 271.8 %reduce-scatter.32.cloned.1.call-done = f32[1280,160]{0,1:T(8,128)} async-done(((f32[1280,2560]{0,1:T(8,128)}), f32[1280,160]{0,1:T(8,128)}) %reduce-scatter.32.cloned.1.call-update) | async-done | bytes 819216 | tf_op jit(solution)/shard_map/reduce_scatter | solution.py:265
  1810.9 280.5 %reduce-scatter.26.cloned.1.call-done = f32[160,1280]{1,0:T(8,128)} async-done(((f32[2560,1280]{1,0:T(8,128)}), f32[160,1280]{1,0:T(8,128)}) %reduce-scatter.26.cloned.1.call-update) | async-done | bytes 819216 | tf_op jit(solution)/shard_map/reduce_scatter | solution.py:257
  2091.5 280.3 %reduce-scatter.24.cloned.1.call-done = f32[160,1280]{1,0:T(8,128)} async-done(((f32[2560,1280]{1,0:T(8,128)}), f32[160,1280]{1,0:T(8,128)}) %reduce-scatter.24.cloned.1.call-update) | async-done | bytes 819216 | tf_op jit(solution)/shard_map/reduce_scatter | solution.py:256
  2371.8 579.8 %reduce-scatter.36.cloned.1.call-done = f32[160,3840]{1,0:T(8,128)} async-done(((f32[2560,3840]{1,0:T(8,128)}), f32[160,3840]{1,0:T(8,128)}) %reduce-scatter.36.cloned.1.call-update) | async-done | bytes 2457616 | tf_op jit(solution)/shard_map/reduce_scatter | solution.py:195
  2951.6 574.5 %reduce-scatter.34.cloned.1.call-done = f32[160,3840]{1,0:T(8,128)} async-done(((f32[2560,3840]{1,0:T(8,128)}), f32[160,3840]{1,0:T(8,128)}) %reduce-scatter.34.cloned.1.call-update) | async-done | bytes 2457616 | tf_op jit(solution)/shard_map/reduce_scatter | solution.py:194
  3526.1 574.6 %reduce-scatter.38.cloned.1.call-done = f32[3840,160]{0,1:T(8,128)} async-done(((f32[3840,2560]{0,1:T(8,128)}), f32[3840,160]{0,1:T(8,128)}) %reduce-scatter.38.cloned.1.call-update) | async-done | bytes 2457616 | tf_op jit(solution)/shard_map/reduce_scatter | solution.py:196
  (418 shorter events, 103.3 us)
Async XLA Ops:
  7.2 218.3 %all-gather.12.cloned.1.call-start = ((), (), s32[]{:S(2)}) async-start(), calls=%async_computation.13 | async-start | bytes 1966080 | tf_op jit(solution)/shard_map/all_gather | solution.py:141
  11.2 3.4 copy-start.62
  11.2 87.3 %copy-start.57 = (f32[128]{0:T(128)}, f32[128]{0:T(128)S(1)}, u32[]{:S(2)}) copy-start(f32[128]{0:T(128)S(1)} %fusion.56) | copy-start | bytes 1540
  94.8 4.3 copy-start.53
  94.8 3.7 copy-start.48
  94.8 4.4 copy-start.61
  97.0 38.0 copy-start.51
  97.0 85.1 %copy-start.52 = (bf16[5,16,256]{2,1,0:T(8,128)(2,1)S(1)}, bf16[5,16,256]{2,1,0:T(8,128)(2,1)}, u32[]{:S(2)}) copy-start(bf16[5,16,256]{2,1,0:T(8,128)(2,1)} %param.26) | copy-start | bytes 122884
  97.0 128.4 %all-gather.14.cloned.1.call-start = ((), (), s32[]{:S(2)}) async-start(), calls=%async_computation.14 | async-start | bytes 6963200 | tf_op jit(solution)/shard_map/all_gather | solution.py:71
  97.8 217.0 %all-gather.16.cloned.1.call-start = ((), (), s32[]{:S(2)}) async-start(), calls=%async_computation.15 | async-start | bytes 6963200 | tf_op jit(solution)/shard_map/all_gather | solution.py:72
  98.5 313.7 %all-gather.18.cloned.1.call-start = ((), (), s32[]{:S(2)}) async-start(), calls=%async_computation.16 | async-start | bytes 6963200 | tf_op jit(solution)/shard_map/all_gather | solution.py:80
  99.1 328.0 %reduce-scatter.16.cloned.1.call-start = ((), (), s32[]{:S(2)}) async-start(), calls=%async_computation.17 | async-start | bytes 3932160 | tf_op jit(solution)/shard_map/reduce_scatter | solution.py:164
  182.1 54.1 %copy-start.12 = (bf16[5,256,256]{2,1,0:T(8,128)(2,1)}, bf16[5,256,256]{2,1,0:T(8,128)(2,1)S(1)}, u32[]{:S(2)}) copy-start(bf16[5,256,256]{2,1,0:T(8,128)(2,1)S(1)} %all_gather.71) | copy-start | bytes 1966084
  225.4 7.6 copy-start.17
  233.0 3.2 copy-start.4
  236.2 3.2 copy-start.2
  243.7 4.7 copy-start.8
  251.1 5.2 copy-start.10
  266.7 4.3 copy-start.41
  266.7 4.3 copy-start.42
  282.3 32.5 copy-start.21
  321.8 96.7 %copy-start.44 = (bf16[256,1280]{1,0:T(8,128)(2,1)}, bf16[256,1280]{1,0:T(8,128)(2,1)S(1)}, u32[]{:S(2)}) copy-start(bf16[256,1280]{1,0:T(8,128)(2,1)S(1)} %get-tuple-element.51) | copy-start | bytes 1966084
  418.5 8.6 copy-start.6
  418.5 22.3 all-gather.20.cloned.1.call-start
  418.6 746.8 %copy-start.46 = (f32[2560]{0:T(1024)}, f32[2560]{0:T(1024)S(1)}, u32[]{:S(2)}) copy-start(f32[2560]{0:T(1024)S(1)} %convert_element_type.82) | copy-start | bytes 30724
  428.7 736.7 %copy-start = (f32[128,2560]{1,0:T(8,128)}, f32[128,2560]{1,0:T(8,128)S(1)}, u32[]{:S(2)}) copy-start(f32[128,2560]{1,0:T(8,128)S(1)} %get-tuple-element.50) | copy-start | bytes 3932164
  428.7 736.7 %copy-start.55 = (f32[128]{0:T(128)}, f32[128]{0:T(128)S(1)}, u32[]{:S(2)}) copy-start(f32[128]{0:T(128)S(1)} %fusion.57) | copy-start | bytes 1540
  430.0 234.1 %all-gather.24.cloned.1.call-start = ((), (), s32[]{:S(2)}) async-start(), calls=%async_computation.20 | async-start | bytes 20889600 | tf_op jit(solution)/shard_map/all_gather | solution.py:87
  430.7 453.7 %all-gather.22.cloned.1.call-start = ((), (), s32[]{:S(2)}) async-start(), calls=%async_computation.19 | async-start | bytes 20889600 | tf_op jit(solution)/shard_map/all_gather | solution.py:86
  431.5 466.7 %all-gather.28.cloned.1.call-start = ((), (), s32[]{:S(2)}) async-start(), calls=%async_computation.23 | async-start | bytes 1966080 | tf_op jit(solution)/shard_map/all_gather | solution.py:185
  432.2 684.6 %all-gather.26.cloned.1.call-start = ((), (), s32[]{:S(2)}) async-start(), calls=%async_computation.21 | async-start | bytes 20889600 | tf_op jit(solution)/shard_map/all_gather | solution.py:88
  432.8 730.1 %reduce-scatter.20.cloned.1.call-start = ((), (), s32[]{:S(2)}) async-start(), calls=%async_computation.24 | async-start | bytes 3932160 | tf_op jit(solution)/shard_map/reduce_scatter | solution.py:198
  1131.7 10.8 copy-start.33
  1131.7 10.8 copy-start.35
  1154.4 11.0 copy-start.15
  1154.4 36.6 all-gather.30.cloned.1.call-start
  1166.8 293.2 %reduce-scatter.40.cloned.1.call-start = ((), (), s32[]{:S(2)}) async-start(), calls=%async_computation.35 | async-start | bytes 696320
  1179.2 9.3 copy-start.23
  1203.1 6.0 copy-start.27
  1218.5 3.1 copy-start.43
  1241.6 11.0 copy-start.3
  1277.8 183.6 %reduce-scatter.22.cloned.1.call-start = ((), (), s32[]{:S(2)}) async-start(), calls=%async_computation.26 | async-start | bytes 3932160 | tf_op jit(solution)/shard_map/reduce_scatter | solution.py:267
  1278.3 5.4 slice-start
  1278.7 5.0 slice-start.1
  1278.7 5.0 copy-start.26
  1287.1 215.3 %reduce-scatter.18.cloned.1.call-start = ((), (), s32[]{:S(2)}) async-start(), calls=%async_computation.22 | async-start | bytes 3932160 | tf_op jit(solution)/shard_map/reduce_scatter | solution.py:178
  1298.3 208.6 %reduce-scatter.28.cloned.1.call-start = ((), (), s32[]{:S(2)}) async-start(), calls=%async_computation.29 | async-start | bytes 1392640 | tf_op jit(solution)/shard_map/reduce_scatter | solution.py:260
  1301.0 238.1 %reduce-scatter.30.cloned.1.call-start = ((), (), s32[]{:S(2)}) async-start(), calls=%async_computation.30 | async-start | bytes 1392640 | tf_op jit(solution)/shard_map/reduce_scatter | solution.py:262
  1303.5 507.4 %reduce-scatter.32.cloned.1.call-start = ((), (), s32[]{:S(2)}) async-start(), calls=%async_computation.31 | async-start | bytes 13926400 | tf_op jit(solution)/shard_map/reduce_scatter | solution.py:265
  1311.5 780.0 %reduce-scatter.26.cloned.1.call-start = ((), (), s32[]{:S(2)}) async-start(), calls=%async_computation.28 | async-start | bytes 13926400 | tf_op jit(solution)/shard_map/reduce_scatter | solution.py:257
  1319.4 1052.4 %reduce-scatter.24.cloned.1.call-start = ((), (), s32[]{:S(2)}) async-start(), calls=%async_computation.27 | async-start | bytes 13926400 | tf_op jit(solution)/shard_map/reduce_scatter | solution.py:256
  1326.2 1625.4 %reduce-scatter.36.cloned.1.call-start = ((), (), s32[]{:S(2)}) async-start(), calls=%async_computation.33 | async-start | bytes 41779200 | tf_op jit(solution)/shard_map/reduce_scatter | solution.py:195
  1343.4 2182.6 %reduce-scatter.34.cloned.1.call-start = ((), (), s32[]{:S(2)}) async-start(), calls=%async_computation.32 | async-start | bytes 41779200 | tf_op jit(solution)/shard_map/reduce_scatter | solution.py:194
  1360.9 2739.7 %reduce-scatter.38.cloned.1.call-start = ((), (), s32[]{:S(2)}) async-start(), calls=%async_computation.34 | async-start | bytes 41779200 | tf_op jit(solution)/shard_map/reduce_scatter | solution.py:196
  1379.5 81.9 %copy-start.7 = (bf16[128,2560]{1,0:T(8,128)(2,1)S(1)}, bf16[128,2560]{1,0:T(8,128)(2,1)}, u32[]{:S(2)}) copy-start(bf16[128,2560]{1,0:T(8,128)(2,1)} %param.17) | copy-start | bytes 1966084
  1379.5 81.9 %copy-start.49 = (f32[2560]{0:T(1024)S(1)}, f32[2560]{0:T(1024)}, u32[]{:S(2)}) copy-start(f32[2560]{0:T(1024)} %copy-done.48) | copy-start | bytes 30724
  1379.5 81.9 %copy-start.58 = (f32[128]{0:T(128)S(1)}, f32[128]{0:T(128)}, u32[]{:S(2)}) copy-start(f32[128]{0:T(128)} %copy-done.57) | copy-start | bytes 1540
  1379.5 83.8 %copy-start.50 = (f32[2560]{0:T(1024)S(1)}, f32[2560]{0:T(1024)}, u32[]{:S(2)}) copy-start(f32[2560]{0:T(1024)} %get-tuple-element.21) | copy-start | bytes 30724
  1379.5 123.0 %copy-start.63 = (f32[128]{0:T(128)S(1)}, f32[128]{0:T(128)}, u32[]{:S(2)}) copy-start(f32[128]{0:T(128)} %copy-done.62) | copy-start | bytes 1540
  1379.5 123.0 %copy-start.1 = (f32[128,2560]{1,0:T(8,128)S(1)}, f32[128,2560]{1,0:T(8,128)}, u32[]{:S(2)}) copy-start(f32[128,2560]{1,0:T(8,128)} %copy-done) | copy-start | bytes 3932164
  1379.5 123.0 %copy-start.16 = (bf16[128,2560]{1,0:T(8,128)(2,1)S(1)}, bf16[128,2560]{1,0:T(8,128)(2,1)}, u32[]{:S(2)}) copy-start(bf16[128,2560]{1,0:T(8,128)(2,1)} %param.33) | copy-start | bytes 1966084
  1379.5 123.0 %copy-start.47 = (f32[2560]{0:T(1024)S(1)}, f32[2560]{0:T(1024)}, u32[]{:S(2)}) copy-start(f32[2560]{0:T(1024)} %copy-done.46) | copy-start | bytes 30724
  1379.5 123.0 %copy-start.56 = (f32[128]{0:T(128)S(1)}, f32[128]{0:T(128)}, u32[]{:S(2)}) copy-start(f32[128]{0:T(128)} %copy-done.55) | copy-start | bytes 1540
  1379.6 123.0 %copy-start.60 = (f32[128]{0:T(128)S(1)}, f32[128]{0:T(128)}, u32[]{:S(2)}) copy-start(f32[128]{0:T(128)} %copy-done.59) | copy-start | bytes 1540
  (25 other events, 39.1 us)
Sparse Core Ops, SparseCore 0:
  97.2 5.2 all-gather.11
  105.2 111.3 all-gather.13
  219.3 95.4 all-gather.15
  317.3 94.9 all-gather.17
  418.6 8.3 reduce-scatter.15
  430.1 10.6 all-gather.19
  444.0 220.0 all-gather.23
  667.3 217.0 all-gather.21
  886.0 7.5 all-gather.27
  896.7 220.0 all-gather.25
  1154.5 8.3 reduce-scatter.19
  1166.9 10.6 all-gather.29
  1277.9 78.0 reduce-scatter.39
  1358.2 6.5 reduce-scatter.21
  1366.8 11.4 reduce-scatter.17
  1381.1 79.8 reduce-scatter.27
  1463.8 75.2 reduce-scatter.29
  1542.0 268.9 reduce-scatter.31
  1813.9 277.4 reduce-scatter.25
  2094.3 277.4 reduce-scatter.23
  2379.5 572.0 reduce-scatter.35
  2959.3 566.7 reduce-scatter.33
  3533.8 566.8 reduce-scatter.37
where the time goes:
time: 4120 us; the launch traced here: 4110 us
  waiting for transfers between devices  3390 us (82%)
  blocking collectives  320 us (8%)
  matrix products  187 us (5%)
  local copies, waits for them, and re-layouts  134 us (3%)
  other arithmetic  55.7 us (1%)
    reduce_scatter x1, waiting for transfers between devices, local(): lax.psum_scatter(grad_up_weight, 'dp', scatter_dimension=0, tiled=True)  580 us
    reduce_scatter x1, waiting for transfers between devices, local(): lax.psum_scatter(grad_down, 'dp', scatter_dimension=1, tiled=True)  575 us
    reduce_scatter x1, waiting for transfers between devices, local(): lax.psum_scatter(grad_gate_weight, 'dp', scatter_dimension=0, tiled=True)  574 us
    reduce_scatter x1, waiting for transfers between devices, local(): lax.psum_scatter(grad_y_weight, 'dp', scatter_dimension=0, tiled=True)  281 us
    reduce_scatter x1, waiting for transfers between devices, local(): lax.psum_scatter(grad_x_weight, 'dp', scatter_dimension=0, tiled=True)  280 us
    reduce_scatter x1, waiting for transfers between devices, local(): lax.psum_scatter(grad_out_weight, 'dp', scatter_dimension=1, tiled=True)  272 us
    all_gather x1, waiting for transfers between devices, fetch_ffn(): lax.all_gather(ffn_up, 'dp', axis=0, tiled=True)  223 us
    all_gather x1, waiting for transfers between devices, fetch_ffn(): lax.all_gather(ffn_down, 'dp', axis=1, tiled=True)  219 us
  transfers between devices with their start and end apart: 23, of which 15 were waited for; matrix products, arithmetic and copies ran while one was open for 5% of the time, Pallas kernels for 0%

commit v1 on v0

v1 whole, which is shorter than its diff:
```python
import jax
import jax.numpy as jnp
from jax import lax
from jax.sharding import PartitionSpec as P

EPSILON = 1e-06
F32 = jnp.float32
BF16 = jnp.bfloat16


def contract_last(left, right):
    return lax.dot_general(left, right, (((1,), (1,)), ((), ())), preferred_element_type=F32)


def contract_first(left, right):
    return lax.dot_general(left, right, (((0,), (0,)), ((), ())), preferred_element_type=F32)


def matmul(left, right):
    return jnp.dot(left, right, preferred_element_type=F32)


def scale_norm(values, gain):
    return values * lax.rsqrt(jnp.mean(values * values, axis=-1, keepdims=True) + EPSILON) * gain


def convolve(values, taps, bias):
    width = taps.shape[0]
    length = values.shape[0]
    padded = jnp.pad(values, ((width - 1, 0), (0, 0)))
    total = jnp.zeros_like(values) + bias
    for shift_by in range(width):
        total = (
            total + taps[shift_by] * padded[width - 1 - shift_by : width - 1 - shift_by + length]
        )
    return total


def lru_terms(pre_a, pre_i, decay_param, conv_out):
    rate = jax.nn.sigmoid(pre_a)
    entry = jax.nn.sigmoid(pre_i)
    log_decay = -8.0 * jax.nn.softplus(decay_param) * rate
    decay = jnp.exp(log_decay)
    driven = jnp.sqrt(-jnp.expm1(2.0 * log_decay)) * (entry * conv_out)
    return (decay, driven)


def combine(earlier, later):
    return (earlier[0] * later[0], later[0] * earlier[1] + later[1])


def linear_scan(decay, driven):
    return lax.associative_scan(combine, (decay, driven), axis=0)[1]


class Grid:
    def __init__(self, n):
        self.n = n
        self.nz = n // 4
        index = lax.axis_index("dp")
        self.x = index % 2
        self.y = (index // 2) % 2
        self.z = index // 4
        self.t = lax.axis_index("tensor")

    def place(self, axis):
        return {"x": self.x, "y": self.y, "t": self.t}[axis]

    def swap(self, value, axis):
        if axis == "t":
            return lax.ppermute(value, "tensor", [(0, 1), (1, 0)])
        bit = {"x": 1, "y": 2}[axis]
        return lax.ppermute(value, "dp", [(i, i ^ bit) for i in range(self.n)])

    def shift(self, value, by):
        return lax.ppermute(value, "dp", [(i, (i + 4 * by) % self.n) for i in range(self.n)])

    def pair(self, mine, other, axis):
        here = self.place(axis)
        return jnp.where(here == 0, jnp.stack([mine, other]), jnp.stack([other, mine]))

    def gather(self, value, axis):
        return self.pair(value, self.swap(value, axis), axis)

    def line(self, pieces):
        out = jnp.zeros((self.nz,) + pieces[0].shape, pieces[0].dtype)
        for k, piece in enumerate(pieces):
            out = lax.dynamic_update_index_in_dim(out, piece, (self.z - k) % self.nz, 0)
        return out

    def gather_z(self, value):
        return self.line([value] + [self.shift(value, k) for k in range(1, self.nz)])

    def pick(self, value, axis, dim, other=False):
        here = self.place(axis)
        return lax.dynamic_index_in_dim(value, 1 - here if other else here, dim, keepdims=False)

    def trade_z(self, value):
        take = lambda k: lax.dynamic_index_in_dim(value, (self.z + k) % self.nz, 0, keepdims=False)
        return self.line([take(0)] + [self.shift(take(k), k) for k in range(1, self.nz)])

    def trade(self, value, axis):
        return self.pair(
            self.pick(value, axis, 0), self.swap(self.pick(value, axis, 0, True), axis), axis
        )

    def reduce(self, value, axis, dim):
        got = self.swap(self.pick(value, axis, dim, True).astype(BF16), axis)
        return self.pick(value, axis, dim).astype(F32) + got.astype(F32)

    def reduce_z(self, value):
        take = lambda k: lax.dynamic_index_in_dim(value, (self.z + k) % self.nz, 0, keepdims=False)
        total = take(0).astype(F32)
        for k in range(1, self.nz):
            total = total + self.shift(take(k).astype(BF16), k).astype(F32)
        return total


def local(n):
    def run(
        inputs,
        gain_mix,
        gain_mlp,
        branch_x,
        branch_y,
        conv_taps,
        conv_bias,
        gate_a,
        bias_a,
        gate_in,
        bias_in,
        decay_param,
        out_proj,
        ffn_gate,
        ffn_up,
        ffn_down,
        cotangent,
    ):
        grid = Grid(n)
        nz = grid.nz
        rows_each, width = inputs.shape
        part = branch_x.shape[0]
        half = branch_x.shape[1]
        quarter = half // 2
        heads, gate_rows, block = gate_a.shape
        units = ffn_gate.shape[1] // nz
        split = part // 2

        slim = conv_bias.shape[0]
        vectors = jnp.concatenate(
            [
                conv_taps.reshape(-1),
                conv_bias,
                bias_a,
                bias_in,
                decay_param,
                gain_mix,
                gain_mlp,
            ]
        )
        n_vec = vectors.shape[0]
        packed = jnp.concatenate(
            [
                jnp.transpose(gate_a, (1, 0, 2)).reshape(gate_rows, half),
                jnp.transpose(gate_in, (1, 0, 2)).reshape(gate_rows, half),
                jnp.pad(vectors, (0, half - n_vec))[None],
            ]
        )
        small = grid.gather(grid.gather(grid.gather_z(packed), "y"), "x")
        small = jnp.transpose(small, (2, 1, 0, 3, 4)).reshape(n, -1, half)
        full_gate_a = jnp.transpose(
            small[:, :gate_rows].reshape(n * gate_rows, heads, block), (1, 0, 2)
        )
        full_gate_in = jnp.transpose(
            small[:, gate_rows : 2 * gate_rows].reshape(n * gate_rows, heads, block), (1, 0, 2)
        )
        vecs = small[:, 2 * gate_rows].astype(F32)
        per = jnp.transpose(vecs[:, : 8 * slim].reshape(n, 8, slim), (1, 0, 2)).reshape(8, half)
        full_taps, full_conv_bias = per[:4], per[4]
        full_bias_a, full_bias_in, full_decay = per[5], per[6], per[7]
        full_gain_mix = vecs[:, 8 * slim : 8 * slim + part].reshape(width)
        full_gain_mlp = vecs[:, 8 * slim + part : 8 * slim + 2 * part].reshape(width)

        def mixer_rows(blocks):
            got = grid.gather(grid.gather_z(grid.trade(blocks, "x")), "y")
            return jnp.transpose(got, (1, 0, 2, 3, 4)).reshape(width, -1)

        out_rows = jnp.transpose(out_proj)
        by_x = lambda w: jnp.stack([w[:, :quarter], w[:, quarter:]])
        full_in = mixer_rows(jnp.concatenate([by_x(branch_x), by_x(branch_y)], axis=-1))
        full_out = mixer_rows(by_x(out_rows))

        def ffn_rows(blocks):
            got = grid.trade_z(blocks)
            first = grid.gather(grid.gather(got[:, :split], "y"), "x")
            second = grid.gather(grid.gather(got[:, split:], "x"), "y")
            first = jnp.transpose(first, (2, 1, 0, 3, 4))
            second = jnp.transpose(second, (2, 0, 1, 3, 4))
            return jnp.concatenate([first, second], axis=3).reshape(width, units)

        by_z = lambda w: jnp.transpose(w.reshape(part, nz, units), (1, 0, 2))
        full_down = ffn_rows(jnp.transpose(ffn_down.reshape(nz, units, part), (0, 2, 1)))
        full_gate = ffn_rows(by_z(ffn_gate))
        full_up = ffn_rows(by_z(ffn_up))

        rows = inputs.astype(F32)
        two = grid.gather(grid.gather(inputs, "t"), "x").reshape(4 * rows_each, width)
        length = 2 * rows_each
        normed = scale_norm(two.astype(F32), full_gain_mix).astype(BF16)
        pre = matmul(normed, full_in).reshape(2, length, half)

        def to_channels(value):
            mine = grid.pick(value, "x", 0)
            other = grid.swap(grid.pick(value, "x", 0, True).astype(BF16), "x").astype(value.dtype)
            here = grid.x == 0
            outs = []
            for k in range(value.shape[2] // quarter):
                a = mine[:, k * quarter : (k + 1) * quarter]
                b = other[:, k * quarter : (k + 1) * quarter]
                outs.append(
                    jnp.where(
                        here, jnp.concatenate([a, b], axis=1), jnp.concatenate([b, a], axis=1)
                    )
                )
            return outs

        def to_rows(value):
            halves = jnp.stack([value[:, :quarter], value[:, quarter:]])
            return grid.trade(halves, "x").reshape(2 * length, quarter)

        pre_x, pre_y = to_channels(pre)
        gated_y, gelu_pull = jax.vjp(jax.nn.gelu, pre_y)
        conv_out, conv_pull = jax.vjp(convolve, pre_x, full_taps, full_conv_bias)
        rounded = conv_out.astype(BF16).reshape(length, heads, block)
        pre_a = (
            jnp.einsum("thd,hde->the", rounded, full_gate_a, preferred_element_type=F32).reshape(
                length, half
            )
            + full_bias_a
        )
        pre_i = (
            jnp.einsum("thd,hde->the", rounded, full_gate_in, preferred_element_type=F32).reshape(
                length, half
            )
            + full_bias_in
        )
        (decay, driven), lru_pull = jax.vjp(lru_terms, pre_a, pre_i, full_decay, conv_out)
        states = linear_scan(decay, driven)
        mixed = to_rows((states * gated_y).astype(BF16))
        branch_out = contract_last(mixed, full_out).reshape(2, 2, rows_each, width)
        branch_out = grid.reduce(grid.reduce(branch_out, "t", 1), "x", 0)
        resid = rows + branch_out

        normed_two_rows, norm_two_pull = jax.vjp(scale_norm, resid, full_gain_mlp)
        to_line = lambda v: grid.gather(grid.gather_z(v), "t")
        tokens = nz * length
        normed_two = to_line(normed_two_rows.astype(BF16)).reshape(tokens, width)
        upstream = to_line(cotangent).reshape(tokens, width)

        def from_line(partial):
            partial = partial.reshape(2, nz, rows_each, width)
            return grid.reduce_z(grid.reduce(partial, "t", 0))

        grad_hidden = matmul(upstream, full_down)
        gate_pre = matmul(normed_two, full_gate)
        up_pre = matmul(normed_two, full_up)
        gate_act, gate_pull = jax.vjp(jax.nn.gelu, gate_pre)
        hidden = (gate_act * up_pre).astype(BF16)
        grad_gate_pre = gate_pull(grad_hidden * up_pre)[0].astype(BF16)
        grad_up_pre = (grad_hidden * gate_act).astype(BF16)
        grad_normed_two = from_line(
            contract_last(grad_gate_pre, full_gate) + contract_last(grad_up_pre, full_up)
        )
        result = (resid + from_line(contract_last(hidden, full_down))).astype(BF16)

        def ffn_reduce(grad):
            grad = grad.reshape(nz, 2, 2, part, units)
            first = grid.reduce(grid.reduce(grad[:, :, :, :split], "x", 2), "y", 1)
            second = grid.reduce(grid.reduce(grad[:, :, :, split:], "y", 1), "x", 1)
            both = jnp.concatenate([first, second], axis=1).astype(BF16)
            return grid.trade_z(both)

        wide = lambda g: jnp.transpose(g, (1, 0, 2)).reshape(part, nz * units).astype(F32)
        grad_gate = wide(ffn_reduce(contract_first(normed_two, grad_gate_pre)))
        grad_up = wide(ffn_reduce(contract_first(normed_two, grad_up_pre)))
        grad_down = ffn_reduce(contract_first(upstream, hidden))
        grad_down = jnp.transpose(grad_down, (0, 2, 1)).reshape(nz * units, part).astype(F32)

        grad_resid_norm, _ = norm_two_pull(grad_normed_two)
        grad_resid = cotangent.astype(F32) + grad_resid_norm
        back = grid.gather(grid.gather(grad_resid.astype(BF16), "t"), "x").reshape(-1, width)
        (grad_mixed,) = to_channels(matmul(back, full_out).reshape(2, length, quarter))
        grad_out = contract_first(back, mixed)
        grad_states = grad_mixed * gated_y
        grad_pre_y = gelu_pull(grad_mixed * states)[0].astype(BF16)
        next_decay = jnp.concatenate([decay[1:], jnp.zeros_like(decay[:1])], axis=0)
        grad_driven = jnp.flip(linear_scan(jnp.flip(next_decay, 0), jnp.flip(grad_states, 0)), 0)
        prior_states = jnp.concatenate([jnp.zeros_like(states[:1]), states[:-1]], axis=0)
        grad_decay = grad_driven * prior_states
        grad_pre_a, grad_pre_i, grad_decay_raw, grad_conv_direct = lru_pull(
            (grad_decay, grad_driven)
        )
        rounded_grad_a = grad_pre_a.astype(BF16)
        rounded_grad_i = grad_pre_i.astype(BF16)
        blocks_a = rounded_grad_a.reshape(length, heads, block)
        blocks_i = rounded_grad_i.reshape(length, heads, block)
        grad_rounded = jnp.einsum(
            "the,hde->thd", blocks_a, full_gate_a, preferred_element_type=F32
        ) + jnp.einsum("the,hde->thd", blocks_i, full_gate_in, preferred_element_type=F32)
        grad_gate_a = jnp.einsum("thd,the->dhe", rounded, blocks_a, preferred_element_type=F32)
        grad_gate_in = jnp.einsum("thd,the->dhe", rounded, blocks_i, preferred_element_type=F32)
        grad_bias_a = jnp.sum(rounded_grad_a.astype(F32), axis=0)
        grad_bias_in = jnp.sum(rounded_grad_i.astype(F32), axis=0)
        grad_conv = grad_conv_direct + grad_rounded.reshape(length, half)
        grad_pre_x, grad_taps, grad_conv_bias = conv_pull(grad_conv)
        grad_in_rows = jnp.concatenate(
            [to_rows(grad_pre_x.astype(BF16)), to_rows(grad_pre_y)], axis=1
        )
        grad_in = contract_first(normed, grad_in_rows)

        def mixer_reduce(grad):
            grad = grad.reshape(nz, 2, 2, part, -1)
            return grid.trade(grid.reduce_z(grid.reduce(grad, "y", 1)).astype(BF16), "x")

        grad_out = mixer_reduce(grad_out)
        grad_out = jnp.transpose(grad_out, (0, 2, 1)).reshape(half, part).astype(F32)
        grad_in = mixer_reduce(grad_in).astype(F32)
        join = lambda g: jnp.concatenate([g[0], g[1]], axis=1)
        grad_branch_x = join(grad_in[:, :, :quarter])
        grad_branch_y = join(grad_in[:, :, quarter:])

        vec = jnp.concatenate(
            [
                grad_taps,
                grad_conv_bias[None],
                grad_bias_a[None],
                grad_bias_in[None],
                grad_decay_raw[None],
            ]
        )
        vec = jnp.transpose(vec.reshape(8, n, slim), (1, 0, 2)).reshape(n, 1, 8 * slim)
        grad_small = jnp.concatenate(
            [
                grad_gate_a.reshape(n, gate_rows, half),
                grad_gate_in.reshape(n, gate_rows, half),
                jnp.pad(vec, ((0, 0), (0, 0), (0, half - 8 * slim))),
            ],
            axis=1,
        ).reshape(nz, 2, 2, 2 * gate_rows + 1, half)
        grad_small = grid.reduce_z(grid.reduce(grid.reduce(grad_small, "x", 2), "y", 1))
        unpack = lambda g: jnp.transpose(g.reshape(gate_rows, heads, block), (1, 0, 2))
        vec = grad_small[2 * gate_rows, : 8 * slim].reshape(8, slim)

        grad_normed = matmul_t(grad_in_rows, full_in).reshape(2, 2, rows_each, width)
        grad_normed = grid.reduce(grid.reduce(grad_normed, "t", 1), "x", 0)
        _, norm_pull = jax.vjp(scale_norm, rows, full_gain_mix)
        grad_rows, _ = norm_pull(grad_normed)
        grad_inputs = grad_resid + grad_rows

        gains = jnp.stack(
            [
                jnp.sum(
                    branch_x.astype(F32) * grad_branch_x + branch_y.astype(F32) * grad_branch_y,
                    axis=1,
                )
                / gain_mix.astype(F32),
                jnp.sum(
                    ffn_gate.astype(F32) * grad_gate + ffn_up.astype(F32) * grad_up,
                    axis=1,
                )
                / gain_mlp.astype(F32),
            ]
        )
        gains = gains + grid.swap(gains, "t")
        gains = lax.dynamic_index_in_dim(gains.reshape(2, 2, split), grid.t, 1, keepdims=False)
        return (
            result,
            grad_inputs,
            gains[0],
            gains[1],
            grad_branch_x,
            grad_branch_y,
            vec[:4],
            vec[4],
            unpack(grad_small[:gate_rows]),
            vec[5],
            unpack(grad_small[gate_rows : 2 * gate_rows]),
            vec[6],
            vec[7],
            grad_out,
            grad_gate,
            grad_up,
            grad_down,
        )

    return run


def matmul_t(left, right):
    return contract_last(left, right)


def solution(mesh):
    in_specs = (
        P(("dp", "tensor"), None),
        P("dp"),
        P("dp"),
        P("dp", "tensor"),
        P("dp", "tensor"),
        P(None, ("tensor", "dp")),
        P(("tensor", "dp")),
        P("tensor", "dp", None),
        P(("tensor", "dp")),
        P("tensor", "dp", None),
        P(("tensor", "dp")),
        P(("tensor", "dp")),
        P("tensor", "dp"),
        P("dp", "tensor"),
        P("dp", "tensor"),
        P("tensor", "dp"),
        P(("dp", "tensor"), None),
    )
    out_specs = (
        P(("dp", "tensor"), None),
        P(("dp", "tensor"), None),
        P(("dp", "tensor")),
        P(("dp", "tensor")),
        P("dp", "tensor"),
        P("dp", "tensor"),
        P(None, ("tensor", "dp")),
        P(("tensor", "dp")),
        P("tensor", "dp", None),
        P(("tensor", "dp")),
        P("tensor", "dp", None),
        P(("tensor", "dp")),
        P(("tensor", "dp")),
        P("tensor", "dp"),
        P("dp", "tensor"),
        P("dp", "tensor"),
        P("tensor", "dp"),
    )
    return jax.shard_map(
        local(mesh.shape["dp"]),
        mesh=mesh,
        in_specs=in_specs,
        out_specs=out_specs,
        check_vma=False,
    )
```

time: 4120 us -> 1600 us (0.39)
  waiting for transfers between devices: 3390 us -> 646 us
  blocking collectives: 320 us -> 0 us
  local copies, waits for them, and re-layouts: 134 us -> 437 us
  starting transfers between devices: 1.51 us -> 162 us
  other arithmetic: 55.7 us -> 206 us
  matrix products: 187 us -> 124 us
    reduce_scatter x12 -> x0, waiting for transfers between devices: 2610 us -> none  [the longest x1 580 us: local(): lax.psum_scatter(grad_up_weight, 'dp', scatter_dimension=0, tiled=True)]
    all_gather x10 -> x0, waiting for transfers between devices: 776 us -> none  [the longest x1 223 us: fetch_ffn(): lax.all_gather(ffn_up, 'dp', axis=0, tiled=True)]
    ppermute x0 -> x102, waiting for transfers between devices: none -> 646 us  [the longest x48 403 us: shift(): lax.ppermute(value, 'dp', [(i, (i + 4 * by) % self.n) for i in range(self...]
    unnamed x3 -> x0, blocking collectives: 194 us -> none
    ppermute x0 -> x102, starting transfers between devices: none -> 162 us  [the longest x48 121 us: shift(): lax.ppermute(value, 'dp', [(i, (i + 4 * by) % self.n) for i in range(self...]
    all_gather x3 -> x0, blocking collectives: 126 us -> none  [the longest x1 47.1 us: fetch_mixer(): lax.all_gather(gate_a, 'dp', axis=1, tiled=True)]
    slice x98, local copies, waits for them, and re-layouts: 73.9 us -> 142 us  [linear_scan(): return lax.associative_scan(combine, (decay, driven), axis=0)[1]]
    select_n x0 -> x31, other arithmetic: none -> 67.4 us  [the longest x30 67.3 us: pair(): jnp.where(here == 0, jnp.stack([mine, other]), jnp.stack([other, mine]))]
  transfers between devices with their start and end apart: 23 -> 102, of which waited for: 15 -> 45; matrix products, arithmetic and copies ran while one was open for 5% -> 41% of each run, Pallas kernels for 0% -> 0%
where the time goes in v1:
time: 1600 us; the launch traced here: 1580 us
  waiting for transfers between devices  646 us (40%)
  local copies, waits for them, and re-layouts  437 us (27%)
  other arithmetic  206 us (13%)
  starting transfers between devices  162 us (10%)
  matrix products  124 us (8%)
    ppermute x48, waiting for transfers between devices, shift(): lax.ppermute(value, 'dp', [(i, (i + 4 * by) % self.n) for i in range(self...  403 us
    ppermute x45, waiting for transfers between devices, swap(): return lax.ppermute(value, 'dp', [(i, i ^ bit) for i in range(self.n)])  243 us
    slice x98, local copies, waits for them, and re-layouts, linear_scan(): return lax.associative_scan(combine, (decay, driven), axis=0)[1]  142 us
    ppermute x48, starting transfers between devices, shift(): lax.ppermute(value, 'dp', [(i, (i + 4 * by) % self.n) for i in range(self...  121 us
    select_n x30, other arithmetic, pair(): jnp.where(here == 0, jnp.stack([mine, other]), jnp.stack([other, mine]))  67.3 us
    unnamed x381, local copies, waits for them, and re-layouts  41.3 us
    ppermute x45, starting transfers between devices, swap(): return lax.ppermute(value, 'dp', [(i, i ^ bit) for i in range(self.n)])  40.3 us
    dot_general x5, matrix products, matmul(): return jnp.dot(left, right, preferred_element_type=F32)  39.4 us
  transfers between devices with their start and end apart: 102, of which 45 were waited for; matrix products, arithmetic and copies ran while one was open for 41% of the time, Pallas kernels for 0%

profile of v1, /device:TPU:0, one launch (start us, length us, event | category | flops | bytes accessed | tf_op | source)
XLA Modules:
  0.0 1578.9 jit_solution(15507736005045790155)
XLA Ops:
  23.3 6.5 constant_dynamic-slice_fusion.12
  88.2 45.5 %collective-permute-done.26 = bf16[160,960]{1,0:T(8,128)(2,1)S(1)} collective-permute-done((bf16[160,960]{1,0:T(8,128)(2,1)}, bf16[160,960]{1,0:T(8,128)(2,1)S(1)}, u32[]{:S(2)}, u32[]{:S(2)}) %collective-permute-start.26) | collective-permute-done | bytes 307232 | tf_op jit(solution)/shard_map/ppermute | solution.py:76
  133.7 5.5 collective-permute-start.32
  139.3 8.0 collective-permute-start.33
  150.7 12.1 collective-permute-done.33
  162.8 6.9 collective-permute-start.39
  170.4 10.0 collective-permute-done.39
  181.7 14.5 collective-permute-done.40
  227.8 14.3 collective-permute-done.16
  263.9 14.1 collective-permute-done.8
  281.1 31.1 %collective-permute-done.9 = bf16[2,160,1280]{2,1,0:T(8,128)(2,1)S(1)} collective-permute-done((bf16[2,160,1280]{2,1,0:T(8,128)(2,1)S(1)}, bf16[2,160,1280]{2,1,0:T(8,128)(2,1)S(1)}, u32[]{:S(2)}, u32[]{:S(2)}) %collective-permute-start.9) | collective-permute-done | bytes 819232 | tf_op jit(solution)/shard_map/ppermute | solution.py:76
  313.7 9.1 collective-permute-done.10
  335.1 5.8 collective-permute-done.4
  353.7 19.1 %collective-permute-done.6 = bf16[2,128,2560]{2,1,0:T(8,128)(2,1)} collective-permute-done((bf16[2,128,2560]{2,1,0:T(8,128)(2,1)}, bf16[2,128,2560]{2,1,0:T(8,128)(2,1)}, u32[]{:S(2)}, u32[]{:S(2)}) %collective-permute-start.6) | collective-permute-done | bytes 1310752 | tf_op jit(solution)/shard_map/ppermute | solution.py:73
  376.5 23.8 %collective-permute-done.11 = bf16[4,2,160,1280]{3,2,1,0:T(8,128)(2,1)} collective-permute-done((bf16[4,2,160,1280]{3,2,1,0:T(8,128)(2,1)S(1)}, bf16[4,2,160,1280]{3,2,1,0:T(8,128)(2,1)}, u32[]{:S(2)}, u32[]{:S(2)}) %collective-permute-start.11) | collective-permute-done | bytes 3276832 | tf_op jit(solution)/shard_map/ppermute | solution.py:73
  405.1 7.5 fusion.10
  422.0 7.2 collective-permute-done.12
  559.5 5.7 collective-permute-done.13
  606.1 16.9 %collective-permute-done.20 = bf16[128,2560]{1,0:T(8,128)(2,1)} collective-permute-done((bf16[128,2560]{1,0:T(8,128)(2,1)S(1)}, bf16[128,2560]{1,0:T(8,128)(2,1)}, u32[]{:S(2)}, u32[]{:S(2)}) %collective-permute-start.20) | collective-permute-done | bytes 655392 | tf_op jit(solution)/shard_map/ppermute | solution.py:73
  628.3 10.2 collective-permute-start.21
  647.2 7.2 collective-permute-done.21
  655.3 25.7 %collective-permute-done.22 = bf16[128,2560]{1,0:T(8,128)(2,1)S(1)} collective-permute-done((bf16[128,2560]{1,0:T(8,128)(2,1)}, bf16[128,2560]{1,0:T(8,128)(2,1)S(1)}, u32[]{:S(2)}, u32[]{:S(2)}) %collective-permute-start.22) | collective-permute-done | bytes 655392 | tf_op jit(solution)/shard_map/ppermute | solution.py:76
  682.6 15.2 collective-permute-done.23
  710.6 7.7 maximum_select_fusion.2
  718.2 8.0 copy.597
  733.1 6.1 slice.711
  744.7 6.5 maximum_select_fusion.1
  751.2 7.2 fusion.250
  758.5 7.2 fusion.251
  765.6 13.4 multiply_convert_fusion.1
  779.0 8.6 fusion.252
  787.6 8.0 copy.580
  795.6 10.6 fusion.42
  806.2 8.5 fusion.40
  814.8 9.3 convolution_add_fusion
  832.8 8.4 fusion.44
  854.9 10.2 fusion.226
  869.8 11.2 fusion.38
  880.9 8.0 fusion.225
  896.1 16.1 %collective-permute-done.70 = bf16[4,2,80,960]{3,2,0,1:T(8,128)(2,1)} collective-permute-done((bf16[4,2,80,960]{3,2,0,1:T(8,128)(2,1)}, bf16[4,2,80,960]{3,2,0,1:T(8,128)(2,1)}, u32[]{:S(2)}, u32[]{:S(2)}) %collective-permute-start.70) | collective-permute-done | bytes 1228832 | tf_op jit(solution)/shard_map/ppermute | solution.py:73
  919.3 5.7 collective-permute-done.72
  926.1 16.5 %collective-permute-done.95 = bf16[4,2,80,960]{3,2,0,1:T(8,128)(2,1)S(1)} collective-permute-done((bf16[4,2,80,960]{3,2,0,1:T(8,128)(2,1)S(1)}, bf16[4,2,80,960]{3,2,0,1:T(8,128)(2,1)S(1)}, u32[]{:S(2)}, u32[]{:S(2)}) %collective-permute-start.95) | collective-permute-done | bytes 1228832 | tf_op jit(solution)/shard_map/ppermute | solution.py:73
  944.0 9.1 collective-permute-done.97
  954.1 13.0 collective-permute-done.78
  968.7 12.5 collective-permute-done.71
  982.5 11.3 collective-permute-done.96
  1000.7 11.5 collective-permute-done.82
  1012.2 5.4 collective-permute-done.83
  1020.4 17.9 %collective-permute-done.75 = bf16[160,960]{1,0:T(8,128)(2,1)S(1)} collective-permute-done((bf16[160,960]{1,0:T(8,128)(2,1)S(1)}, bf16[160,960]{1,0:T(8,128)(2,1)S(1)}, u32[]{:S(2)}, u32[]{:S(2)}) %collective-permute-start.75) | collective-permute-done | bytes 307232 | tf_op jit(solution)/shard_map/ppermute | solution.py:76
  1038.4 6.8 collective-permute-done.76
  1058.8 10.6 collective-permute-done.57
  1069.4 28.4 %collective-permute-start.47 = (bf16[128,2560]{1,0:T(8,128)(2,1)S(1)}, bf16[128,2560]{1,0:T(8,128)(2,1)S(1)}, u32[]{:S(2)}, u32[]{:S(2)}) collective-permute-start(bf16[128,2560]{1,0:T(8,128)(2,1)S(1)} %get-tuple-element.199), channel_id=1, source_target_pairs={{0,8},{2,10},{4,12},{6,14},{8,16},{10,18},{12,20},{14,22},{16,24},... | collective-permute-start | bytes 1966088 | tf_op jit(solution)/shard_map/ppermute | solution.py:76
  1098.1 48.3 %collective-permute-done.56 = bf16[128,2560]{1,0:T(8,128)(2,1)S(1)} collective-permute-done((bf16[128,2560]{1,0:T(8,128)(2,1)}, bf16[128,2560]{1,0:T(8,128)(2,1)S(1)}, u32[]{:S(2)}, u32[]{:S(2)}) %collective-permute-start.56) | collective-permute-done | bytes 655392 | tf_op jit(solution)/shard_map/ppermute | solution.py:76
  1151.3 30.3 %collective-permute-done.48 = bf16[128,2560]{1,0:T(8,128)(2,1)S(1)} collective-permute-done((bf16[128,2560]{1,0:T(8,128)(2,1)S(1)}, bf16[128,2560]{1,0:T(8,128)(2,1)S(1)}, u32[]{:S(2)}, u32[]{:S(2)}) %collective-permute-start.48) | collective-permute-done | bytes 655392 | tf_op jit(solution)/shard_map/ppermute | solution.py:76
  1220.0 18.2 %collective-permute-done.59 = bf16[2,128,2560]{2,1,0:T(8,128)(2,1)} collective-permute-done((bf16[2,128,2560]{2,1,0:T(8,128)(2,1)}, bf16[2,128,2560]{2,1,0:T(8,128)(2,1)}, u32[]{:S(2)}, u32[]{:S(2)}) %collective-permute-start.59) | collective-permute-done | bytes 1310752 | tf_op jit(solution)/shard_map/ppermute | solution.py:73
  1336.3 11.3 rev.6
  1370.9 5.6 multiply_reduce_fusion.5
  1398.5 5.8 fusion.77
  1419.1 5.8 collective-permute-done.86
  1451.7 41.0 %collective-permute-done.65 = bf16[4,2,160,1280]{3,2,1,0:T(8,128)(2,1)} collective-permute-done((bf16[4,2,160,1280]{3,2,1,0:T(8,128)(2,1)S(1)}, bf16[4,2,160,1280]{3,2,1,0:T(8,128)(2,1)}, u32[]{:S(2)}, u32[]{:S(2)}) %collective-permute-start.65) | collective-permute-done | bytes 3276832 | tf_op jit(solution)/shard_map/ppermute | solution.py:73
  1502.7 5.9 collective-permute-done.94
  1509.6 8.9 collective-permute-done.68
  1518.4 46.3 %collective-permute-done.67 = bf16[2,160,1280]{2,1,0:T(8,128)(2,1)S(1)} collective-permute-done((bf16[2,160,1280]{2,1,0:T(8,128)(2,1)S(1)}, bf16[2,160,1280]{2,1,0:T(8,128)(2,1)S(1)}, u32[]{:S(2)}, u32[]{:S(2)}) %collective-permute-start.67) | collective-permute-done | bytes 819232 | tf_op jit(solution)/shard_map/ppermute | solution.py:76
  1566.8 6.5 collective-permute-done.69
  (1039 shorter events, 715.3 us)
Async XLA Ops:
  7.2 53.0 %collective-permute-start = (bf16[33,1280]{1,0:T(8,128)(2,1)S(1)}, bf16[33,1280]{1,0:T(8,128)(2,1)}, u32[]{:S(2)}, u32[]{:S(2)}) collective-permute-start(bf16[33,1280]{1,0:T(8,128)(2,1)S(1)} %constant_dynamic-update-slice_fusion), channel_id=1, source_target_pairs={{0,8},{2,10},{4,12},{6,14},{8,16},{10,18},{12,20},{14,22},{16,24},... | collective-permute-start | bytes 253448 | tf_op jit(solution)/shard_map/ppermute | solution.py:76
  10.3 51.9 %collective-permute-start.1 = (bf16[33,1280]{1,0:T(8,128)(2,1)S(1)}, bf16[33,1280]{1,0:T(8,128)(2,1)}, u32[]{:S(2)}, u32[]{:S(2)}) collective-permute-start(bf16[33,1280]{1,0:T(8,128)(2,1)S(1)} %constant_dynamic-update-slice_fusion), channel_id=1, source_target_pairs={{0,16},{2,18},{4,20},{6,22},{8,24},{10,26},{12,28},{14,30},{16,0},... | collective-permute-start | bytes 253448 | tf_op jit(solution)/shard_map/ppermute | solution.py:76
  12.9 54.5 %collective-permute-start.2 = (bf16[33,1280]{1,0:T(8,128)(2,1)S(1)}, bf16[33,1280]{1,0:T(8,128)(2,1)}, u32[]{:S(2)}, u32[]{:S(2)}) collective-permute-start(bf16[33,1280]{1,0:T(8,128)(2,1)S(1)} %constant_dynamic-update-slice_fusion), channel_id=1, source_target_pairs={{0,24},{2,26},{4,28},{6,30},{8,0},{10,2},{12,4},{14,6},{16,8},{18,... | collective-permute-start | bytes 253448 | tf_op jit(solution)/shard_map/ppermute | solution.py:76
  16.2 64.5 %collective-permute-start.14 = (bf16[160,640]{1,0:T(8,128)(2,1)}, bf16[160,640]{1,0:T(8,128)(2,1)S(1)}, u32[]{:S(2)}, u32[]{:S(2)}) collective-permute-start(bf16[160,640]{1,0:T(8,128)(2,1)} %get-tuple-element.294), channel_id=1, source_target_pairs={{0,2},{2,0},{4,6},{6,4},{8,10},{10,8},{12,14},{14,12},{16,18},{18,... | collective-permute-start | bytes 614408 | tf_op jit(solution)/shard_map/ppermute | solution.py:73
  30.6 54.3 %collective-permute-start.25 = (bf16[160,960]{1,0:T(8,128)(2,1)}, bf16[160,960]{1,0:T(8,128)(2,1)}, u32[]{:S(2)}, u32[]{:S(2)}) collective-permute-start(bf16[160,960]{1,0:T(8,128)(2,1)} %bitcast.685), channel_id=1, source_target_pairs={{0,8},{2,10},{4,12},{6,14},{8,16},{10,18},{12,20},{14,22},{16,24},... | collective-permute-start | bytes 921608 | tf_op jit(solution)/shard_map/ppermute | solution.py:76
  60.3 188.0 %collective-permute-start.50 = (bf16[128,2560]{1,0:T(8,128)(2,1)}, bf16[128,2560]{1,0:T(8,128)(2,1)}, u32[]{:S(2)}, u32[]{:S(2)}) collective-permute-start(bf16[128,2560]{1,0:T(8,128)(2,1)} %param.33), channel_id=1, source_target_pairs={{0,8},{2,10},{4,12},{6,14},{8,16},{10,18},{12,20},{14,22},{16,24},... | collective-permute-start | bytes 1966088 | tf_op jit(solution)/shard_map/ppermute | solution.py:76
  62.2 188.5 %collective-permute-start.51 = (bf16[128,2560]{1,0:T(8,128)(2,1)}, bf16[128,2560]{1,0:T(8,128)(2,1)}, u32[]{:S(2)}, u32[]{:S(2)}) collective-permute-start(bf16[128,2560]{1,0:T(8,128)(2,1)} %param.33), channel_id=1, source_target_pairs={{0,16},{2,18},{4,20},{6,22},{8,24},{10,26},{12,28},{14,30},{16,0},... | collective-permute-start | bytes 1966088 | tf_op jit(solution)/shard_map/ppermute | solution.py:76
  67.4 186.8 %collective-permute-start.52 = (bf16[128,2560]{1,0:T(8,128)(2,1)}, bf16[128,2560]{1,0:T(8,128)(2,1)}, u32[]{:S(2)}, u32[]{:S(2)}) collective-permute-start(bf16[128,2560]{1,0:T(8,128)(2,1)} %param.33), channel_id=1, source_target_pairs={{0,24},{2,26},{4,28},{6,30},{8,0},{10,2},{12,4},{14,6},{16,8},{18,... | collective-permute-start | bytes 1966088 | tf_op jit(solution)/shard_map/ppermute | solution.py:76
  80.7 53.0 %collective-permute-start.26 = (bf16[160,960]{1,0:T(8,128)(2,1)}, bf16[160,960]{1,0:T(8,128)(2,1)S(1)}, u32[]{:S(2)}, u32[]{:S(2)}) collective-permute-start(bf16[160,960]{1,0:T(8,128)(2,1)} %bitcast.792), channel_id=1, source_target_pairs={{0,16},{2,18},{4,20},{6,22},{8,24},{10,26},{12,28},{14,30},{16,0},... | collective-permute-start | bytes 921608 | tf_op jit(solution)/shard_map/ppermute | solution.py:76
  84.9 54.3 %collective-permute-start.27 = (bf16[160,960]{1,0:T(8,128)(2,1)S(1)}, bf16[160,960]{1,0:T(8,128)(2,1)S(1)}, u32[]{:S(2)}, u32[]{:S(2)}) collective-permute-start(bf16[160,960]{1,0:T(8,128)(2,1)S(1)} %bitcast.791), channel_id=1, source_target_pairs={{0,24},{2,26},{4,28},{6,30},{8,0},{10,2},{12,4},{14,6},{16,8},{18,... | collective-permute-start | bytes 921608 | tf_op jit(solution)/shard_map/ppermute | solution.py:76
  169.8 41.8 %collective-permute-start.7 = (bf16[160,1280]{1,0:T(8,128)(2,1)S(1)}, bf16[160,1280]{1,0:T(8,128)(2,1)S(1)}, u32[]{:S(2)}, u32[]{:S(2)}) collective-permute-start(bf16[160,1280]{1,0:T(8,128)(2,1)S(1)} %copy-done.105), channel_id=1, source_target_pairs={{0,2},{2,0},{4,6},{6,4},{8,10},{10,8},{12,14},{14,12},{16,18},{18,... | collective-permute-start | bytes 1228808 | tf_op jit(solution)/shard_map/ppermute | solution.py:73
  215.0 27.1 %collective-permute-start.16 = (bf16[2,160,640]{2,1,0:T(8,128)(2,1)S(1)}, bf16[2,160,640]{2,1,0:T(8,128)(2,1)S(1)}, u32[]{:S(2)}, u32[]{:S(2)}) collective-permute-start(bf16[2,160,640]{2,1,0:T(8,128)(2,1)S(1)} %maximum_select_fusion.46), channel_id=1, source_target_pairs={{0,16},{2,18},{4,20},{6,22},{8,24},{10,26},{12,28},{14,30},{16,0},... | collective-permute-start | bytes 1228808 | tf_op jit(solution)/shard_map/ppermute | solution.py:76
  246.9 76.5 %collective-permute-start.30 = (bf16[4,80,960]{2,1,0:T(8,128)(2,1)S(1)}, bf16[4,80,960]{2,1,0:T(8,128)(2,1)S(1)}, u32[]{:S(2)}, u32[]{:S(2)}) collective-permute-start(bf16[4,80,960]{2,1,0:T(8,128)(2,1)S(1)} %get-tuple-element.236), channel_id=1, source_target_pairs={{0,2},{2,0},{4,6},{6,4},{8,10},{10,8},{12,14},{14,12},{16,18},{18,... | collective-permute-start | bytes 1843208 | tf_op jit(solution)/shard_map/ppermute | solution.py:73
  248.3 79.5 %collective-permute-start.28 = (bf16[4,80,960]{2,1,0:T(8,128)(2,1)S(1)}, bf16[4,80,960]{2,1,0:T(8,128)(2,1)S(1)}, u32[]{:S(2)}, u32[]{:S(2)}) collective-permute-start(bf16[4,80,960]{2,1,0:T(8,128)(2,1)S(1)} %get-tuple-element.237), channel_id=1, source_target_pairs={{0,4},{2,6},{4,0},{6,2},{8,12},{10,14},{12,8},{14,10},{16,20},{18,... | collective-permute-start | bytes 1843208 | tf_op jit(solution)/shard_map/ppermute | solution.py:73
  250.7 81.2 %collective-permute-start.37 = (bf16[4,80,960]{2,1,0:T(8,128)(2,1)S(1)}, bf16[4,80,960]{2,1,0:T(8,128)(2,1)S(1)}, u32[]{:S(2)}, u32[]{:S(2)}) collective-permute-start(bf16[4,80,960]{2,1,0:T(8,128)(2,1)S(1)} %get-tuple-element.246), channel_id=1, source_target_pairs={{0,2},{2,0},{4,6},{6,4},{8,10},{10,8},{12,14},{14,12},{16,18},{18,... | collective-permute-start | bytes 1843208 | tf_op jit(solution)/shard_map/ppermute | solution.py:73
  260.6 51.5 %collective-permute-start.9 = (bf16[2,160,1280]{2,1,0:T(8,128)(2,1)S(1)}, bf16[2,160,1280]{2,1,0:T(8,128)(2,1)S(1)}, u32[]{:S(2)}, u32[]{:S(2)}) collective-permute-start(bf16[2,160,1280]{2,1,0:T(8,128)(2,1)S(1)} %maximum_select_fusion.34), channel_id=1, source_target_pairs={{0,16},{2,18},{4,20},{6,22},{8,24},{10,26},{12,28},{14,30},{16,0},... | collective-permute-start | bytes 2457608 | tf_op jit(solution)/shard_map/ppermute | solution.py:76
  278.0 44.8 %collective-permute-start.10 = (bf16[2,160,1280]{2,1,0:T(8,128)(2,1)S(1)}, bf16[2,160,1280]{2,1,0:T(8,128)(2,1)S(1)}, u32[]{:S(2)}, u32[]{:S(2)}) collective-permute-start(bf16[2,160,1280]{2,1,0:T(8,128)(2,1)S(1)} %maximum_select_fusion.34), channel_id=1, source_target_pairs={{0,24},{2,26},{4,28},{6,30},{8,0},{10,2},{12,4},{14,6},{16,8},{18,... | collective-permute-start | bytes 2457608 | tf_op jit(solution)/shard_map/ppermute | solution.py:76
  312.1 258.1 %collective-permute-start.35 = (bf16[4,80,960]{2,1,0:T(8,128)(2,1)}, bf16[4,80,960]{2,1,0:T(8,128)(2,1)}, u32[]{:S(2)}, u32[]{:S(2)}) collective-permute-start(bf16[4,80,960]{2,1,0:T(8,128)(2,1)} %get-tuple-element.247), channel_id=1, source_target_pairs={{0,4},{2,6},{4,0},{6,2},{8,12},{10,14},{12,8},{14,10},{16,20},{18,... | collective-permute-start | bytes 1843208 | tf_op jit(solution)/shard_map/ppermute | solution.py:73
  323.4 76.8 %collective-permute-start.11 = (bf16[4,2,160,1280]{3,2,1,0:T(8,128)(2,1)S(1)}, bf16[4,2,160,1280]{3,2,1,0:T(8,128)(2,1)}, u32[]{:S(2)}, u32[]{:S(2)}) collective-permute-start(bf16[4,2,160,1280]{3,2,1,0:T(8,128)(2,1)S(1)} %bitcast_dynamic-update-slice_fusion), channel_id=1, source_target_pairs={{0,4},{2,6},{4,0},{6,2},{8,12},{10,14},{12,8},{14,10},{16,20},{18,... | collective-permute-start | bytes 9830408 | tf_op jit(solution)/shard_map/ppermute | solution.py:73
  327.7 249.2 %collective-permute-start.44 = (bf16[4,80,960]{2,1,0:T(8,128)(2,1)}, bf16[4,80,960]{2,1,0:T(8,128)(2,1)}, u32[]{:S(2)}, u32[]{:S(2)}) collective-permute-start(bf16[4,80,960]{2,1,0:T(8,128)(2,1)} %get-tuple-element.256), channel_id=1, source_target_pairs={{0,2},{2,0},{4,6},{6,4},{8,10},{10,8},{12,14},{14,12},{16,18},{18,... | collective-permute-start | bytes 1843208 | tf_op jit(solution)/shard_map/ppermute | solution.py:73
  331.9 251.0 %collective-permute-start.42 = (bf16[4,80,960]{2,1,0:T(8,128)(2,1)}, bf16[4,80,960]{2,1,0:T(8,128)(2,1)}, u32[]{:S(2)}, u32[]{:S(2)}) collective-permute-start(bf16[4,80,960]{2,1,0:T(8,128)(2,1)} %get-tuple-element.257), channel_id=1, source_target_pairs={{0,4},{2,6},{4,0},{6,2},{8,12},{10,14},{12,8},{14,10},{16,20},{18,... | collective-permute-start | bytes 1843208 | tf_op jit(solution)/shard_map/ppermute | solution.py:73
  340.9 31.8 %collective-permute-start.6 = (bf16[2,128,2560]{2,1,0:T(8,128)(2,1)}, bf16[2,128,2560]{2,1,0:T(8,128)(2,1)}, u32[]{:S(2)}, u32[]{:S(2)}) collective-permute-start(bf16[2,128,2560]{2,1,0:T(8,128)(2,1)} %maximum_select_fusion.18), channel_id=1, source_target_pairs={{0,2},{2,0},{4,6},{6,4},{8,10},{10,8},{12,14},{14,12},{16,18},{18,... | collective-permute-start | bytes 3932168 | tf_op jit(solution)/shard_map/ppermute | solution.py:73
  372.7 182.3 %collective-permute-start.18 = (bf16[4,2,160,640]{3,2,1,0:T(8,128)(2,1)}, bf16[4,2,160,640]{3,2,1,0:T(8,128)(2,1)}, u32[]{:S(2)}, u32[]{:S(2)}) collective-permute-start(bf16[4,2,160,640]{3,2,1,0:T(8,128)(2,1)} %bitcast_dynamic-update-slice_fusion.11), channel_id=1, source_target_pairs={{0,4},{2,6},{4,0},{6,2},{8,12},{10,14},{12,8},{14,10},{16,20},{18,... | collective-permute-start | bytes 4915208 | tf_op jit(solution)/shard_map/ppermute | solution.py:73
  429.3 281.3 %collective-permute-start.53 = (bf16[4,128,2560]{2,1,0:T(8,128)(2,1)}, bf16[4,128,2560]{2,1,0:T(8,128)(2,1)}, u32[]{:S(2)}, u32[]{:S(2)}) collective-permute-start(bf16[4,128,2560]{2,1,0:T(8,128)(2,1)} %bitcast_dynamic-update-slice_fusion.3), channel_id=1, source_target_pairs={{0,1},{1,0},{2,3},{3,2},{4,5},{5,4},{6,7},{7,6},{8,9},{9,8},{10,11... | collective-permute-start | bytes 7864328 | tf_op jit(solution)/shard_map/ppermute | solution.py:71
  565.2 38.1 %collective-permute-start.31 = (bf16[2,4,80,960]{3,2,1,0:T(8,128)(2,1)}, bf16[2,4,80,960]{3,2,1,0:T(8,128)(2,1)}, u32[]{:S(2)}, u32[]{:S(2)}) collective-permute-start(bf16[2,4,80,960]{3,2,1,0:T(8,128)(2,1)} %maximum_select_fusion.23), channel_id=1, source_target_pairs={{0,4},{2,6},{4,0},{6,2},{8,12},{10,14},{12,8},{14,10},{16,20},{18,... | collective-permute-start | bytes 3686408 | tf_op jit(solution)/shard_map/ppermute | solution.py:73
  576.9 51.3 %collective-permute-start.29 = (bf16[2,4,80,960]{3,2,1,0:T(8,128)(2,1)}, bf16[2,4,80,960]{3,2,1,0:T(8,128)(2,1)}, u32[]{:S(2)}, u32[]{:S(2)}) collective-permute-start(bf16[2,4,80,960]{3,2,1,0:T(8,128)(2,1)} %maximum_select_fusion.21), channel_id=1, source_target_pairs={{0,2},{2,0},{4,6},{6,4},{8,10},{10,8},{12,14},{14,12},{16,18},{18,... | collective-permute-start | bytes 3686408 | tf_op jit(solution)/shard_map/ppermute | solution.py:73
  582.9 61.6 %collective-permute-start.38 = (bf16[2,4,80,960]{3,2,1,0:T(8,128)(2,1)}, bf16[2,4,80,960]{3,2,1,0:T(8,128)(2,1)}, u32[]{:S(2)}, u32[]{:S(2)}) collective-permute-start(bf16[2,4,80,960]{3,2,1,0:T(8,128)(2,1)} %maximum_select_fusion.26), channel_id=1, source_target_pairs={{0,4},{2,6},{4,0},{6,2},{8,12},{10,14},{12,8},{14,10},{16,20},{18,... | collective-permute-start | bytes 3686408 | tf_op jit(solution)/shard_map/ppermute | solution.py:73
  595.3 27.7 %collective-permute-start.20 = (bf16[128,2560]{1,0:T(8,128)(2,1)S(1)}, bf16[128,2560]{1,0:T(8,128)(2,1)}, u32[]{:S(2)}, u32[]{:S(2)}) collective-permute-start(bf16[128,2560]{1,0:T(8,128)(2,1)S(1)} %fusion.111), channel_id=1, source_target_pairs={{0,2},{2,0},{4,6},{6,4},{8,10},{10,8},{12,14},{14,12},{16,18},{18,... | collective-permute-start | bytes 1966088 | tf_op jit(solution)/shard_map/ppermute | solution.py:73
  603.4 95.4 %collective-permute-start.36 = (bf16[2,4,80,960]{3,2,1,0:T(8,128)(2,1)}, bf16[2,4,80,960]{3,2,1,0:T(8,128)(2,1)}, u32[]{:S(2)}, u32[]{:S(2)}) collective-permute-start(bf16[2,4,80,960]{3,2,1,0:T(8,128)(2,1)} %maximum_select_fusion.24), channel_id=1, source_target_pairs={{0,2},{2,0},{4,6},{6,4},{8,10},{10,8},{12,14},{14,12},{16,18},{18,... | collective-permute-start | bytes 3686408 | tf_op jit(solution)/shard_map/ppermute | solution.py:73
  623.0 81.8 %collective-permute-start.45 = (bf16[2,4,80,960]{3,2,1,0:T(8,128)(2,1)S(1)}, bf16[2,4,80,960]{3,2,1,0:T(8,128)(2,1)S(1)}, u32[]{:S(2)}, u32[]{:S(2)}) collective-permute-start(bf16[2,4,80,960]{3,2,1,0:T(8,128)(2,1)S(1)} %copy-done.92), channel_id=1, source_target_pairs={{0,4},{2,6},{4,0},{6,2},{8,12},{10,14},{12,8},{14,10},{16,20},{18,... | collective-permute-start | bytes 3686408 | tf_op jit(solution)/shard_map/ppermute | solution.py:73
  628.3 26.1 %collective-permute-start.21 = (bf16[128,2560]{1,0:T(8,128)(2,1)}, bf16[128,2560]{1,0:T(8,128)(2,1)S(1)}, u32[]{:S(2)}, u32[]{:S(2)}) collective-permute-start(bf16[128,2560]{1,0:T(8,128)(2,1)} %get-tuple-element.173), channel_id=1, source_target_pairs={{0,8},{2,10},{4,12},{6,14},{8,16},{10,18},{12,20},{14,22},{16,24},... | collective-permute-start | bytes 1966088 | tf_op jit(solution)/shard_map/ppermute | solution.py:76
  644.5 60.9 %collective-permute-start.43 = (bf16[2,4,80,960]{3,2,1,0:T(8,128)(2,1)S(1)}, bf16[2,4,80,960]{3,2,1,0:T(8,128)(2,1)S(1)}, u32[]{:S(2)}, u32[]{:S(2)}) collective-permute-start(bf16[2,4,80,960]{3,2,1,0:T(8,128)(2,1)S(1)} %copy-done.93), channel_id=1, source_target_pairs={{0,2},{2,0},{4,6},{6,4},{8,10},{10,8},{12,14},{14,12},{16,18},{18,... | collective-permute-start | bytes 3686408 | tf_op jit(solution)/shard_map/ppermute | solution.py:73
  654.4 26.6 %collective-permute-start.22 = (bf16[128,2560]{1,0:T(8,128)(2,1)}, bf16[128,2560]{1,0:T(8,128)(2,1)S(1)}, u32[]{:S(2)}, u32[]{:S(2)}) collective-permute-start(bf16[128,2560]{1,0:T(8,128)(2,1)} %get-tuple-element.173), channel_id=1, source_target_pairs={{0,16},{2,18},{4,20},{6,22},{8,24},{10,26},{12,28},{14,30},{16,0},... | collective-permute-start | bytes 1966088 | tf_op jit(solution)/shard_map/ppermute | solution.py:76
  698.7 45.9 %collective-permute-start.24 = (bf16[4,128,2560]{2,1,0:T(8,128)(2,1)}, bf16[4,128,2560]{2,1,0:T(8,128)(2,1)}, u32[]{:S(2)}, u32[]{:S(2)}) collective-permute-start(bf16[4,128,2560]{2,1,0:T(8,128)(2,1)} %bitcast_dynamic-update-slice_fusion.7), channel_id=1, source_target_pairs={{0,1},{1,0},{2,3},{3,2},{4,5},{5,4},{6,7},{7,6},{8,9},{9,8},{10,11... | collective-permute-start | bytes 7864328 | tf_op jit(solution)/shard_map/ppermute | solution.py:71
  829.7 215.9 %collective-permute-start.54 = (bf16[4,128,2560]{2,1,0:T(8,128)(2,1)}, bf16[4,128,2560]{2,1,0:T(8,128)(2,1)}, u32[]{:S(2)}, u32[]{:S(2)}) collective-permute-start(bf16[4,128,2560]{2,1,0:T(8,128)(2,1)} %fusion.12), channel_id=1, source_target_pairs={{0,1},{1,0},{2,3},{3,2},{4,5},{5,4},{6,7},{7,6},{8,9},{9,8},{10,11... | collective-permute-start | bytes 7864328 | tf_op jit(solution)/shard_map/ppermute | solution.py:71
  846.0 207.4 %collective-permute-start.46 = (bf16[4,128,2560]{2,1,0:T(8,128)(2,1)}, bf16[4,128,2560]{2,1,0:T(8,128)(2,1)S(1)}, u32[]{:S(2)}, u32[]{:S(2)}) collective-permute-start(bf16[4,128,2560]{2,1,0:T(8,128)(2,1)} %fusion.11), channel_id=1, source_target_pairs={{0,1},{1,0},{2,3},{3,2},{4,5},{5,4},{6,7},{7,6},{8,9},{9,8},{10,11... | collective-permute-start | bytes 7864328 | tf_op jit(solution)/shard_map/ppermute | solution.py:71
  852.6 40.6 %collective-permute-start.77 = (bf16[4,2,80,960]{3,2,0,1:T(8,128)(2,1)}, bf16[4,2,80,960]{3,2,0,1:T(8,128)(2,1)}, u32[]{:S(2)}, u32[]{:S(2)}) collective-permute-start(bf16[4,2,80,960]{3,2,0,1:T(8,128)(2,1)} %fusion.71), channel_id=1, source_target_pairs={{0,2},{2,0},{4,6},{6,4},{8,10},{10,8},{12,14},{14,12},{16,18},{18,... | collective-permute-start | bytes 3686408 | tf_op jit(solution)/shard_map/ppermute | solution.py:73
  853.3 62.1 %collective-permute-start.79 = (bf16[4,2,80,960]{3,2,1,0:T(8,128)(2,1)S(1)}, bf16[4,2,80,960]{3,2,1,0:T(8,128)(2,1)}, u32[]{:S(2)}, u32[]{:S(2)}) collective-permute-start(bf16[4,2,80,960]{3,2,1,0:T(8,128)(2,1)S(1)} %fusion.68), channel_id=1, source_target_pairs={{0,4},{2,6},{4,0},{6,2},{8,12},{10,14},{12,8},{14,10},{16,20},{18,... | collective-permute-start | bytes 3686408 | tf_op jit(solution)/shard_map/ppermute | solution.py:73
  868.3 43.9 %collective-permute-start.70 = (bf16[4,2,80,960]{3,2,0,1:T(8,128)(2,1)}, bf16[4,2,80,960]{3,2,0,1:T(8,128)(2,1)}, u32[]{:S(2)}, u32[]{:S(2)}) collective-permute-start(bf16[4,2,80,960]{3,2,0,1:T(8,128)(2,1)} %fusion.70), channel_id=1, source_target_pairs={{0,2},{2,0},{4,6},{6,4},{8,10},{10,8},{12,14},{14,12},{16,18},{18,... | collective-permute-start | bytes 3686408 | tf_op jit(solution)/shard_map/ppermute | solution.py:73
  893.2 31.8 %collective-permute-start.72 = (bf16[4,2,80,960]{3,2,1,0:T(8,128)(2,1)S(1)}, bf16[4,2,80,960]{3,2,1,0:T(8,128)(2,1)S(1)}, u32[]{:S(2)}, u32[]{:S(2)}) collective-permute-start(bf16[4,2,80,960]{3,2,1,0:T(8,128)(2,1)S(1)} %fusion.67), channel_id=1, source_target_pairs={{0,4},{2,6},{4,0},{6,2},{8,12},{10,14},{12,8},{14,10},{16,20},{18,... | collective-permute-start | bytes 3686408 | tf_op jit(solution)/shard_map/ppermute | solution.py:73
  912.2 30.4 %collective-permute-start.95 = (bf16[4,2,80,960]{3,2,0,1:T(8,128)(2,1)S(1)}, bf16[4,2,80,960]{3,2,0,1:T(8,128)(2,1)S(1)}, u32[]{:S(2)}, u32[]{:S(2)}) collective-permute-start(bf16[4,2,80,960]{3,2,0,1:T(8,128)(2,1)S(1)} %fusion.72), channel_id=1, source_target_pairs={{0,2},{2,0},{4,6},{6,4},{8,10},{10,8},{12,14},{14,12},{16,18},{18,... | collective-permute-start | bytes 3686408 | tf_op jit(solution)/shard_map/ppermute | solution.py:73
  915.4 37.6 %collective-permute-start.97 = (bf16[4,2,80,960]{3,2,1,0:T(8,128)(2,1)S(1)}, bf16[4,2,80,960]{3,2,1,0:T(8,128)(2,1)S(1)}, u32[]{:S(2)}, u32[]{:S(2)}) collective-permute-start(bf16[4,2,80,960]{3,2,1,0:T(8,128)(2,1)S(1)} %fusion.69), channel_id=1, source_target_pairs={{0,4},{2,6},{4,0},{6,2},{8,12},{10,14},{12,8},{14,10},{16,20},{18,... | collective-permute-start | bytes 3686408 | tf_op jit(solution)/shard_map/ppermute | solution.py:73
  925.0 42.1 %collective-permute-start.78 = (bf16[4,80,960]{2,1,0:T(8,128)(2,1)S(1)}, bf16[4,80,960]{2,1,0:T(8,128)(2,1)S(1)}, u32[]{:S(2)}, u32[]{:S(2)}) collective-permute-start(bf16[4,80,960]{2,1,0:T(8,128)(2,1)S(1)} %fusion.121), channel_id=1, source_target_pairs={{0,4},{2,6},{4,0},{6,2},{8,12},{10,14},{12,8},{14,10},{16,20},{18,... | collective-permute-start | bytes 1843208 | tf_op jit(solution)/shard_map/ppermute | solution.py:73
  953.1 28.1 %collective-permute-start.71 = (bf16[4,80,960]{2,1,0:T(8,128)(2,1)S(1)}, bf16[4,80,960]{2,1,0:T(8,128)(2,1)S(1)}, u32[]{:S(2)}, u32[]{:S(2)}) collective-permute-start(bf16[4,80,960]{2,1,0:T(8,128)(2,1)S(1)} %fusion.119), channel_id=1, source_target_pairs={{0,4},{2,6},{4,0},{6,2},{8,12},{10,14},{12,8},{14,10},{16,20},{18,... | collective-permute-start | bytes 1843208 | tf_op jit(solution)/shard_map/ppermute | solution.py:73
  1012.2 26.2 %collective-permute-start.75 = (bf16[160,960]{1,0:T(8,128)(2,1)S(1)}, bf16[160,960]{1,0:T(8,128)(2,1)S(1)}, u32[]{:S(2)}, u32[]{:S(2)}) collective-permute-start(bf16[160,960]{1,0:T(8,128)(2,1)S(1)} %get-tuple-element.222), channel_id=1, source_target_pairs={{0,16},{2,18},{4,20},{6,22},{8,24},{10,26},{12,28},{14,30},{16,0},... | collective-permute-start | bytes 921608 | tf_op jit(solution)/shard_map/ppermute | solution.py:76
  1017.6 27.6 %collective-permute-start.76 = (bf16[160,960]{1,0:T(8,128)(2,1)S(1)}, bf16[160,960]{1,0:T(8,128)(2,1)S(1)}, u32[]{:S(2)}, u32[]{:S(2)}) collective-permute-start(bf16[160,960]{1,0:T(8,128)(2,1)S(1)} %get-tuple-element.219), channel_id=1, source_target_pairs={{0,24},{2,26},{4,28},{6,30},{8,0},{10,2},{12,4},{14,6},{16,8},{18,... | collective-permute-start | bytes 921608 | tf_op jit(solution)/shard_map/ppermute | solution.py:76
  1052.6 93.8 %collective-permute-start.56 = (bf16[128,2560]{1,0:T(8,128)(2,1)}, bf16[128,2560]{1,0:T(8,128)(2,1)S(1)}, u32[]{:S(2)}, u32[]{:S(2)}) collective-permute-start(bf16[128,2560]{1,0:T(8,128)(2,1)} %get-tuple-element.198), channel_id=1, source_target_pairs={{0,16},{2,18},{4,20},{6,22},{8,24},{10,26},{12,28},{14,30},{16,0},... | collective-permute-start | bytes 1966088 | tf_op jit(solution)/shard_map/ppermute | solution.py:76
  1053.3 93.1 %collective-permute-start.55 = (bf16[128,2560]{1,0:T(8,128)(2,1)}, bf16[128,2560]{1,0:T(8,128)(2,1)S(1)}, u32[]{:S(2)}, u32[]{:S(2)}) collective-permute-start(bf16[128,2560]{1,0:T(8,128)(2,1)} %get-tuple-element.196), channel_id=1, source_target_pairs={{0,8},{2,10},{4,12},{6,14},{8,16},{10,18},{12,20},{14,22},{16,24},... | collective-permute-start | bytes 1966088 | tf_op jit(solution)/shard_map/ppermute | solution.py:76
  1054.5 92.7 %collective-permute-start.49 = (bf16[128,2560]{1,0:T(8,128)(2,1)S(1)}, bf16[128,2560]{1,0:T(8,128)(2,1)S(1)}, u32[]{:S(2)}, u32[]{:S(2)}) collective-permute-start(bf16[128,2560]{1,0:T(8,128)(2,1)S(1)} %get-tuple-element.200), channel_id=1, source_target_pairs={{0,24},{2,26},{4,28},{6,30},{8,0},{10,2},{12,4},{14,6},{16,8},{18,... | collective-permute-start | bytes 1966088 | tf_op jit(solution)/shard_map/ppermute | solution.py:76
  1058.4 123.2 %collective-permute-start.48 = (bf16[128,2560]{1,0:T(8,128)(2,1)S(1)}, bf16[128,2560]{1,0:T(8,128)(2,1)S(1)}, u32[]{:S(2)}, u32[]{:S(2)}) collective-permute-start(bf16[128,2560]{1,0:T(8,128)(2,1)S(1)} %get-tuple-element.201), channel_id=1, source_target_pairs={{0,16},{2,18},{4,20},{6,22},{8,24},{10,26},{12,28},{14,30},{16,0},... | collective-permute-start | bytes 1966088 | tf_op jit(solution)/shard_map/ppermute | solution.py:76
  1069.4 112.2 %collective-permute-start.47 = (bf16[128,2560]{1,0:T(8,128)(2,1)S(1)}, bf16[128,2560]{1,0:T(8,128)(2,1)S(1)}, u32[]{:S(2)}, u32[]{:S(2)}) collective-permute-start(bf16[128,2560]{1,0:T(8,128)(2,1)S(1)} %get-tuple-element.199), channel_id=1, source_target_pairs={{0,8},{2,10},{4,12},{6,14},{8,16},{10,18},{12,20},{14,22},{16,24},... | collective-permute-start | bytes 1966088 | tf_op jit(solution)/shard_map/ppermute | solution.py:76
  1146.4 38.8 %collective-permute-start.99 = (bf16[160,960]{1,0:T(8,128)(2,1)S(1)}, bf16[160,960]{1,0:T(8,128)(2,1)S(1)}, u32[]{:S(2)}, u32[]{:S(2)}) collective-permute-start(bf16[160,960]{1,0:T(8,128)(2,1)S(1)} %copy-done.106), channel_id=1, source_target_pairs={{0,8},{2,10},{4,12},{6,14},{8,16},{10,18},{12,20},{14,22},{16,24},... | collective-permute-start | bytes 921608 | tf_op jit(solution)/shard_map/ppermute | solution.py:76
  1146.5 54.2 %collective-permute-start.100 = (bf16[160,960]{1,0:T(8,128)(2,1)}, bf16[160,960]{1,0:T(8,128)(2,1)}, u32[]{:S(2)}, u32[]{:S(2)}) collective-permute-start(bf16[160,960]{1,0:T(8,128)(2,1)} %get-tuple-element.218), channel_id=1, source_target_pairs={{0,16},{2,18},{4,20},{6,22},{8,24},{10,26},{12,28},{14,30},{16,0},... | collective-permute-start | bytes 921608 | tf_op jit(solution)/shard_map/ppermute | solution.py:76
  1147.3 55.1 %collective-permute-start.101 = (bf16[160,960]{1,0:T(8,128)(2,1)}, bf16[160,960]{1,0:T(8,128)(2,1)}, u32[]{:S(2)}, u32[]{:S(2)}) collective-permute-start(bf16[160,960]{1,0:T(8,128)(2,1)} %get-tuple-element.215), channel_id=1, source_target_pairs={{0,24},{2,26},{4,28},{6,30},{8,0},{10,2},{12,4},{14,6},{16,8},{18,... | collective-permute-start | bytes 921608 | tf_op jit(solution)/shard_map/ppermute | solution.py:76
  1206.8 31.5 %collective-permute-start.59 = (bf16[2,128,2560]{2,1,0:T(8,128)(2,1)}, bf16[2,128,2560]{2,1,0:T(8,128)(2,1)}, u32[]{:S(2)}, u32[]{:S(2)}) collective-permute-start(bf16[2,128,2560]{2,1,0:T(8,128)(2,1)} %maximum_select_fusion.31), channel_id=1, source_target_pairs={{0,2},{2,0},{4,6},{6,4},{8,10},{10,8},{12,14},{14,12},{16,18},{18,... | collective-permute-start | bytes 3932168 | tf_op jit(solution)/shard_map/ppermute | solution.py:73
  1256.8 186.5 %collective-permute-start.90 = (bf16[4,2,160,640]{3,2,1,0:T(8,128)(2,1)}, bf16[4,2,160,640]{3,2,1,0:T(8,128)(2,1)}, u32[]{:S(2)}, u32[]{:S(2)}) collective-permute-start(bf16[4,2,160,640]{3,2,1,0:T(8,128)(2,1)} %fusion.46), channel_id=1, source_target_pairs={{0,4},{2,6},{4,0},{6,2},{8,12},{10,14},{12,8},{14,10},{16,20},{18,... | collective-permute-start | bytes 4915208 | tf_op jit(solution)/shard_map/ppermute | solution.py:73
  1329.0 66.9 %collective-permute-start.62 = (bf16[256,640]{1,0:T(8,128)(2,1)}, bf16[256,640]{1,0:T(8,128)(2,1)}, u32[]{:S(2)}, u32[]{:S(2)}) collective-permute-start(bf16[256,640]{1,0:T(8,128)(2,1)} %get-tuple-element.276), channel_id=1, source_target_pairs={{0,2},{2,0},{4,6},{6,4},{8,10},{10,8},{12,14},{14,12},{16,18},{18,... | collective-permute-start | bytes 983048 | tf_op jit(solution)/shard_map/ppermute | solution.py:73
  1417.0 75.8 %collective-permute-start.65 = (bf16[4,2,160,1280]{3,2,1,0:T(8,128)(2,1)S(1)}, bf16[4,2,160,1280]{3,2,1,0:T(8,128)(2,1)}, u32[]{:S(2)}, u32[]{:S(2)}) collective-permute-start(bf16[4,2,160,1280]{3,2,1,0:T(8,128)(2,1)S(1)} %fusion.9), channel_id=1, source_target_pairs={{0,4},{2,6},{4,0},{6,2},{8,12},{10,14},{12,8},{14,10},{16,20},{18,... | collective-permute-start | bytes 9830408 | tf_op jit(solution)/shard_map/ppermute | solution.py:73
  1446.5 51.7 %collective-permute-start.93 = (bf16[2,160,640]{2,1,0:T(8,128)(2,1)S(1)}, bf16[2,160,640]{2,1,0:T(8,128)(2,1)S(1)}, u32[]{:S(2)}, u32[]{:S(2)}) collective-permute-start(bf16[2,160,640]{2,1,0:T(8,128)(2,1)S(1)} %get-tuple-element.203), channel_id=1, source_target_pairs={{0,24},{2,26},{4,28},{6,30},{8,0},{10,2},{12,4},{14,6},{16,8},{18,... | collective-permute-start | bytes 1228808 | tf_op jit(solution)/shard_map/ppermute | solution.py:76
  1447.6 52.6 %collective-permute-start.92 = (bf16[2,160,640]{2,1,0:T(8,128)(2,1)S(1)}, bf16[2,160,640]{2,1,0:T(8,128)(2,1)S(1)}, u32[]{:S(2)}, u32[]{:S(2)}) collective-permute-start(bf16[2,160,640]{2,1,0:T(8,128)(2,1)S(1)} %get-tuple-element.204), channel_id=1, source_target_pairs={{0,16},{2,18},{4,20},{6,22},{8,24},{10,26},{12,28},{14,30},{16,0},... | collective-permute-start | bytes 1228808 | tf_op jit(solution)/shard_map/ppermute | solution.py:76
  1448.2 52.0 %collective-permute-start.91 = (bf16[2,160,640]{2,1,0:T(8,128)(2,1)S(1)}, bf16[2,160,640]{2,1,0:T(8,128)(2,1)S(1)}, u32[]{:S(2)}, u32[]{:S(2)}) collective-permute-start(bf16[2,160,640]{2,1,0:T(8,128)(2,1)S(1)} %get-tuple-element.202), channel_id=1, source_target_pairs={{0,8},{2,10},{4,12},{6,14},{8,16},{10,18},{12,20},{14,22},{16,24},... | collective-permute-start | bytes 1228808 | tf_op jit(solution)/shard_map/ppermute | solution.py:76
  1497.6 67.2 %collective-permute-start.67 = (bf16[2,160,1280]{2,1,0:T(8,128)(2,1)S(1)}, bf16[2,160,1280]{2,1,0:T(8,128)(2,1)S(1)}, u32[]{:S(2)}, u32[]{:S(2)}) collective-permute-start(bf16[2,160,1280]{2,1,0:T(8,128)(2,1)S(1)} %get-tuple-element.191), channel_id=1, source_target_pairs={{0,16},{2,18},{4,20},{6,22},{8,24},{10,26},{12,28},{14,30},{16,0},... | collective-permute-start | bytes 2457608 | tf_op jit(solution)/shard_map/ppermute | solution.py:76
  1498.3 66.5 %collective-permute-start.66 = (bf16[2,160,1280]{2,1,0:T(8,128)(2,1)S(1)}, bf16[2,160,1280]{2,1,0:T(8,128)(2,1)S(1)}, u32[]{:S(2)}, u32[]{:S(2)}) collective-permute-start(bf16[2,160,1280]{2,1,0:T(8,128)(2,1)S(1)} %get-tuple-element.189), channel_id=1, source_target_pairs={{0,8},{2,10},{4,12},{6,14},{8,16},{10,18},{12,20},{14,22},{16,24},... | collective-permute-start | bytes 2457608 | tf_op jit(solution)/shard_map/ppermute | solution.py:76
  1501.3 64.8 %collective-permute-start.64 = (bf16[128,2560]{1,0:T(8,128)(2,1)S(1)}, bf16[128,2560]{1,0:T(8,128)(2,1)S(1)}, u32[]{:S(2)}, u32[]{:S(2)}) collective-permute-start(bf16[128,2560]{1,0:T(8,128)(2,1)S(1)} %fusion.118), channel_id=1, source_target_pairs={{0,2},{2,0},{4,6},{6,4},{8,10},{10,8},{12,14},{14,12},{16,18},{18,... | collective-permute-start | bytes 1966088 | tf_op jit(solution)/shard_map/ppermute | solution.py:73
  (217 other events, 2922.5 us)

commit v2 on v1

v2 whole, which is shorter than its diff:
```python
import math

import jax
import jax.numpy as jnp
from jax import lax
from jax.experimental import pallas as pl
from jax.experimental.pallas import tpu as pltpu
from jax.sharding import PartitionSpec as P

EPSILON = 1e-06
F32 = jnp.float32
BF16 = jnp.bfloat16


def matmul(left, right):
    return jnp.dot(left, right, preferred_element_type=F32)


def contract_last(left, right):
    return lax.dot_general(left, right, (((1,), (1,)), ((), ())), preferred_element_type=F32)


def contract_first(left, right):
    return lax.dot_general(left, right, (((0,), (0,)), ((), ())), preferred_element_type=F32)


def scale_norm(values, gain):
    return values * lax.rsqrt(jnp.mean(values * values, axis=-1, keepdims=True) + EPSILON) * gain


def down(value, by, fill):
    row = lax.broadcasted_iota(jnp.int32, value.shape, 0)
    return jnp.where(row < by, fill, pltpu.roll(value, by, 0))


def up(value, by, fill):
    length = value.shape[0]
    row = lax.broadcasted_iota(jnp.int32, value.shape, 0)
    return jnp.where(row >= length - by, fill, pltpu.roll(value, length - by, 0))


def scan(shift, decay, driven):
    by = 1
    while by < decay.shape[0]:
        driven = driven + decay * shift(driven, by, 0.0)
        if 2 * by < decay.shape[0]:
            decay = decay * shift(decay, by, 1.0)
        by *= 2
    return driven


def minus_expm1(u):
    series = 1.0 + u * (1 / 7)
    for k in (6, 5, 4, 3, 2):
        series = 1.0 + u * (1 / k) * series
    return jnp.where(u > -0.25, -u * series, 1.0 - jnp.exp(u))


def gelu_parts(v):
    inner = 0.7978845608 * (v + 0.044715 * v * v * v)
    tanh = jnp.tanh(inner)
    value = 0.5 * v * (1.0 + tanh)
    slope = 0.5 * (1.0 + tanh) + 0.5 * v * (1.0 - tanh * tanh) * 0.7978845608 * (
        1.0 + 3 * 0.044715 * v * v
    )
    return value, slope


def mixer_forward(px, py, ga, gi, vec, mixed, states, conv, rate, entry):
    taps = vec[...]
    value = px[...]
    total = taps[4:5] + taps[0:1] * value
    for k in range(1, 4):
        total = total + taps[k : k + 1] * down(value, k, 0.0)
    rounded = total.astype(BF16)
    r = jax.nn.sigmoid(matmul(rounded, ga[0]) + taps[5:6])
    e = jax.nn.sigmoid(matmul(rounded, gi[0]) + taps[6:7])
    log_decay = -8.0 * taps[7:8] * r
    driven = jnp.sqrt(minus_expm1(2.0 * log_decay)) * (e * total)
    s = scan(down, jnp.exp(log_decay), driven)
    mixed[...] = (s * gelu_parts(py[...])[0]).astype(BF16)
    states[...] = s
    conv[...] = total
    rate[...] = r
    entry[...] = e


def mixer_backward(gm, px, py, ga, gi, vec, states, conv, rate, entry, gpx, gga, ggi, gvec):
    taps = vec[...]
    s, total, r, e, grad = states[...], conv[...], rate[...], entry[...], gm[...]
    gated = gelu_parts(py[...])[0]
    log_decay = -8.0 * taps[7:8] * r
    decay = jnp.exp(log_decay)
    root = jnp.sqrt(minus_expm1(2.0 * log_decay))
    grad_driven = scan(up, up(decay, 1, 0.0), grad * gated)
    grad_decay = grad_driven * down(s, 1, 0.0)
    grad_root = grad_driven * (e * total)
    grad_log = grad_decay * decay - grad_root * (decay * decay) / root
    grad_rate = grad_log * (-8.0 * taps[7:8])
    grad_entry = grad_driven * root * total
    ra = (grad_rate * r * (1.0 - r)).astype(BF16)
    ri = (grad_entry * e * (1.0 - e)).astype(BF16)
    rounded = total.astype(BF16)
    gga[...] = contract_first(rounded, ra)
    ggi[...] = contract_first(rounded, ri)
    grad_conv = (
        grad_driven * root * e + contract_last(ra, ga[0]) + contract_last(ri, gi[0])
    )
    value = px[...]
    back = taps[0:1] * grad_conv
    sums = [jnp.sum(grad_conv * value, axis=0, keepdims=True)]
    for k in range(1, 4):
        back = back + taps[k : k + 1] * up(grad_conv, k, 0.0)
        sums.append(jnp.sum(grad_conv * down(value, k, 0.0), axis=0, keepdims=True))
    gpx[...] = back.astype(BF16)
    sums.append(jnp.sum(grad_conv, axis=0, keepdims=True))
    sums.append(jnp.sum(ra.astype(F32), axis=0, keepdims=True))
    sums.append(jnp.sum(ri.astype(F32), axis=0, keepdims=True))
    sums.append(jnp.sum(grad_log * (-8.0 * r), axis=0, keepdims=True))
    gvec[...] = jnp.concatenate(sums, axis=0)


def by_head(kernel, heads, length, block, kinds, outs):
    spec = {
        "r": pl.BlockSpec((length, block), lambda h: (0, h)),
        "g": pl.BlockSpec((1, block, block), lambda h: (h, 0, 0)),
        "v": pl.BlockSpec((8, block), lambda h: (0, h)),
        "w": pl.BlockSpec((block, block), lambda h: (0, h)),
    }
    sizes = {"r": (length, heads * block), "v": (8, heads * block), "w": (block, heads * block)}
    return pl.pallas_call(
        kernel,
        grid=(heads,),
        in_specs=[spec[k] for k in kinds],
        out_specs=[spec[k] for k, _ in outs],
        out_shape=[jax.ShapeDtypeStruct(sizes[k], d) for k, d in outs],
        compiler_params=pltpu.CompilerParams(vmem_limit_bytes=32 * 1024 * 1024),
    )


def scalar(value):
    return jnp.asarray(value, jnp.int32).reshape(1)


def whole(shape):
    return pl.BlockSpec(shape, lambda *_: (0,) * len(shape))


def params(mib):
    return pltpu.CompilerParams(vmem_limit_bytes=mib * 1024 * 1024)


def cut(values, z, nz):
    part, columns = values[0].shape
    units = columns // nz
    n = len(values)

    def kernel(where, *refs):
        for here in range(nz):

            @pl.when(where[0] == here)
            def _():
                for k in range(nz):
                    first = (here + k) % nz * units
                    for w in range(n):
                        refs[n + k][w] = refs[w][:, first : first + units]

    return pl.pallas_call(
        kernel,
        in_specs=[pl.BlockSpec(memory_space=pltpu.SMEM)] + [whole((part, columns))] * n,
        out_specs=[whole((n, part, units))] * nz,
        out_shape=[jax.ShapeDtypeStruct((n, part, units), values[0].dtype)] * nz,
        compiler_params=params(40),
    )(scalar(z), *values)


def line_up(pieces, z):
    nz = len(pieces)
    n, *rest = pieces[0].shape

    def kernel(where, *refs):
        for k in range(nz):
            to = lax.rem(where[0] - k + nz, nz)
            for w in range(n):
                refs[-1][w, to] = refs[k][w]

    return pl.pallas_call(
        kernel,
        in_specs=[pl.BlockSpec(memory_space=pltpu.SMEM)] + [whole((n, *rest))] * nz,
        out_specs=whole((n, nz, *rest)),
        out_shape=jax.ShapeDtypeStruct((n, nz, *rest), pieces[0].dtype),
        compiler_params=params(40),
    )(scalar(z), *pieces)


def norm_rows(here, across, gain, t):
    rows, width = here[0].shape

    def kernel(where, gain, *refs):
        for s in range(2):
            for other in range(2):
                value = refs[2 * s + other][...].astype(F32)
                scale = lax.rsqrt(jnp.mean(value * value, axis=-1, keepdims=True) + EPSILON)
                place = 1 - where[0] if other else where[0]
                first = pl.multiple_of((2 * s + place) * rows, rows)
                refs[4][pl.ds(first, rows), :] = (value * scale * gain[...]).astype(BF16)

    return pl.pallas_call(
        kernel,
        in_specs=[pl.BlockSpec(memory_space=pltpu.SMEM), whole((1, width))]
        + [whole((rows, width))] * 4,
        out_specs=whole((4 * rows, width)),
        out_shape=jax.ShapeDtypeStruct((4 * rows, width), BF16),
        compiler_params=params(32),
    )(scalar(t), gain.reshape(1, width), *here, *across)


def join(pieces, weights, z):
    nz = len(pieces)
    n, part, units = pieces[0].shape
    shape = weights[0].shape

    def kernel(where, *refs):
        for w in range(n):
            out, sums = refs[n + nz + w], refs[2 * n + nz + w]
            for here in range(nz):

                @pl.when(where[0] == here)
                def _():
                    for k in range(nz):
                        first = (here - k) % nz * units
                        out[:, first : first + units] = refs[n + k][w].astype(F32)

            sums[...] = jnp.sum(out[...] * refs[w][...].astype(F32), axis=1, keepdims=True)

    outs = pl.pallas_call(
        kernel,
        in_specs=[pl.BlockSpec(memory_space=pltpu.SMEM)]
        + [whole(shape)] * n
        + [whole((n, part, units))] * nz,
        out_specs=[whole(shape)] * n + [whole((part, 1))] * n,
        out_shape=[jax.ShapeDtypeStruct(shape, F32)] * n
        + [jax.ShapeDtypeStruct((part, 1), F32)] * n,
        compiler_params=params(48),
    )(scalar(z), *weights, *pieces)
    return outs[:n], outs[n:]


def reorder(value, nz, back):
    rows, width = value.shape
    part = width // (4 * nz)

    def kernel(source, out):
        for k in range(4):
            for z in range(nz):
                natural, own = (z * 4 + k) * part, (k * nz + z) * part
                to, of = (natural, own) if back else (own, natural)
                out[:, to : to + part] = source[:, of : of + part]

    return pl.pallas_call(
        kernel,
        in_specs=[whole(value.shape)],
        out_specs=whole(value.shape),
        out_shape=jax.ShapeDtypeStruct(value.shape, value.dtype),
        compiler_params=params(32),
    )(value)


TILE = 256
GATE, UP, DOWN = range(3)


def rows_of(width):
    return pl.BlockSpec((TILE, width), lambda i: (i, 0))


def weight_of(weights, which):
    corners, _, *rest = weights.shape
    return pl.BlockSpec((corners, 1, *rest), lambda i: (0, which, 0, 0, 0))


def flat(ref):
    return ref[...].reshape(-1, ref.shape[-1])


def ffn_down_back(act, weights):
    tokens, width = act.shape
    units = weights.shape[-1]

    def kernel(act, down, out):
        out[...] = matmul(act[...], flat(down))

    return pl.pallas_call(
        kernel,
        grid=(tokens // TILE,),
        in_specs=[rows_of(width), weight_of(weights, DOWN)],
        out_specs=rows_of(units),
        out_shape=jax.ShapeDtypeStruct((tokens, units), F32),
        compiler_params=params(48),
    )(act, weights)


def ffn_middle(act, weights, grad_hidden):
    tokens, width = act.shape
    units = weights.shape[-1]

    def kernel(act, grad, gate, up, hidden, grads):
        value = act[...]
        gate_pre = matmul(value, flat(gate))
        up_pre = matmul(value, flat(up))
        active, slope = gelu_parts(gate_pre)
        hidden[...] = (active * up_pre).astype(BF16)
        grads[0] = (slope * (grad[...] * up_pre)).astype(BF16)
        grads[1] = (grad[...] * active).astype(BF16)

    return pl.pallas_call(
        kernel,
        grid=(tokens // TILE,),
        in_specs=[
            rows_of(width),
            rows_of(units),
            weight_of(weights, GATE),
            weight_of(weights, UP),
        ],
        out_specs=[rows_of(units), pl.BlockSpec((2, TILE, units), lambda i: (0, i, 0))],
        out_shape=[
            jax.ShapeDtypeStruct((tokens, units), BF16),
            jax.ShapeDtypeStruct((2, tokens, units), BF16),
        ],
        compiler_params=params(56),
    )(act, grad_hidden, weights, weights)


def ffn_collect(acts, weights, which, dtype):
    n, tokens, units = acts.shape
    width = weights.shape[0] * weights.shape[2] * weights.shape[3]

    def kernel(acts, *refs):
        total = contract_last(acts[0], flat(refs[0]))
        for p in range(1, n):
            total = total + contract_last(acts[p], flat(refs[p]))
        refs[n][...] = total.astype(dtype)

    return pl.pallas_call(
        kernel,
        grid=(tokens // TILE,),
        in_specs=[pl.BlockSpec((n, TILE, units), lambda i: (0, i, 0))]
        + [weight_of(weights, w) for w in which],
        out_specs=rows_of(width),
        out_shape=jax.ShapeDtypeStruct((tokens, width), dtype),
        compiler_params=params(56),
    )(acts, *[weights] * n)


def weight_grad(acts, grads, lead, tail, dtype, n=None, at=0, into=None):
    tokens, width = acts[0].shape
    m, _, columns = grads[0].shape
    n = n or m
    p = len(acts)
    shape = lead + tail
    block = math.prod(shape)
    at_once = math.lcm(block, 128) // block
    ones = (0,) * len(lead), (0,) * (len(tail) + 1)
    full = (width // block, *lead, n, *tail, columns)

    def kernel(*refs):
        total = contract_first(refs[0][...], refs[p][0])
        for k in range(1, p):
            total = total + contract_first(refs[k][...], refs[p + k][0])
        refs[-1][...] = total.reshape(refs[-1].shape).astype(dtype)

    return pl.pallas_call(
        kernel,
        grid=(m, width // block // at_once),
        in_specs=[pl.BlockSpec((tokens, block * at_once), lambda w, i: (0, i))] * p
        + [pl.BlockSpec((1, tokens, columns), lambda w, i: (w, 0, 0))] * p
        + ([] if into is None else [pl.BlockSpec(memory_space=pl.ANY)]),
        out_specs=pl.BlockSpec(
            (at_once, *lead, 1, *tail, columns), lambda w, i: (i, *ones[0], w + at, *ones[1])
        ),
        out_shape=jax.ShapeDtypeStruct(full, dtype),
        input_output_aliases={} if into is None else {2 * p: 0},
        compiler_params=params(48),
    )(*acts, *grads, *([] if into is None else [into]))


def after(value, *deps):
    return lax.optimization_barrier((value,) + deps)[0]


class Grid:
    def __init__(self, n):
        self.n = n
        self.nz = n // 4
        index = lax.axis_index("dp")
        self.x = index % 2
        self.y = (index // 2) % 2
        self.z = index // 4
        self.t = lax.axis_index("tensor")
        self.corners = [[4 * z + k for k in range(4)] for z in range(self.nz)]
        self.planes = [[4 * z + 2 * y + x for z in range(self.nz) for y in range(2)] for x in range(2)]

    def place(self, axis):
        return {"x": self.x, "y": self.y, "t": self.t}[axis]

    def swap(self, value, axis):
        if axis == "t":
            return lax.ppermute(value, "tensor", [(0, 1), (1, 0)])
        bit = {"x": 1, "y": 2}[axis]
        return lax.ppermute(value, "dp", [(i, i ^ bit) for i in range(self.n)])

    def shift(self, value, by):
        return lax.ppermute(value, "dp", [(i, (i + 4 * by) % self.n) for i in range(self.n)])

    def pair(self, mine, other, axis):
        here = self.place(axis)
        return jnp.where(here == 0, jnp.stack([mine, other]), jnp.stack([other, mine]))

    def pick(self, value, axis, dim, other=False):
        here = self.place(axis)
        return lax.dynamic_index_in_dim(value, 1 - here if other else here, dim, keepdims=False)

    def shifts(self, pieces):
        return [pieces[0]] + [self.shift(p, k) for k, p in enumerate(pieces) if k]

    def trade(self, value, axis):
        return self.pair(
            self.pick(value, axis, 0), self.swap(self.pick(value, axis, 0, True), axis), axis
        )

    def reduce(self, value, axis, dim):
        got = self.swap(self.pick(value, axis, dim, True).astype(BF16), axis)
        return self.pick(value, axis, dim).astype(F32) + got.astype(F32)

    def reduce_z(self, value):
        take = lambda k: lax.dynamic_index_in_dim(value, (self.z + k) % self.nz, 0, keepdims=False)
        total = take(0).astype(F32)
        for k in range(1, self.nz):
            total = total + self.shift(take(k).astype(BF16), k).astype(F32)
        return total


def local(n):
    def run(
        inputs,
        gain_mix,
        gain_mlp,
        branch_x,
        branch_y,
        conv_taps,
        conv_bias,
        gate_a,
        bias_a,
        gate_in,
        bias_in,
        decay_param,
        out_proj,
        ffn_gate,
        ffn_up,
        ffn_down,
        cotangent,
    ):
        grid = Grid(n)
        nz = grid.nz
        rows_each, width = inputs.shape
        part, half = branch_x.shape
        quarter = half // 2
        heads, gate_rows, block = gate_a.shape
        units = ffn_gate.shape[1] // nz
        split = part // 2
        run_len = nz * part
        length = 2 * rows_each
        slim = conv_bias.shape[0]
        here_x = grid.x == 0

        vectors = jnp.concatenate(
            [conv_taps.reshape(-1), conv_bias, bias_a, bias_in, decay_param, gain_mix, gain_mlp]
        )
        pad_rows = -(2 * gate_rows + 1) % 16 + 1
        packed = jnp.concatenate(
            [
                jnp.transpose(gate_a, (1, 0, 2)).reshape(gate_rows, half),
                jnp.transpose(gate_in, (1, 0, 2)).reshape(gate_rows, half),
                jnp.pad(vectors[None], ((0, pad_rows - 1), (0, half - vectors.shape[0]))),
            ]
        )
        early = grid.shifts([packed[None]] * nz)
        small = line_up(early, grid.z)[0]
        small = grid.pair(small, grid.swap(small, "y"), "y")
        small = grid.pair(small, grid.swap(small, "x"), "x")
        small = jnp.transpose(small, (2, 1, 0, 3, 4)).reshape(n, -1, half)
        gates = small[:, : 2 * gate_rows].reshape(n, 2, gate_rows, heads, block)
        gates = jnp.transpose(gates, (1, 3, 0, 2, 4)).reshape(2, heads, n * gate_rows, block)
        full_gate_a, full_gate_in = gates[0], gates[1]
        vecs = small[:, 2 * gate_rows].astype(F32)
        per = jnp.transpose(vecs[:, : 8 * slim].reshape(n, 8, slim), (1, 0, 2)).reshape(8, half)
        decay_row = per[7:8]
        per = jnp.concatenate([per[:7], jax.nn.softplus(decay_row)])
        full_gain_mix = vecs[:, 8 * slim : 8 * slim + part].reshape(width)
        full_gain_mlp = vecs[:, 8 * slim + part : 8 * slim + 2 * part].reshape(width)

        by_x = lambda w: jnp.stack([w[:, :quarter], w[:, quarter:]])
        mine = jnp.concatenate([by_x(branch_x), by_x(branch_y)], axis=-1)
        mine = grid.trade(mine, "x").reshape(2 * part, -1)
        full_in = lax.all_gather(mine, "dp", axis=0, tiled=True, axis_index_groups=grid.planes)
        across = grid.swap(after(inputs, mine), "x")

        normed = norm_rows(
            (inputs, grid.swap(inputs, "t")), (across, grid.swap(across, "t")), full_gain_mix, grid.t
        )

        down_rows = jnp.transpose(ffn_down)
        slices = cut((ffn_gate, ffn_up, down_rows), grid.z, nz)
        slices = grid.shifts(slices)
        out_mine = grid.trade(by_x(jnp.transpose(out_proj)), "x").reshape(1, 2 * part, -1)
        out_line = grid.shifts([after(out_mine, slices[1])] * nz)
        weights = lax.all_gather(
            after(line_up(slices, grid.z)[None], full_in, small),
            "dp",
            axis=0,
            tiled=True,
            axis_index_groups=grid.corners,
        )

        def to_line(value, *deps):
            value = after(reorder(value, nz, False), *deps)
            return grid.shifts([value] * nz)

        rows = inputs.astype(F32)
        cot_line = to_line(cotangent, slices[1])
        pre = matmul(normed, full_in).reshape(2, length, 2 * quarter)

        def whole_half(mine, other):
            return jnp.where(
                here_x, jnp.concatenate([mine, other], 1), jnp.concatenate([other, mine], 1)
            )

        def to_rows(value):
            low, high = value[:, :quarter], value[:, quarter:]
            away = grid.swap(jnp.where(here_x, high, low), "x")
            return jnp.concatenate([jnp.where(here_x, low, high), away])

        got = grid.swap(pre[1].astype(BF16), "x").astype(F32)
        got = after(got, cot_line[1])
        out_here = line_up(after(out_line, got), grid.z)[0]
        full_out = grid.pair(out_here, grid.swap(out_here, "y"), "y")
        full_out = jnp.swapaxes(full_out, 0, 1).reshape(width, -1)
        pre_x = whole_half(pre[0, :, :quarter], got[:, :quarter])
        pre_y = whole_half(pre[0, :, quarter:], got[:, quarter:])
        mixed, states, conv, rate, entry = by_head(
            mixer_forward, heads, length, block, "rrggv", [("r", BF16)] + [("r", F32)] * 4
        )(pre_x, pre_y, full_gate_a, full_gate_in, per)
        mixed = after(to_rows(mixed), cot_line[2])
        branch_out = contract_last(mixed, full_out).reshape(2, 2, rows_each, width)
        branch_out = grid.reduce(branch_out, "t", 1)
        branch_out = branch_out[0] + grid.swap(branch_out[1].astype(BF16), "x").astype(F32)
        resid = after(rows + branch_out, *cot_line)

        normed_two_rows, norm_two_pull = jax.vjp(scale_norm, resid, full_gain_mlp)
        def from_line(acts, which, *deps):
            other = ffn_collect(acts[1], weights, which, BF16)
            other = grid.swap(other, "t")
            value = ffn_collect(acts[0], weights, which, F32) + other.astype(F32)
            value = after(value.reshape(nz, rows_each, width), *deps)
            away = [value[k].astype(BF16) for k in range(1, nz)]
            return away, [value[0]] + [grid.shift(v, -1 - k) for k, v in enumerate(away)]

        def total(got):
            return reorder(sum(g.astype(F32) for g in got), nz, True)

        def both_t(line):
            rows = jnp.concatenate(line)
            return rows, grid.swap(rows, "t")

        upstream = both_t(cot_line)
        grad_hidden = [ffn_down_back(u, weights) for u in upstream]
        normed_two = both_t(to_line(normed_two_rows.astype(BF16)))
        hidden, grad_pre = zip(
            *[ffn_middle(a, weights, g) for a, g in zip(normed_two, grad_hidden)]
        )
        hidden = [h[None] for h in hidden]
        sent, got_result = from_line(hidden, (DOWN,))
        upstream, normed_two = after((upstream, normed_two), *sent)
        grad_ffn = weight_grad(normed_two, grad_pre, (), (nz, part), BF16, 3)
        grad_ffn = weight_grad(upstream, hidden, (), (nz, part), BF16, 3, 2, grad_ffn)
        grad_pre = after(grad_pre, grad_ffn, got_result[1])
        sent, got_two = from_line(grad_pre, (GATE, UP))

        def ffn_send(value, *deps):
            value = after(value, *deps)
            take = lambda k: lax.dynamic_index_in_dim(value, (grid.z + k) % nz, 1, keepdims=False)
            return grid.shifts([take(k) for k in range(nz)])

        grad_ffn = lax.psum_scatter(
            grad_ffn, "dp", scatter_dimension=0, tiled=True, axis_index_groups=grid.corners
        )
        grad_normed_two = total(after(got_two, *got_result[1:]))
        grad_ffn = ffn_send(grad_ffn[0], got_two[1])

        grad_resid_norm, _ = norm_two_pull(grad_normed_two)
        grad_resid = cotangent.astype(F32) + grad_resid_norm
        back = grad_resid.astype(BF16)
        back = jnp.stack([back, grid.swap(back, "x")])
        back = jnp.swapaxes(grid.pair(back, grid.swap(back, "t"), "t"), 0, 1)
        back = back.reshape(2 * length, width)
        grad_mixed = matmul(back, full_out).reshape(2, length, quarter)
        grad_mixed = whole_half(
            grad_mixed[0], grid.swap(grad_mixed[1].astype(BF16), "x").astype(F32)
        )
        grad_mixed = after(grad_mixed, grad_ffn[1])
        grad_pre_y = gelu_parts(pre_y)[1] * (grad_mixed * states)
        grad_y_rows = to_rows(grad_pre_y.astype(BF16))

        def mixer_reduce(grad):
            grad = grad.reshape(nz, 2, 2, part, -1)
            away = grid.swap(grid.pick(grad, "y", 1, True).astype(BF16), "y")
            return grid.pick(grad, "y", 1), away

        def mixer_send(value, *deps):
            here, away = after(value, *deps)
            value = here + away.astype(F32)
            take = lambda k: lax.dynamic_index_in_dim(value, (grid.z + k) % nz, 0, keepdims=False)
            got = [take(0)] + [grid.shift(take(k).astype(BF16), k) for k in range(1, nz)]
            return got

        def mixer_finish(got):
            return grid.trade(got, "x")

        grad_oy = weight_grad([back], [mixed[None]], (2,), (2, part), BF16, 2)
        grad_oy = weight_grad([normed], [grad_y_rows[None]], (2,), (2, part), BF16, 2, 1, grad_oy)
        grad_oy = lax.psum_scatter(
            grad_oy.reshape(2 * nz, 2, 2, part, quarter),
            "dp",
            scatter_dimension=0,
            tiled=True,
            axis_index_groups=grid.planes,
        )[0]
        grad_pre_x, grad_gate_a, grad_gate_in, grad_vec = by_head(
            mixer_backward,
            heads,
            length,
            block,
            "rrrggvrrrr",
            [("r", BF16), ("w", F32), ("w", F32), ("v", F32)],
        )(grad_mixed, pre_x, pre_y, full_gate_a, full_gate_in, per, states, conv, rate, entry)
        grad_vec = jnp.concatenate([grad_vec[:7], grad_vec[7:] * jax.nn.sigmoid(decay_row)])
        grad_x_rows = to_rows(grad_pre_x)
        grad_x = mixer_reduce(weight_grad([normed], [grad_x_rows[None]], (), (4, part), F32))
        grad_x = mixer_send(grad_x, *grad_ffn[1:])
        grad_in_rows = jnp.concatenate([grad_x_rows, grad_y_rows], axis=1)

        result = (resid + total(got_result)).astype(BF16)
        (grad_gate, grad_up, grad_down), sums = join(
            after(grad_ffn, *grad_x[1:]), (ffn_gate, ffn_up, down_rows), grid.z
        )
        grad_down = jnp.transpose(grad_down)
        grad_oy = after(grad_oy, *grad_x[1:])
        grad_out = mixer_finish(grad_oy[0])
        grad_out = jnp.transpose(grad_out, (0, 2, 1)).reshape(half, part).astype(F32)
        beside = lambda g: jnp.concatenate([g[0], g[1]], axis=1).astype(F32)
        grad_branch_y = beside(mixer_finish(grad_oy[1]))
        grad_x = sum(g.astype(F32) for g in grad_x).astype(BF16)
        grad_branch_x = beside(mixer_finish(grad_x))

        vec = jnp.transpose(grad_vec.reshape(8, n, slim), (1, 0, 2)).reshape(n, 1, 8 * slim)
        grad_small = jnp.concatenate(
            [
                grad_gate_a.reshape(n, gate_rows, half),
                grad_gate_in.reshape(n, gate_rows, half),
                jnp.pad(vec, ((0, 0), (0, pad_rows - 1), (0, half - 8 * slim))),
            ],
            axis=1,
        ).reshape(nz, 2, 2, 2 * gate_rows + pad_rows, half)
        grad_small = after(grad_small, grad_x_rows)
        grad_small = grid.reduce_z(grid.reduce(grid.reduce(grad_small, "x", 2), "y", 1))
        unpack = lambda g: jnp.transpose(g.reshape(gate_rows, heads, block), (1, 0, 2))
        vec = grad_small[2 * gate_rows, : 8 * slim].reshape(8, slim)

        grad_normed = contract_last(grad_in_rows, full_in).reshape(2, 2, rows_each, width)
        grad_normed = grid.reduce(grad_normed, "t", 1)
        grad_normed = grad_normed[0] + grid.swap(grad_normed[1].astype(BF16), "x").astype(F32)
        _, norm_pull = jax.vjp(scale_norm, rows, full_gain_mix)
        grad_rows, _ = norm_pull(grad_normed)
        grad_inputs = grad_resid + grad_rows

        gains = jnp.stack(
            [
                jnp.sum(
                    branch_x.astype(F32) * grad_branch_x + branch_y.astype(F32) * grad_branch_y,
                    axis=1,
                )
                / gain_mix.astype(F32),
                (sums[0] + sums[1])[:, 0]
                / gain_mlp.astype(F32),
            ]
        )
        gains = gains + grid.swap(gains, "t")
        gains = lax.dynamic_index_in_dim(gains.reshape(2, 2, split), grid.t, 1, keepdims=False)
        return (
            result,
            grad_inputs,
            gains[0],
            gains[1],
            grad_branch_x,
            grad_branch_y,
            vec[:4],
            vec[4],
            unpack(grad_small[:gate_rows]),
            vec[5],
            unpack(grad_small[gate_rows : 2 * gate_rows]),
            vec[6],
            vec[7],
            grad_out,
            grad_gate,
            grad_up,
            grad_down,
        )

    return run


def solution(mesh):
    in_specs = (
        P(("dp", "tensor"), None),
        P("dp"),
        P("dp"),
        P("dp", "tensor"),
        P("dp", "tensor"),
        P(None, ("tensor", "dp")),
        P(("tensor", "dp")),
        P("tensor", "dp", None),
        P(("tensor", "dp")),
        P("tensor", "dp", None),
        P(("tensor", "dp")),
        P(("tensor", "dp")),
        P("tensor", "dp"),
        P("dp", "tensor"),
        P("dp", "tensor"),
        P("tensor", "dp"),
        P(("dp", "tensor"), None),
    )
    out_specs = (
        P(("dp", "tensor"), None),
        P(("dp", "tensor"), None),
        P(("dp", "tensor")),
        P(("dp", "tensor")),
        P("dp", "tensor"),
        P("dp", "tensor"),
        P(None, ("tensor", "dp")),
        P(("tensor", "dp")),
        P("tensor", "dp", None),
        P(("tensor", "dp")),
        P("tensor", "dp", None),
        P(("tensor", "dp")),
        P(("tensor", "dp")),
        P("tensor", "dp"),
        P("dp", "tensor"),
        P("dp", "tensor"),
        P("tensor", "dp"),
    )
    return jax.shard_map(
        local(mesh.shape["dp"]),
        mesh=mesh,
        in_specs=in_specs,
        out_specs=out_specs,
        check_vma=False,
    )
```

time: 1600 us -> 999 us (0.62)
  local copies, waits for them, and re-layouts: 437 us -> 90.2 us
  other arithmetic: 206 us -> 44.7 us
  Pallas kernels: 0 us -> 139 us
  matrix products: 124 us -> 16.9 us
  waiting for transfers between devices: 646 us -> 565 us
  starting transfers between devices: 162 us -> 115 us
    slice x108 -> x13, local copies, waits for them, and re-layouts: 171 us -> 3.29 us  [the longest x1 1.23 us: run(): gates = small[:, :2 * gate_rows].reshape(n, 2, gate_rows, heads, block)]
    pallas_call x0 -> x25, Pallas kernels: none -> 139 us  [the longest x5 37.9 us: weight_grad(): pl.pallas_call(kernel, grid=(m, width // block // at_once), in_specs=[pl....]
    select_n x30 -> x6, other arithmetic: 67.3 us -> 5.67 us  [pair(): jnp.where(here == 0, jnp.stack([mine, other]), jnp.stack([other, mine]))]
    ppermute x45 -> x20, waiting for transfers between devices: 243 us -> 184 us  [swap(): return lax.ppermute(value, 'dp', [(i, i ^ bit) for i in range(self.n)])]
    dot_general x11 -> x0, matrix products: 50.2 us -> none  [the longest x5 37.9 us: contract_first(): lax.dot_general(left, right, (((0,), (0,)), ((), ())), preferred_element_...]
    ppermute x48 -> x30, waiting for transfers between devices: 403 us -> 362 us  [shift(): lax.ppermute(value, 'dp', [(i, (i + 4 * by) % self.n) for i in range(self...]
    ppermute x48 -> x30, starting transfers between devices: 121 us -> 80.5 us  [shift(): lax.ppermute(value, 'dp', [(i, (i + 4 * by) % self.n) for i in range(self...]
    dynamic_update_slice x38 -> x0, local copies, waits for them, and re-layouts: 36 us -> none  [line(): out = lax.dynamic_update_index_in_dim(out, piece, (self.z - k) % self.nz, 0)]
  transfers between devices with their start and end apart: 102 -> 64, of which waited for: 45 -> 35; matrix products, arithmetic and copies ran while one was open for 41% -> 9% of each run, Pallas kernels for 0% -> 9%
where the time goes in v2:
time: 999 us; the launch traced here: 987 us
  waiting for transfers between devices  565 us (57%)
  Pallas kernels  139 us (14%)
  starting transfers between devices  115 us (12%)
  local copies, waits for them, and re-layouts  90.2 us (9%)
  other arithmetic  44.7 us (4%)
  matrix products  16.9 us (2%)
  between operations  15.7 us (2%)
    ppermute x30, waiting for transfers between devices, shift(): lax.ppermute(value, 'dp', [(i, (i + 4 * by) % self.n) for i in range(self...  362 us
    ppermute x20, waiting for transfers between devices, swap(): return lax.ppermute(value, 'dp', [(i, i ^ bit) for i in range(self.n)])  184 us
    ppermute x30, starting transfers between devices, shift(): lax.ppermute(value, 'dp', [(i, (i + 4 * by) % self.n) for i in range(self...  80.5 us
    unnamed x202, local copies, waits for them, and re-layouts  54.9 us
    pallas_call x5, Pallas kernels, weight_grad(): pl.pallas_call(kernel, grid=(m, width // block // at_once), in_specs=[pl....  37.9 us
    pallas_call x4, Pallas kernels, ffn_collect(): pl.pallas_call(kernel, grid=(tokens // TILE,), in_specs=[pl.BlockSpec((n,...  37.7 us
    ppermute x20, starting transfers between devices, swap(): return lax.ppermute(value, 'dp', [(i, i ^ bit) for i in range(self.n)])  34 us
    pallas_call x2, Pallas kernels, ffn_middle(): pl.pallas_call(kernel, grid=(tokens // TILE,), in_specs=[rows_of(width),...  23.8 us
  transfers between devices with their start and end apart: 64, of which 35 were waited for; matrix products, arithmetic and copies ran while one was open for 9% of the time, Pallas kernels for 9%

profile of v2, /device:TPU:0, one launch (start us, length us, event | category | flops | bytes accessed | tf_op | source)
XLA Modules:
  0.0 987.1 jit_solution(18357276864529118248)
XLA Ops:
  9.7 3.0 collective-permute-start.6
  12.7 9.5 collective-permute-done.6
  23.5 3.9 collective-permute-start.2
  31.2 6.9 collective-permute-done.1.refs_2_
  40.8 14.3 %collective-permute-done.3 = bf16[4,48,1280]{2,1,0:T(8,128)(2,1)} collective-permute-done((bf16[4,48,1280]{2,1,0:T(8,128)(2,1)S(1)}, bf16[4,48,1280]{2,1,0:T(8,128)(2,1)}, u32[]{:S(2)}, u32[]{:S(2)}) %collective-permute-start.3) | collective-permute-done | bytes 491552 | tf_op jit(solution)/shard_map/ppermute | solution.py:410
  66.7 22.4 %collective-permute-done.10.refs_1_ = bf16[3,160,960]{2,1,0:T(8,128)(2,1)S(1)} collective-permute-done((bf16[3,160,960]{2,1,0:T(8,128)(2,1)S(1)}, bf16[3,160,960]{2,1,0:T(8,128)(2,1)S(1)}, u32[]{:S(2)}, u32[]{:S(2)}) %collective-permute-start.10) | collective-permute-done | bytes 921632 | tf_op jit(solution)/shard_map/ppermute | solution.py:413
  89.1 77.2 %collective-permute-done.25.refs_2_ = bf16[3,160,960]{2,1,0:T(8,128)(2,1)S(1)} collective-permute-done((bf16[3,160,960]{2,1,0:T(8,128)(2,1)S(1)}, bf16[3,160,960]{2,1,0:T(8,128)(2,1)S(1)}, u32[]{:S(2)}, u32[]{:S(2)}) %collective-permute-start.25) | collective-permute-done | bytes 921632 | tf_op jit(solution)/shard_map/ppermute | solution.py:413
  170.0 14.6 %all-gather.3.cloned.1.call-done = bf16[2560,1280]{1,0:T(8,128)(2,1)} async-done(((bf16[320,1280]{1,0:T(8,128)(2,1)}), bf16[2560,1280]{1,0:T(8,128)(2,1)}) %all-gather.3.cloned.1.call-update) | async-done | bytes 6553616 | tf_op jit(solution)/shard_map/all_gather | solution.py:505
  189.8 17.1 %collective-permute-done.14 = bf16[160,640]{1,0:T(8,128)(2,1)} collective-permute-done((bf16[160,640]{1,0:T(8,128)(2,1)}, bf16[160,640]{1,0:T(8,128)(2,1)}, u32[]{:S(2)}, u32[]{:S(2)}) %collective-permute-start.14) | collective-permute-done | bytes 204832 | tf_op jit(solution)/shard_map/ppermute | solution.py:410
  208.8 26.6 %collective-permute-start.17 = (bf16[1,320,640]{2,1,0:T(8,128)(2,1)}, bf16[1,320,640]{2,1,0:T(8,128)(2,1)}, u32[]{:S(2)}, u32[]{:S(2)}) collective-permute-start(bf16[1,320,640]{2,1,0:T(8,128)(2,1)} %bitcast.33.refs_0_), channel_id=1, source_target_pairs={{0,24},{2,26},{4,28},{6,30},{8,0},{10,2},{12,4},{14,6},{16,8},{18,... | collective-permute-start | bytes 1228808 | tf_op jit(solution)/shard_map/ppermute | solution.py:413
  235.4 4.4 collective-permute-start.16
  242.3 4.0 reshape.380
  253.4 6.5 fusion.66
  262.8 14.9 %collective-permute-done.9 = bf16[256,1280]{1,0:T(8,128)(2,1)S(1)} collective-permute-done((bf16[256,1280]{1,0:T(8,128)(2,1)S(1)}, bf16[256,1280]{1,0:T(8,128)(2,1)S(1)}, u32[]{:S(2)}, u32[]{:S(2)}) %collective-permute-start.9) | collective-permute-done | bytes 655392 | tf_op jit(solution)/shard_map/ppermute | solution.py:410
  277.6 5.8 collective-permute-start.13
  288.0 3.8 collective-permute-start.18
  293.0 6.0 shard_map.300
  306.9 14.0 %collective-permute-done.12 = bf16[256,640]{1,0:T(8,128)(2,1)} collective-permute-done((bf16[256,640]{1,0:T(8,128)(2,1)}, bf16[256,640]{1,0:T(8,128)(2,1)}, u32[]{:S(2)}, u32[]{:S(2)}) %collective-permute-start.12) | collective-permute-done | bytes 327712 | tf_op jit(solution)/shard_map/ppermute | solution.py:410
  322.1 40.1 %collective-permute-done.18 = bf16[4,320,640]{2,1,0:T(8,128)(2,1)} collective-permute-done((bf16[4,320,640]{2,1,0:T(8,128)(2,1)}, bf16[4,320,640]{2,1,0:T(8,128)(2,1)}, u32[]{:S(2)}, u32[]{:S(2)}) %collective-permute-start.18) | collective-permute-done | bytes 1638432 | tf_op jit(solution)/shard_map/ppermute | solution.py:410
  362.2 3.4 fusion
  385.7 11.3 %collective-permute-done.20 = bf16[128,2560]{1,0:T(8,128)(2,1)} collective-permute-done((bf16[128,2560]{1,0:T(8,128)(2,1)}, bf16[128,2560]{1,0:T(8,128)(2,1)}, u32[]{:S(2)}, u32[]{:S(2)}) %collective-permute-start.20) | collective-permute-done | bytes 655392 | tf_op jit(solution)/shard_map/ppermute | solution.py:410
  408.1 10.2 %collective-permute-done.24 = bf16[128,2560]{1,0:T(8,128)(2,1)S(1)} collective-permute-done((bf16[128,2560]{1,0:T(8,128)(2,1)S(1)}, bf16[128,2560]{1,0:T(8,128)(2,1)S(1)}, u32[]{:S(2)}, u32[]{:S(2)}) %collective-permute-start.24) | collective-permute-done | bytes 655392 | tf_op jit(solution)/shard_map/ppermute | solution.py:413
  418.3 40.4 %collective-permute-done.23 = bf16[128,2560]{1,0:T(8,128)(2,1)S(1)} collective-permute-done((bf16[128,2560]{1,0:T(8,128)(2,1)S(1)}, bf16[128,2560]{1,0:T(8,128)(2,1)S(1)}, u32[]{:S(2)}, u32[]{:S(2)}) %collective-permute-start.23) | collective-permute-done | bytes 655392 | tf_op jit(solution)/shard_map/ppermute | solution.py:413
  463.6 5.5 shard_map.307.grad
  470.4 11.9 %shard_map.308 = (bf16[512,960]{1,0:T(8,128)(2,1)}, bf16[2,512,960]{2,1,0:T(8,128)(2,1)}) custom-call(bf16[512,2560]{1,0:T(8,128)(2,1)} %collective-permute-done.27.act.refs_1_, f32[512,960]{1,0:T(8,128)} %copy-done.17, bf16[4,3,4,160,960]{4,3,2,1,0:T(8,128)(2,1)} %all-gather.5.cloned.1.call-done.down.gate.up.refs_0_.refs_1_, ...), custom_call_target="tpu_custom_call" | custom-call | tf_op jit(solution)/shard_map/pallas_call | solution.py:316
  482.3 6.9 shard_map.309
  489.7 6.0 shard_map.304.grad
  497.0 11.9 %shard_map.305 = (bf16[512,960]{1,0:T(8,128)(2,1)}, bf16[2,512,960]{2,1,0:T(8,128)(2,1)}) custom-call(bf16[512,2560]{1,0:T(8,128)(2,1)} %pad_maximum_fusion.1.act.refs_0_, f32[512,960]{1,0:T(8,128)} %copy-done.18, bf16[4,3,4,160,960]{4,3,2,1,0:T(8,128)(2,1)} %all-gather.5.cloned.1.call-done.down.gate.up.refs_0_.refs_1_, ...), custom_call_target="tpu_custom_call" | custom-call | tf_op jit(solution)/shard_map/pallas_call | solution.py:316
  508.9 7.3 shard_map.306
  516.2 3.2 convert_add_fusion.1
  524.2 15.9 %shard_map.311.refs_4_ = bf16[4,3,4,160,960]{4,3,2,1,0:T(8,128)(2,1)} custom-call(bf16[512,2560]{1,0:T(8,128)(2,1)} %pad_maximum_fusion.1.act.refs_0_, bf16[512,2560]{1,0:T(8,128)(2,1)} %collective-permute-done.27.act.refs_1_, bf16[2,512,960]{2,1,0:T(8,128)(2,1)S(1)} %copy-done.15, bf16[2,512,960]{2,1,0:T(8,128)(2,1)S(1)} %copy-done.16), custom_call_target="tpu_custom_call" | custom-call | tf_op jit(solution)/shard_map/pallas_call | solution.py:372
  540.1 8.9 shard_map.312
  549.1 16.7 %collective-permute-done.30 = bf16[128,2560]{1,0:T(8,128)(2,1)} collective-permute-done((bf16[128,2560]{1,0:T(8,128)(2,1)S(1)}, bf16[128,2560]{1,0:T(8,128)(2,1)}, u32[]{:S(2)}, u32[]{:S(2)}) %collective-permute-start.30) | collective-permute-done | bytes 655392 | tf_op jit(solution)/shard_map/ppermute | solution.py:413
  565.8 11.4 %shard_map.314 = bf16[512,2560]{1,0:T(8,128)(2,1)} custom-call(bf16[2,512,960]{2,1,0:T(8,128)(2,1)} %get-tuple-element.95.refs_3_.acts, bf16[4,3,4,160,960]{4,3,2,1,0:T(8,128)(2,1)} %all-gather.5.cloned.1.call-done.down.gate.up.refs_0_.refs_1_, bf16[4,3,4,160,960]{4,3,2,1,0:T(8,128)(2,1)} %all-gather.5.cloned.1.call-done.down.gate.up.refs_0_.refs_1_), custom_call_target="tpu_custom_call" | custom-call | tf_op jit(solution)/shard_map/pallas_call | solution.py:344
  580.3 12.2 %shard_map.313 = f32[512,2560]{1,0:T(8,128)} custom-call(bf16[2,512,960]{2,1,0:T(8,128)(2,1)} %get-tuple-element.94.refs_2_.acts, bf16[4,3,4,160,960]{4,3,2,1,0:T(8,128)(2,1)} %all-gather.5.cloned.1.call-done.down.gate.up.refs_0_.refs_1_, bf16[4,3,4,160,960]{4,3,2,1,0:T(8,128)(2,1)} %all-gather.5.cloned.1.call-done.down.gate.up.refs_0_.refs_1_), custom_call_target="tpu_custom_call" | custom-call | tf_op jit(solution)/shard_map/pallas_call | solution.py:344
  592.4 3.3 convert_add_fusion
  601.1 51.5 %collective-permute-done.31 = bf16[128,2560]{1,0:T(8,128)(2,1)S(1)} collective-permute-done((bf16[128,2560]{1,0:T(8,128)(2,1)}, bf16[128,2560]{1,0:T(8,128)(2,1)S(1)}, u32[]{:S(2)}, u32[]{:S(2)}) %collective-permute-start.31) | collective-permute-done | bytes 655392 | tf_op jit(solution)/shard_map/ppermute | solution.py:413
  652.7 14.0 %collective-permute-done.35 = bf16[128,2560]{1,0:T(8,128)(2,1)S(1)} collective-permute-done((bf16[128,2560]{1,0:T(8,128)(2,1)S(1)}, bf16[128,2560]{1,0:T(8,128)(2,1)S(1)}, u32[]{:S(2)}, u32[]{:S(2)}) %collective-permute-start.35) | collective-permute-done | bytes 655392 | tf_op jit(solution)/shard_map/ppermute | solution.py:413
  671.8 29.9 %collective-permute-done.37 = bf16[128,2560]{1,0:T(8,128)(2,1)S(1)} collective-permute-done((bf16[128,2560]{1,0:T(8,128)(2,1)S(1)}, bf16[128,2560]{1,0:T(8,128)(2,1)S(1)}, u32[]{:S(2)}, u32[]{:S(2)}) %collective-permute-start.37) | collective-permute-done | bytes 655392 | tf_op jit(solution)/shard_map/ppermute | solution.py:410
  703.4 3.4 collective-permute-done.38
  711.4 3.9 dynamic-slice_bitcast_fusion.2
  715.3 8.3 collective-permute-start.40
  726.6 8.9 collective-permute-done.39
  735.6 11.9 %collective-permute-done.40.refs_4_ = bf16[3,160,960]{2,1,0:T(8,128)(2,1)S(1)} collective-permute-done((bf16[3,160,960]{2,1,0:T(8,128)(2,1)S(1)}, bf16[3,160,960]{2,1,0:T(8,128)(2,1)S(1)}, u32[]{:S(2)}, u32[]{:S(2)}) %collective-permute-start.40) | collective-permute-done | bytes 921632 | tf_op jit(solution)/shard_map/ppermute | solution.py:413
  749.7 4.2 shard_map.318.refs_2_
  753.9 4.0 collective-permute-done.42
  757.9 4.2 shard_map.319
  774.6 8.4 shard_map.316
  795.2 3.0 collective-permute-done.41
  798.2 6.0 fusion.23
  804.2 12.7 %collective-permute-done.54 = bf16[4,2,48,1280]{3,2,1,0:T(8,128)(2,1)S(1)} collective-permute-done((bf16[4,2,48,1280]{3,2,1,0:T(8,128)(2,1)S(1)}, bf16[4,2,48,1280]{3,2,1,0:T(8,128)(2,1)S(1)}, u32[]{:S(2)}, u32[]{:S(2)}) %collective-permute-start.54) | collective-permute-done | bytes 983072 | tf_op jit(solution)/shard_map/ppermute | solution.py:410
  819.0 4.7 shard_map.317
  823.7 3.9 dynamic-slice_bitcast_fusion
  828.3 4.0 collective-permute-start.58
  832.4 3.3 fusion.3
  835.7 9.5 collective-permute-done.56
  845.1 3.5 collective-permute-done.58
  850.1 26.4 %collective-permute-done.57 = bf16[48,1280]{1,0:T(8,128)(2,1)S(1)} collective-permute-done((bf16[48,1280]{1,0:T(8,128)(2,1)S(1)}, bf16[48,1280]{1,0:T(8,128)(2,1)S(1)}, u32[]{:S(2)}, u32[]{:S(2)}) %collective-permute-start.57) | collective-permute-done | bytes 122912 | tf_op jit(solution)/shard_map/ppermute | solution.py:413
  883.4 13.6 %collective-permute-done.46.refs_5_ = bf16[3,160,960]{2,1,0:T(8,128)(2,1)S(1)} collective-permute-done((bf16[3,160,960]{2,1,0:T(8,128)(2,1)}, bf16[3,160,960]{2,1,0:T(8,128)(2,1)S(1)}, u32[]{:S(2)}, u32[]{:S(2)}) %collective-permute-start.46) | collective-permute-done | bytes 921632 | tf_op jit(solution)/shard_map/ppermute | solution.py:413
  897.0 3.1 convert_add_fusion.2
  906.9 10.4 %collective-permute-done.50 = bf16[2,160,640]{2,1,0:T(8,128)(2,1)S(1)} collective-permute-done((bf16[2,160,640]{2,1,0:T(8,128)(2,1)S(1)}, bf16[2,160,640]{2,1,0:T(8,128)(2,1)S(1)}, u32[]{:S(2)}, u32[]{:S(2)}) %collective-permute-start.50) | collective-permute-done | bytes 409632 | tf_op jit(solution)/shard_map/ppermute | solution.py:413
  917.4 43.0 %collective-permute-done.49 = bf16[2,160,640]{2,1,0:T(8,128)(2,1)S(1)} collective-permute-done((bf16[2,160,640]{2,1,0:T(8,128)(2,1)S(1)}, bf16[2,160,640]{2,1,0:T(8,128)(2,1)S(1)}, u32[]{:S(2)}, u32[]{:S(2)}) %collective-permute-start.49) | collective-permute-done | bytes 409632 | tf_op jit(solution)/shard_map/ppermute | solution.py:413
  962.4 6.5 shard_map.320
  972.7 3.5 collective-permute-done.52
  (426 shorter events, 180.1 us)
Async XLA Ops:
  7.2 177.5 %all-gather.3.cloned.1.call-start = ((), (), s32[]{:S(2)}) async-start(), calls=%async_computation.2 | async-start | bytes 7372800 | tf_op jit(solution)/shard_map/all_gather | solution.py:505
  9.7 12.5 %collective-permute-start.6 = (bf16[160,1280]{1,0:T(8,128)(2,1)S(1)}, bf16[160,1280]{1,0:T(8,128)(2,1)S(1)}, u32[]{:S(2)}, u32[]{:S(2)}) collective-permute-start(bf16[160,1280]{1,0:T(8,128)(2,1)S(1)} %get-tuple-element.191), channel_id=1, source_target_pairs={{0,2},{2,0},{4,6},{6,4},{8,10},{10,8},{12,14},{14,12},{16,18},{18,... | collective-permute-start | bytes 1228808 | tf_op jit(solution)/shard_map/ppermute | solution.py:410
  23.2 438.6 %all-gather.5.cloned.1.call-start = ((), (), s32[]{:S(2)}) async-start(), calls=%async_computation.3 | async-start | bytes 19660800 | tf_op jit(solution)/shard_map/all_gather | solution.py:517
  23.5 7.7 collective-permute-start.2
  27.4 10.7 %collective-permute-start.1 = (bf16[1,48,1280]{2,1,0:T(8,128)(2,1)S(1)}, bf16[1,48,1280]{2,1,0:T(8,128)(2,1)S(1)}, u32[]{:S(2)}, u32[]{:S(2)}) collective-permute-start(bf16[1,48,1280]{2,1,0:T(8,128)(2,1)S(1)} %fusion.48.refs_0_), channel_id=1, source_target_pairs={{0,16},{2,18},{4,20},{6,22},{8,24},{10,26},{12,28},{14,30},{16,0},... | collective-permute-start | bytes 368648 | tf_op jit(solution)/shard_map/ppermute | solution.py:413
  27.4 10.7 %collective-permute-start = (bf16[1,48,1280]{2,1,0:T(8,128)(2,1)S(1)}, bf16[1,48,1280]{2,1,0:T(8,128)(2,1)S(1)}, u32[]{:S(2)}, u32[]{:S(2)}) collective-permute-start(bf16[1,48,1280]{2,1,0:T(8,128)(2,1)S(1)} %fusion.48.refs_0_), channel_id=1, source_target_pairs={{0,8},{2,10},{4,12},{6,14},{8,16},{10,18},{12,20},{14,22},{16,24},... | collective-permute-start | bytes 368648 | tf_op jit(solution)/shard_map/ppermute | solution.py:413
  38.2 17.0 %collective-permute-start.3 = (bf16[4,48,1280]{2,1,0:T(8,128)(2,1)S(1)}, bf16[4,48,1280]{2,1,0:T(8,128)(2,1)}, u32[]{:S(2)}, u32[]{:S(2)}) collective-permute-start(bf16[4,48,1280]{2,1,0:T(8,128)(2,1)S(1)} %bitcast.260), channel_id=1, source_target_pairs={{0,4},{2,6},{4,0},{6,2},{8,12},{10,14},{12,8},{14,10},{16,20},{18,... | collective-permute-start | bytes 1474568 | tf_op jit(solution)/shard_map/ppermute | solution.py:410
  56.5 110.1 %collective-permute-start.4 = (bf16[2,4,48,1280]{3,2,1,0:T(8,128)(2,1)S(1)}, bf16[2,4,48,1280]{3,2,1,0:T(8,128)(2,1)S(1)}, u32[]{:S(2)}, u32[]{:S(2)}) collective-permute-start(bf16[2,4,48,1280]{3,2,1,0:T(8,128)(2,1)S(1)} %maximum_select_fusion.7), channel_id=1, source_target_pairs={{0,2},{2,0},{4,6},{6,4},{8,10},{10,8},{12,14},{14,12},{16,18},{18,... | collective-permute-start | bytes 2949128 | tf_op jit(solution)/shard_map/ppermute | solution.py:410
  60.0 29.1 %collective-permute-start.10 = (bf16[3,160,960]{2,1,0:T(8,128)(2,1)S(1)}, bf16[3,160,960]{2,1,0:T(8,128)(2,1)S(1)}, u32[]{:S(2)}, u32[]{:S(2)}) collective-permute-start(bf16[3,160,960]{2,1,0:T(8,128)(2,1)S(1)} %get-tuple-element.71), channel_id=1, source_target_pairs={{0,8},{2,10},{4,12},{6,14},{8,16},{10,18},{12,20},{14,22},{16,24},... | collective-permute-start | bytes 2764808 | tf_op jit(solution)/shard_map/ppermute | solution.py:413
  61.5 104.8 %collective-permute-start.25 = (bf16[3,160,960]{2,1,0:T(8,128)(2,1)S(1)}, bf16[3,160,960]{2,1,0:T(8,128)(2,1)S(1)}, u32[]{:S(2)}, u32[]{:S(2)}) collective-permute-start(bf16[3,160,960]{2,1,0:T(8,128)(2,1)S(1)} %get-tuple-element.83), channel_id=1, source_target_pairs={{0,16},{2,18},{4,20},{6,22},{8,24},{10,26},{12,28},{14,30},{16,0},... | collective-permute-start | bytes 2764808 | tf_op jit(solution)/shard_map/ppermute | solution.py:413
  63.8 102.6 %collective-permute-start.26 = (bf16[3,160,960]{2,1,0:T(8,128)(2,1)S(1)}, bf16[3,160,960]{2,1,0:T(8,128)(2,1)S(1)}, u32[]{:S(2)}, u32[]{:S(2)}) collective-permute-start(bf16[3,160,960]{2,1,0:T(8,128)(2,1)S(1)} %get-tuple-element.84), channel_id=1, source_target_pairs={{0,24},{2,26},{4,28},{6,30},{8,0},{10,2},{12,4},{14,6},{16,8},{18,... | collective-permute-start | bytes 2764808 | tf_op jit(solution)/shard_map/ppermute | solution.py:413
  184.7 526.7 %reduce-scatter.7.cloned.1.call-start = ((), (), s32[]{:S(2)}) async-start(), calls=%async_computation.5 | async-start | bytes 19660800
  185.7 54.0 %collective-permute-start.7 = (bf16[128,2560]{1,0:T(8,128)(2,1)S(1)}, bf16[128,2560]{1,0:T(8,128)(2,1)S(1)}, u32[]{:S(2)}, u32[]{:S(2)}) collective-permute-start(bf16[128,2560]{1,0:T(8,128)(2,1)S(1)} %copy-done.12), channel_id=1, source_target_pairs={{0,2},{2,0},{4,6},{6,4},{8,10},{10,8},{12,14},{14,12},{16,18},{18,... | collective-permute-start | bytes 1966088 | tf_op jit(solution)/shard_map/ppermute | solution.py:410
  188.1 18.8 %collective-permute-start.14 = (bf16[160,640]{1,0:T(8,128)(2,1)}, bf16[160,640]{1,0:T(8,128)(2,1)}, u32[]{:S(2)}, u32[]{:S(2)}) collective-permute-start(bf16[160,640]{1,0:T(8,128)(2,1)} %get-tuple-element.209), channel_id=1, source_target_pairs={{0,2},{2,0},{4,6},{6,4},{8,10},{10,8},{12,14},{14,12},{16,18},{18,... | collective-permute-start | bytes 614408 | tf_op jit(solution)/shard_map/ppermute | solution.py:410
  188.7 57.6 %collective-permute-start.5 = (bf16[128,2560]{1,0:T(8,128)(2,1)S(1)}, bf16[128,2560]{1,0:T(8,128)(2,1)S(1)}, u32[]{:S(2)}, u32[]{:S(2)}) collective-permute-start(bf16[128,2560]{1,0:T(8,128)(2,1)S(1)} %copy-done.12), channel_id=1, source_target_pairs={{0,1},{1,0},{2,3},{3,2},{4,5},{5,4},{6,7},{7,6},{8,9},{9,8},{10,11... | collective-permute-start | bytes 1966088 | tf_op jit(solution)/shard_map/ppermute | solution.py:408
  208.8 74.7 %collective-permute-start.17 = (bf16[1,320,640]{2,1,0:T(8,128)(2,1)}, bf16[1,320,640]{2,1,0:T(8,128)(2,1)}, u32[]{:S(2)}, u32[]{:S(2)}) collective-permute-start(bf16[1,320,640]{2,1,0:T(8,128)(2,1)} %bitcast.33.refs_0_), channel_id=1, source_target_pairs={{0,24},{2,26},{4,28},{6,30},{8,0},{10,2},{12,4},{14,6},{16,8},{18,... | collective-permute-start | bytes 1228808 | tf_op jit(solution)/shard_map/ppermute | solution.py:413
  235.4 50.0 %collective-permute-start.16 = (bf16[1,320,640]{2,1,0:T(8,128)(2,1)}, bf16[1,320,640]{2,1,0:T(8,128)(2,1)}, u32[]{:S(2)}, u32[]{:S(2)}) collective-permute-start(bf16[1,320,640]{2,1,0:T(8,128)(2,1)} %bitcast.33.refs_0_), channel_id=1, source_target_pairs={{0,16},{2,18},{4,20},{6,22},{8,24},{10,26},{12,28},{14,30},{16,0},... | collective-permute-start | bytes 1228808 | tf_op jit(solution)/shard_map/ppermute | solution.py:413
  239.8 45.6 %collective-permute-start.15 = (bf16[1,320,640]{2,1,0:T(8,128)(2,1)}, bf16[1,320,640]{2,1,0:T(8,128)(2,1)}, u32[]{:S(2)}, u32[]{:S(2)}) collective-permute-start(bf16[1,320,640]{2,1,0:T(8,128)(2,1)} %bitcast.33.refs_0_), channel_id=1, source_target_pairs={{0,8},{2,10},{4,12},{6,14},{8,16},{10,18},{12,20},{14,22},{16,24},... | collective-permute-start | bytes 1228808 | tf_op jit(solution)/shard_map/ppermute | solution.py:413
  239.8 8.1 collective-permute-start.8
  247.2 36.4 %collective-permute-start.11 = (bf16[128,2560]{1,0:T(8,128)(2,1)}, bf16[128,2560]{1,0:T(8,128)(2,1)}, u32[]{:S(2)}, u32[]{:S(2)}) collective-permute-start(bf16[128,2560]{1,0:T(8,128)(2,1)} %shard_map.298), channel_id=1, source_target_pairs={{0,8},{2,10},{4,12},{6,14},{8,16},{10,18},{12,20},{14,22},{16,24},... | collective-permute-start | bytes 1966088 | tf_op jit(solution)/shard_map/ppermute | solution.py:413
  260.0 17.6 %collective-permute-start.9 = (bf16[256,1280]{1,0:T(8,128)(2,1)S(1)}, bf16[256,1280]{1,0:T(8,128)(2,1)S(1)}, u32[]{:S(2)}, u32[]{:S(2)}) collective-permute-start(bf16[256,1280]{1,0:T(8,128)(2,1)S(1)} %slice.376), channel_id=1, source_target_pairs={{0,2},{2,0},{4,6},{6,4},{8,10},{10,8},{12,14},{14,12},{16,18},{18,... | collective-permute-start | bytes 1966088 | tf_op jit(solution)/shard_map/ppermute | solution.py:410
  277.6 44.4 %collective-permute-start.13 = (bf16[128,2560]{1,0:T(8,128)(2,1)}, bf16[128,2560]{1,0:T(8,128)(2,1)}, u32[]{:S(2)}, u32[]{:S(2)}) collective-permute-start(bf16[128,2560]{1,0:T(8,128)(2,1)} %shard_map.298), channel_id=1, source_target_pairs={{0,16},{2,18},{4,20},{6,22},{8,24},{10,26},{12,28},{14,30},{16,0},... | collective-permute-start | bytes 1966088 | tf_op jit(solution)/shard_map/ppermute | solution.py:413
  288.0 74.2 %collective-permute-start.18 = (bf16[4,320,640]{2,1,0:T(8,128)(2,1)}, bf16[4,320,640]{2,1,0:T(8,128)(2,1)}, u32[]{:S(2)}, u32[]{:S(2)}) collective-permute-start(bf16[4,320,640]{2,1,0:T(8,128)(2,1)} %bitcast.34), channel_id=1, source_target_pairs={{0,4},{2,6},{4,0},{6,2},{8,12},{10,14},{12,8},{14,10},{16,20},{18,... | collective-permute-start | bytes 4915208 | tf_op jit(solution)/shard_map/ppermute | solution.py:410
  304.3 16.6 %collective-permute-start.12 = (bf16[256,640]{1,0:T(8,128)(2,1)}, bf16[256,640]{1,0:T(8,128)(2,1)}, u32[]{:S(2)}, u32[]{:S(2)}) collective-permute-start(bf16[256,640]{1,0:T(8,128)(2,1)} %get-tuple-element.197), channel_id=1, source_target_pairs={{0,2},{2,0},{4,6},{6,4},{8,10},{10,8},{12,14},{14,12},{16,18},{18,... | collective-permute-start | bytes 983048 | tf_op jit(solution)/shard_map/ppermute | solution.py:410
  370.9 3.4 collective-permute-start.19
  370.9 27.8 %collective-permute-start.21 = (bf16[128,2560]{1,0:T(8,128)(2,1)}, bf16[128,2560]{1,0:T(8,128)(2,1)}, u32[]{:S(2)}, u32[]{:S(2)}) collective-permute-start(bf16[128,2560]{1,0:T(8,128)(2,1)} %shard_map.298), channel_id=1, source_target_pairs={{0,24},{2,26},{4,28},{6,30},{8,0},{10,2},{12,4},{14,6},{16,8},{18,... | collective-permute-start | bytes 1966088 | tf_op jit(solution)/shard_map/ppermute | solution.py:413
  379.1 17.9 %collective-permute-start.20 = (bf16[128,2560]{1,0:T(8,128)(2,1)}, bf16[128,2560]{1,0:T(8,128)(2,1)}, u32[]{:S(2)}, u32[]{:S(2)}) collective-permute-start(bf16[128,2560]{1,0:T(8,128)(2,1)} %fusion.35), channel_id=1, source_target_pairs={{0,2},{2,0},{4,6},{6,4},{8,10},{10,8},{12,14},{14,12},{16,18},{18,... | collective-permute-start | bytes 1966088 | tf_op jit(solution)/shard_map/ppermute | solution.py:410
  400.3 18.1 %collective-permute-start.24 = (bf16[128,2560]{1,0:T(8,128)(2,1)S(1)}, bf16[128,2560]{1,0:T(8,128)(2,1)S(1)}, u32[]{:S(2)}, u32[]{:S(2)}) collective-permute-start(bf16[128,2560]{1,0:T(8,128)(2,1)S(1)} %shard_map.302), channel_id=1, source_target_pairs={{0,24},{2,26},{4,28},{6,30},{8,0},{10,2},{12,4},{14,6},{16,8},{18,... | collective-permute-start | bytes 1966088 | tf_op jit(solution)/shard_map/ppermute | solution.py:413
  403.1 55.6 %collective-permute-start.23 = (bf16[128,2560]{1,0:T(8,128)(2,1)S(1)}, bf16[128,2560]{1,0:T(8,128)(2,1)S(1)}, u32[]{:S(2)}, u32[]{:S(2)}) collective-permute-start(bf16[128,2560]{1,0:T(8,128)(2,1)S(1)} %shard_map.302), channel_id=1, source_target_pairs={{0,16},{2,18},{4,20},{6,22},{8,24},{10,26},{12,28},{14,30},{16,0},... | collective-permute-start | bytes 1966088 | tf_op jit(solution)/shard_map/ppermute | solution.py:413
  403.1 55.6 %collective-permute-start.22 = (bf16[128,2560]{1,0:T(8,128)(2,1)S(1)}, bf16[128,2560]{1,0:T(8,128)(2,1)S(1)}, u32[]{:S(2)}, u32[]{:S(2)}) collective-permute-start(bf16[128,2560]{1,0:T(8,128)(2,1)S(1)} %shard_map.302), channel_id=1, source_target_pairs={{0,8},{2,10},{4,12},{6,14},{8,16},{10,18},{12,20},{14,22},{16,24},... | collective-permute-start | bytes 1966088 | tf_op jit(solution)/shard_map/ppermute | solution.py:413
  408.1 52.2 %collective-permute-start.28 = (bf16[512,2560]{1,0:T(8,128)(2,1)}, bf16[512,2560]{1,0:T(8,128)(2,1)S(1)}, u32[]{:S(2)}, u32[]{:S(2)}) collective-permute-start(bf16[512,2560]{1,0:T(8,128)(2,1)} %constant_dynamic-update-slice_fusion.act.refs_0_), channel_id=1, source_target_pairs={{0,1},{1,0},{2,3},{3,2},{4,5},{5,4},{6,7},{7,6},{8,9},{9,8},{10,11... | collective-permute-start | bytes 7864328 | tf_op jit(solution)/shard_map/ppermute | solution.py:408
  460.3 10.1 %collective-permute-start.27 = (bf16[512,2560]{1,0:T(8,128)(2,1)}, bf16[512,2560]{1,0:T(8,128)(2,1)}, u32[]{:S(2)}, u32[]{:S(2)}) collective-permute-start(bf16[512,2560]{1,0:T(8,128)(2,1)} %pad_maximum_fusion.1.act.refs_0_), channel_id=1, source_target_pairs={{0,1},{1,0},{2,3},{3,2},{4,5},{5,4},{6,7},{7,6},{8,9},{9,8},{10,11... | collective-permute-start | bytes 7864328 | tf_op jit(solution)/shard_map/ppermute | solution.py:408
  489.2 27.0 %collective-permute-start.29 = (bf16[512,2560]{1,0:T(8,128)(2,1)}, bf16[512,2560]{1,0:T(8,128)(2,1)S(1)}, u32[]{:S(2)}, u32[]{:S(2)}) collective-permute-start(bf16[512,2560]{1,0:T(8,128)(2,1)} %shard_map.309), channel_id=1, source_target_pairs={{0,1},{1,0},{2,3},{3,2},{4,5},{5,4},{6,7},{7,6},{8,9},{9,8},{10,11... | collective-permute-start | bytes 7864328 | tf_op jit(solution)/shard_map/ppermute | solution.py:408
  549.0 420.2 %reduce-scatter.5.cloned.1.call-start = ((), (), s32[]{:S(2)}) async-start(), calls=%async_computation.4 | async-start | bytes 7372800 | tf_op jit(solution)/shard_map/reduce_scatter | solution.py:631
  549.0 16.8 %collective-permute-start.30 = (bf16[128,2560]{1,0:T(8,128)(2,1)S(1)}, bf16[128,2560]{1,0:T(8,128)(2,1)}, u32[]{:S(2)}, u32[]{:S(2)}) collective-permute-start(bf16[128,2560]{1,0:T(8,128)(2,1)S(1)} %get-tuple-element.172), channel_id=1, source_target_pairs={{0,24},{2,26},{4,28},{6,30},{8,0},{10,2},{12,4},{14,6},{16,8},{18,... | collective-permute-start | bytes 1966088 | tf_op jit(solution)/shard_map/ppermute | solution.py:413
  577.2 15.2 %collective-permute-start.33 = (bf16[512,2560]{1,0:T(8,128)(2,1)}, bf16[512,2560]{1,0:T(8,128)(2,1)S(1)}, u32[]{:S(2)}, u32[]{:S(2)}) collective-permute-start(bf16[512,2560]{1,0:T(8,128)(2,1)} %shard_map.314), channel_id=1, source_target_pairs={{0,1},{1,0},{2,3},{3,2},{4,5},{5,4},{6,7},{7,6},{8,9},{9,8},{10,11... | collective-permute-start | bytes 7864328 | tf_op jit(solution)/shard_map/ppermute | solution.py:408
  577.2 23.9 %collective-permute-start.32 = (bf16[128,2560]{1,0:T(8,128)(2,1)}, bf16[128,2560]{1,0:T(8,128)(2,1)S(1)}, u32[]{:S(2)}, u32[]{:S(2)}) collective-permute-start(bf16[128,2560]{1,0:T(8,128)(2,1)} %get-tuple-element.173), channel_id=1, source_target_pairs={{0,8},{2,10},{4,12},{6,14},{8,16},{10,18},{12,20},{14,22},{16,24},... | collective-permute-start | bytes 1966088 | tf_op jit(solution)/shard_map/ppermute | solution.py:413
  578.9 73.7 %collective-permute-start.31 = (bf16[128,2560]{1,0:T(8,128)(2,1)}, bf16[128,2560]{1,0:T(8,128)(2,1)S(1)}, u32[]{:S(2)}, u32[]{:S(2)}) collective-permute-start(bf16[128,2560]{1,0:T(8,128)(2,1)} %get-tuple-element.174), channel_id=1, source_target_pairs={{0,16},{2,18},{4,20},{6,22},{8,24},{10,26},{12,28},{14,30},{16,0},... | collective-permute-start | bytes 1966088 | tf_op jit(solution)/shard_map/ppermute | solution.py:413
  596.2 56.5 %collective-permute-start.36 = (bf16[128,2560]{1,0:T(8,128)(2,1)S(1)}, bf16[128,2560]{1,0:T(8,128)(2,1)S(1)}, u32[]{:S(2)}, u32[]{:S(2)}) collective-permute-start(bf16[128,2560]{1,0:T(8,128)(2,1)S(1)} %get-tuple-element.169), channel_id=1, source_target_pairs={{0,8},{2,10},{4,12},{6,14},{8,16},{10,18},{12,20},{14,22},{16,24},... | collective-permute-start | bytes 1966088 | tf_op jit(solution)/shard_map/ppermute | solution.py:413
  597.6 69.1 %collective-permute-start.35 = (bf16[128,2560]{1,0:T(8,128)(2,1)S(1)}, bf16[128,2560]{1,0:T(8,128)(2,1)S(1)}, u32[]{:S(2)}, u32[]{:S(2)}) collective-permute-start(bf16[128,2560]{1,0:T(8,128)(2,1)S(1)} %get-tuple-element.170), channel_id=1, source_target_pairs={{0,16},{2,18},{4,20},{6,22},{8,24},{10,26},{12,28},{14,30},{16,0},... | collective-permute-start | bytes 1966088 | tf_op jit(solution)/shard_map/ppermute | solution.py:413
  599.7 67.0 %collective-permute-start.34 = (bf16[128,2560]{1,0:T(8,128)(2,1)S(1)}, bf16[128,2560]{1,0:T(8,128)(2,1)S(1)}, u32[]{:S(2)}, u32[]{:S(2)}) collective-permute-start(bf16[128,2560]{1,0:T(8,128)(2,1)S(1)} %get-tuple-element.171), channel_id=1, source_target_pairs={{0,24},{2,26},{4,28},{6,30},{8,0},{10,2},{12,4},{14,6},{16,8},{18,... | collective-permute-start | bytes 1966088 | tf_op jit(solution)/shard_map/ppermute | solution.py:413
  670.3 31.4 %collective-permute-start.37 = (bf16[128,2560]{1,0:T(8,128)(2,1)S(1)}, bf16[128,2560]{1,0:T(8,128)(2,1)S(1)}, u32[]{:S(2)}, u32[]{:S(2)}) collective-permute-start(bf16[128,2560]{1,0:T(8,128)(2,1)S(1)} %fusion.60), channel_id=1, source_target_pairs={{0,2},{2,0},{4,6},{6,4},{8,10},{10,8},{12,14},{14,12},{16,18},{18,... | collective-permute-start | bytes 1966088 | tf_op jit(solution)/shard_map/ppermute | solution.py:410
  703.4 3.4 collective-permute-start.38
  715.3 32.2 %collective-permute-start.40 = (bf16[3,160,960]{2,1,0:T(8,128)(2,1)S(1)}, bf16[3,160,960]{2,1,0:T(8,128)(2,1)S(1)}, u32[]{:S(2)}, u32[]{:S(2)}) collective-permute-start(bf16[3,160,960]{2,1,0:T(8,128)(2,1)S(1)} %get-tuple-element.165), channel_id=1, source_target_pairs={{0,8},{2,10},{4,12},{6,14},{8,16},{10,18},{12,20},{14,22},{16,24},... | collective-permute-start | bytes 2764808 | tf_op jit(solution)/shard_map/ppermute | solution.py:413
  725.9 9.5 collective-permute-start.39
  748.6 9.3 collective-permute-start.42
  787.5 10.7 %collective-permute-start.41 = (bf16[256,640]{1,0:T(8,128)(2,1)S(1)}, bf16[256,640]{1,0:T(8,128)(2,1)S(1)}, u32[]{:S(2)}, u32[]{:S(2)}) collective-permute-start(bf16[256,640]{1,0:T(8,128)(2,1)S(1)} %get-tuple-element.193), channel_id=1, source_target_pairs={{0,2},{2,0},{4,6},{6,4},{8,10},{10,8},{12,14},{14,12},{16,18},{18,... | collective-permute-start | bytes 983048 | tf_op jit(solution)/shard_map/ppermute | solution.py:410
  788.8 28.1 %collective-permute-start.54 = (bf16[4,2,48,1280]{3,2,1,0:T(8,128)(2,1)S(1)}, bf16[4,2,48,1280]{3,2,1,0:T(8,128)(2,1)S(1)}, u32[]{:S(2)}, u32[]{:S(2)}) collective-permute-start(bf16[4,2,48,1280]{3,2,1,0:T(8,128)(2,1)S(1)} %fusion.31), channel_id=1, source_target_pairs={{0,2},{2,0},{4,6},{6,4},{8,10},{10,8},{12,14},{14,12},{16,18},{18,... | collective-permute-start | bytes 2949128 | tf_op jit(solution)/shard_map/ppermute | solution.py:410
  793.6 89.7 %collective-permute-start.47 = (bf16[3,160,960]{2,1,0:T(8,128)(2,1)}, bf16[3,160,960]{2,1,0:T(8,128)(2,1)}, u32[]{:S(2)}, u32[]{:S(2)}) collective-permute-start(bf16[3,160,960]{2,1,0:T(8,128)(2,1)} %get-tuple-element.162), channel_id=1, source_target_pairs={{0,24},{2,26},{4,28},{6,30},{8,0},{10,2},{12,4},{14,6},{16,8},{18,... | collective-permute-start | bytes 2764808 | tf_op jit(solution)/shard_map/ppermute | solution.py:413
  817.1 11.0 %collective-permute-start.55 = (bf16[4,48,1280]{2,1,0:T(8,128)(2,1)S(1)}, bf16[4,48,1280]{2,1,0:T(8,128)(2,1)S(1)}, u32[]{:S(2)}, u32[]{:S(2)}) collective-permute-start(bf16[4,48,1280]{2,1,0:T(8,128)(2,1)S(1)} %fusion.37), channel_id=1, source_target_pairs={{0,4},{2,6},{4,0},{6,2},{8,12},{10,14},{12,8},{14,10},{16,20},{18,... | collective-permute-start | bytes 1474568 | tf_op jit(solution)/shard_map/ppermute | solution.py:410
  818.9 58.3 %collective-permute-start.43 = (bf16[2,128,2560]{2,1,0:T(8,128)(2,1)S(1)}, bf16[2,128,2560]{2,1,0:T(8,128)(2,1)S(1)}, u32[]{:S(2)}, u32[]{:S(2)}) collective-permute-start(bf16[2,128,2560]{2,1,0:T(8,128)(2,1)S(1)} %fusion.16), channel_id=1, source_target_pairs={{0,1},{1,0},{2,3},{3,2},{4,5},{5,4},{6,7},{7,6},{8,9},{9,8},{10,11... | collective-permute-start | bytes 3932168 | tf_op jit(solution)/shard_map/ppermute | solution.py:408
  828.3 16.9 %collective-permute-start.56 = (bf16[48,1280]{1,0:T(8,128)(2,1)S(1)}, bf16[48,1280]{1,0:T(8,128)(2,1)S(1)}, u32[]{:S(2)}, u32[]{:S(2)}) collective-permute-start(bf16[48,1280]{1,0:T(8,128)(2,1)S(1)} %get-tuple-element.185), channel_id=1, source_target_pairs={{0,8},{2,10},{4,12},{6,14},{8,16},{10,18},{12,20},{14,22},{16,24},... | collective-permute-start | bytes 368648 | tf_op jit(solution)/shard_map/ppermute | solution.py:413
  828.3 20.3 %collective-permute-start.58 = (bf16[48,1280]{1,0:T(8,128)(2,1)S(1)}, bf16[48,1280]{1,0:T(8,128)(2,1)S(1)}, u32[]{:S(2)}, u32[]{:S(2)}) collective-permute-start(bf16[48,1280]{1,0:T(8,128)(2,1)S(1)} %get-tuple-element.186), channel_id=1, source_target_pairs={{0,24},{2,26},{4,28},{6,30},{8,0},{10,2},{12,4},{14,6},{16,8},{18,... | collective-permute-start | bytes 368648 | tf_op jit(solution)/shard_map/ppermute | solution.py:413
  832.4 44.1 %collective-permute-start.57 = (bf16[48,1280]{1,0:T(8,128)(2,1)S(1)}, bf16[48,1280]{1,0:T(8,128)(2,1)S(1)}, u32[]{:S(2)}, u32[]{:S(2)}) collective-permute-start(bf16[48,1280]{1,0:T(8,128)(2,1)S(1)} %get-tuple-element.187), channel_id=1, source_target_pairs={{0,16},{2,18},{4,20},{6,22},{8,24},{10,26},{12,28},{14,30},{16,0},... | collective-permute-start | bytes 368648 | tf_op jit(solution)/shard_map/ppermute | solution.py:413
  845.1 51.8 %collective-permute-start.46 = (bf16[3,160,960]{2,1,0:T(8,128)(2,1)}, bf16[3,160,960]{2,1,0:T(8,128)(2,1)S(1)}, u32[]{:S(2)}, u32[]{:S(2)}) collective-permute-start(bf16[3,160,960]{2,1,0:T(8,128)(2,1)} %get-tuple-element.164), channel_id=1, source_target_pairs={{0,16},{2,18},{4,20},{6,22},{8,24},{10,26},{12,28},{14,30},{16,0},... | collective-permute-start | bytes 2764808 | tf_op jit(solution)/shard_map/ppermute | solution.py:413
  848.6 48.3 %collective-permute-start.45 = (bf16[4,2,160,640]{3,2,1,0:T(8,128)(2,1)}, bf16[4,2,160,640]{3,2,1,0:T(8,128)(2,1)}, u32[]{:S(2)}, u32[]{:S(2)}) collective-permute-start(bf16[4,2,160,640]{3,2,1,0:T(8,128)(2,1)} %fusion.3), channel_id=1, source_target_pairs={{0,4},{2,6},{4,0},{6,2},{8,12},{10,14},{12,8},{14,10},{16,20},{18,... | collective-permute-start | bytes 4915208 | tf_op jit(solution)/shard_map/ppermute | solution.py:410
  879.9 24.3 %collective-permute-start.44 = (bf16[128,2560]{1,0:T(8,128)(2,1)}, bf16[128,2560]{1,0:T(8,128)(2,1)S(1)}, u32[]{:S(2)}, u32[]{:S(2)}) collective-permute-start(bf16[128,2560]{1,0:T(8,128)(2,1)} %fusion.36), channel_id=1, source_target_pairs={{0,2},{2,0},{4,6},{6,4},{8,10},{10,8},{12,14},{14,12},{16,18},{18,... | collective-permute-start | bytes 1966088 | tf_op jit(solution)/shard_map/ppermute | solution.py:410
  900.2 17.1 %collective-permute-start.50 = (bf16[2,160,640]{2,1,0:T(8,128)(2,1)S(1)}, bf16[2,160,640]{2,1,0:T(8,128)(2,1)S(1)}, u32[]{:S(2)}, u32[]{:S(2)}) collective-permute-start(bf16[2,160,640]{2,1,0:T(8,128)(2,1)S(1)} %get-tuple-element.166), channel_id=1, source_target_pairs={{0,24},{2,26},{4,28},{6,30},{8,0},{10,2},{12,4},{14,6},{16,8},{18,... | collective-permute-start | bytes 1228808 | tf_op jit(solution)/shard_map/ppermute | solution.py:413
  901.8 58.5 %collective-permute-start.49 = (bf16[2,160,640]{2,1,0:T(8,128)(2,1)S(1)}, bf16[2,160,640]{2,1,0:T(8,128)(2,1)S(1)}, u32[]{:S(2)}, u32[]{:S(2)}) collective-permute-start(bf16[2,160,640]{2,1,0:T(8,128)(2,1)S(1)} %get-tuple-element.167), channel_id=1, source_target_pairs={{0,16},{2,18},{4,20},{6,22},{8,24},{10,26},{12,28},{14,30},{16,0},... | collective-permute-start | bytes 1228808 | tf_op jit(solution)/shard_map/ppermute | solution.py:413
  902.3 58.1 %collective-permute-start.48 = (bf16[2,160,640]{2,1,0:T(8,128)(2,1)S(1)}, bf16[2,160,640]{2,1,0:T(8,128)(2,1)S(1)}, u32[]{:S(2)}, u32[]{:S(2)}) collective-permute-start(bf16[2,160,640]{2,1,0:T(8,128)(2,1)S(1)} %get-tuple-element.168), channel_id=1, source_target_pairs={{0,8},{2,10},{4,12},{6,14},{8,16},{10,18},{12,20},{14,22},{16,24},... | collective-permute-start | bytes 1228808 | tf_op jit(solution)/shard_map/ppermute | solution.py:413
  960.6 8.4 collective-permute-start.51
  970.4 5.8 collective-permute-start.52
  972.1 6.3 collective-permute-start.59
  977.8 1.7 collective-permute-start.53
  (98 other events, 694.8 us)
Sparse Core Ops, SparseCore 0:
  23.3 161.2 all-gather.2
  186.5 212.0 all-gather.4
  549.1 161.1 reduce-scatter.6
  762.3 201.4 reduce-scatter.4

commit v3 on v2

--- a/solution.py
+++ b/solution.py
@@ -275,8 +275,8 @@
 
 
 def weight_of(weights, which):
-    corners, _, *rest = weights.shape
-    return pl.BlockSpec((corners, 1, *rest), lambda i: (0, which, 0, 0, 0))
+    corners, _, *rest = weights[0].shape
+    return pl.BlockSpec((corners, 1, *rest), lambda i: (0, which % 2, 0, 0, 0))
 
 
 def flat(ref):
@@ -285,7 +285,7 @@
 
 def ffn_down_back(act, weights):
     tokens, width = act.shape
-    units = weights.shape[-1]
+    units = weights[0].shape[-1]
 
     def kernel(act, down, out):
         out[...] = matmul(act[...], flat(down))
@@ -297,12 +297,12 @@
         out_specs=rows_of(units),
         out_shape=jax.ShapeDtypeStruct((tokens, units), F32),
         compiler_params=params(48),
-    )(act, weights)
+    )(act, weights[1])
 
 
 def ffn_middle(act, weights, grad_hidden):
     tokens, width = act.shape
-    units = weights.shape[-1]
+    units = weights[0].shape[-1]
 
     def kernel(act, grad, gate, up, hidden, grads):
         value = act[...]
@@ -328,12 +328,12 @@
             jax.ShapeDtypeStruct((2, tokens, units), BF16),
         ],
         compiler_params=params(56),
-    )(act, grad_hidden, weights, weights)
+    )(act, grad_hidden, weights[0], weights[0])
 
 
 def ffn_collect(acts, weights, which, dtype):
     n, tokens, units = acts.shape
-    width = weights.shape[0] * weights.shape[2] * weights.shape[3]
+    width = math.prod(weights[1].shape[:-1])
 
     def kernel(acts, *refs):
         total = contract_last(acts[0], flat(refs[0]))
@@ -349,7 +349,7 @@
         out_specs=rows_of(width),
         out_shape=jax.ShapeDtypeStruct((tokens, width), dtype),
         compiler_params=params(56),
-    )(acts, *[weights] * n)
+    )(acts, *[weights[w // 2] for w in which])
 
 
 def weight_grad(acts, grads, lead, tail, dtype, n=None, at=0, into=None):
@@ -473,6 +473,9 @@
         slim = conv_bias.shape[0]
         here_x = grid.x == 0
 
+        down_rows = jnp.transpose(ffn_down)
+        slices = grid.shifts(cut((ffn_gate, ffn_up), grid.z, nz))
+
         vectors = jnp.concatenate(
             [conv_taps.reshape(-1), conv_bias, bias_a, bias_in, decay_param, gain_mix, gain_mlp]
         )
@@ -484,7 +487,7 @@
                 jnp.pad(vectors[None], ((0, pad_rows - 1), (0, half - vectors.shape[0]))),
             ]
         )
-        early = grid.shifts([packed[None]] * nz)
+        early = grid.shifts([after(packed[None], slices[1])] * nz)
         small = line_up(early, grid.z)[0]
         small = grid.pair(small, grid.swap(small, "y"), "y")
         small = grid.pair(small, grid.swap(small, "x"), "x")
@@ -500,34 +503,29 @@
         full_gain_mlp = vecs[:, 8 * slim + part : 8 * slim + 2 * part].reshape(width)
 
         by_x = lambda w: jnp.stack([w[:, :quarter], w[:, quarter:]])
-        mine = jnp.concatenate([by_x(branch_x), by_x(branch_y)], axis=-1)
-        mine = grid.trade(mine, "x").reshape(2 * part, -1)
-        full_in = lax.all_gather(mine, "dp", axis=0, tiled=True, axis_index_groups=grid.planes)
+        mine = [by_x(w) for w in (branch_x, branch_y, jnp.transpose(out_proj))]
+        mine = grid.trade(jnp.concatenate(mine, axis=-1), "x").reshape(2 * part, -1)
+        mixer = lax.all_gather(mine, "dp", axis=0, tiled=True, axis_index_groups=grid.planes)
+        full_in, full_out = mixer[:, : 2 * quarter], mixer[:, 2 * quarter :]
         across = grid.swap(after(inputs, mine), "x")
 
         normed = norm_rows(
             (inputs, grid.swap(inputs, "t")), (across, grid.swap(across, "t")), full_gain_mix, grid.t
         )
 
-        down_rows = jnp.transpose(ffn_down)
-        slices = cut((ffn_gate, ffn_up, down_rows), grid.z, nz)
-        slices = grid.shifts(slices)
-        out_mine = grid.trade(by_x(jnp.transpose(out_proj)), "x").reshape(1, 2 * part, -1)
-        out_line = grid.shifts([after(out_mine, slices[1])] * nz)
-        weights = lax.all_gather(
-            after(line_up(slices, grid.z)[None], full_in, small),
-            "dp",
-            axis=0,
-            tiled=True,
-            axis_index_groups=grid.corners,
-        )
+        def plane(own):
+            return lax.all_gather(own, "dp", axis=0, tiled=True, axis_index_groups=grid.corners)
+
+        slices = line_up(after(slices, normed, full_gate_a, full_gate_in, per), grid.z)[None]
+        weights_pair = plane(after(slices, mixer))
+        down_slices = grid.shifts(after(tuple(cut((down_rows,), grid.z, nz)), slices))
 
         def to_line(value, *deps):
             value = after(reorder(value, nz, False), *deps)
             return grid.shifts([value] * nz)
 
         rows = inputs.astype(F32)
-        cot_line = to_line(cotangent, slices[1])
+        cot_line = to_line(cotangent, down_slices[1])
         pre = matmul(normed, full_in).reshape(2, length, 2 * quarter)
 
         def whole_half(mine, other):
@@ -541,16 +539,15 @@
             return jnp.concatenate([jnp.where(here_x, low, high), away])
 
         got = grid.swap(pre[1].astype(BF16), "x").astype(F32)
-        got = after(got, cot_line[1])
-        out_here = line_up(after(out_line, got), grid.z)[0]
-        full_out = grid.pair(out_here, grid.swap(out_here, "y"), "y")
-        full_out = jnp.swapaxes(full_out, 0, 1).reshape(width, -1)
+        got = after(got, *down_slices[1:])
+        weights_down = plane(after(line_up(down_slices, grid.z)[None], weights_pair))
+        weights = (weights_pair, weights_down)
         pre_x = whole_half(pre[0, :, :quarter], got[:, :quarter])
         pre_y = whole_half(pre[0, :, quarter:], got[:, quarter:])
         mixed, states, conv, rate, entry = by_head(
             mixer_forward, heads, length, block, "rrggv", [("r", BF16)] + [("r", F32)] * 4
         )(pre_x, pre_y, full_gate_a, full_gate_in, per)
-        mixed = after(to_rows(mixed), cot_line[2])
+        mixed = after(to_rows(mixed), cot_line[1])
         branch_out = contract_last(mixed, full_out).reshape(2, 2, rows_each, width)
         branch_out = grid.reduce(branch_out, "t", 1)
         branch_out = branch_out[0] + grid.swap(branch_out[1].astype(BF16), "x").astype(F32)

time: 999 us -> 976 us (0.977)
  waiting for transfers between devices: 565 us -> 542 us
    all_gather x1, waiting for transfers between devices: 14.6 us -> 59.8 us  [run(): lax.all_gather(mine, 'dp', axis=0, tiled=True, axis_index_groups=grid.pla...]
    ppermute x20 -> x18, waiting for transfers between devices: 184 us -> 140 us  [swap(): return lax.ppermute(value, 'dp', [(i, i ^ bit) for i in range(self.n)])]
    ppermute x30, waiting for transfers between devices: 362 us -> 324 us  [shift(): lax.ppermute(value, 'dp', [(i, (i + 4 * by) % self.n) for i in range(self...]
    all_gather x1 -> x2, waiting for transfers between devices: 0.01 us -> 14.2 us  [plane(): lax.all_gather(own, 'dp', axis=0, tiled=True, axis_index_groups=grid.corn...]
    ppermute x20 -> x18, starting transfers between devices: 34 us -> 23.7 us  [swap(): return lax.ppermute(value, 'dp', [(i, i ^ bit) for i in range(self.n)])]
    unnamed x202 -> x216, local copies, waits for them, and re-layouts: 54.9 us -> 54.7 us
  transfers between devices with their start and end apart: 64 -> 63, of which waited for: 35 -> 35; matrix products, arithmetic and copies ran while one was open for 9% -> 9% of each run, Pallas kernels for 9% -> 9%
where the time goes in v3:
time: 976 us; the launch traced here: 964 us
  waiting for transfers between devices  542 us (56%)
  Pallas kernels  139 us (14%)
  starting transfers between devices  114 us (12%)
  local copies, waits for them, and re-layouts  90 us (9%)
  other arithmetic  42.7 us (4%)
  matrix products  20.7 us (2%)
  between operations  15.8 us (2%)
    ppermute x30, waiting for transfers between devices, shift(): lax.ppermute(value, 'dp', [(i, (i + 4 * by) % self.n) for i in range(self...  324 us
    ppermute x18, waiting for transfers between devices, swap(): return lax.ppermute(value, 'dp', [(i, i ^ bit) for i in range(self.n)])  140 us
    ppermute x30, starting transfers between devices, shift(): lax.ppermute(value, 'dp', [(i, (i + 4 * by) % self.n) for i in range(self...  89.3 us
    all_gather x1, waiting for transfers between devices, run(): lax.all_gather(mine, 'dp', axis=0, tiled=True, axis_index_groups=grid.pla...  59.8 us
    unnamed x216, local copies, waits for them, and re-layouts  54.7 us
    pallas_call x4, Pallas kernels, ffn_collect(): pl.pallas_call(kernel, grid=(tokens // TILE,), in_specs=[pl.BlockSpec((n,...  38.4 us
    pallas_call x5, Pallas kernels, weight_grad(): pl.pallas_call(kernel, grid=(m, width // block // at_once), in_specs=[pl....  37.6 us
    pallas_call x2, Pallas kernels, ffn_middle(): pl.pallas_call(kernel, grid=(tokens // TILE,), in_specs=[rows_of(width),...  23.8 us
  transfers between devices with their start and end apart: 63, of which 35 were waited for; matrix products, arithmetic and copies ran while one was open for 9% of the time, Pallas kernels for 9%

profile of v3, /device:TPU:0, one launch (start us, length us, event | category | flops | bytes accessed | tf_op | source)
XLA Modules:
  0.0 963.7 jit_solution(11225755387485822279)
XLA Ops:
  12.8 13.9 %collective-permute-done.7 = bf16[160,1920]{1,0:T(8,128)(2,1)S(1)} collective-permute-done((bf16[160,1920]{1,0:T(8,128)(2,1)S(1)}, bf16[160,1920]{1,0:T(8,128)(2,1)S(1)}, u32[]{:S(2)}, u32[]{:S(2)}) %collective-permute-start.7) | collective-permute-done | bytes 614432 | tf_op jit(solution)/shard_map/ppermute | solution.py:410
  34.8 22.3 %collective-permute-done.refs_1_ = bf16[2,160,960]{2,1,0:T(8,128)(2,1)S(1)} collective-permute-done((bf16[2,160,960]{2,1,0:T(8,128)(2,1)S(1)}, bf16[2,160,960]{2,1,0:T(8,128)(2,1)S(1)}, u32[]{:S(2)}, u32[]{:S(2)}) %collective-permute-start) | collective-permute-done | bytes 614432 | tf_op jit(solution)/shard_map/ppermute | solution.py:413
  57.1 13.6 %collective-permute-start.3 = (bf16[1,48,1280]{2,1,0:T(8,128)(2,1)S(1)}, bf16[1,48,1280]{2,1,0:T(8,128)(2,1)S(1)}, u32[]{:S(2)}, u32[]{:S(2)}) collective-permute-start(bf16[1,48,1280]{2,1,0:T(8,128)(2,1)S(1)} %fusion.51.refs_0_), channel_id=1, source_target_pairs={{0,24},{2,26},{4,28},{6,30},{8,0},{10,2},{12,4},{14,6},{16,8},{18,... | collective-permute-start | bytes 368648 | tf_op jit(solution)/shard_map/ppermute | solution.py:413
  77.4 13.7 %collective-permute-done.2.refs_2_ = bf16[1,48,1280]{2,1,0:T(8,128)(2,1)S(1)} collective-permute-done((bf16[1,48,1280]{2,1,0:T(8,128)(2,1)S(1)}, bf16[1,48,1280]{2,1,0:T(8,128)(2,1)S(1)}, u32[]{:S(2)}, u32[]{:S(2)}) %collective-permute-start.2) | collective-permute-done | bytes 122912 | tf_op jit(solution)/shard_map/ppermute | solution.py:413
  92.4 7.6 collective-permute-done.4
  103.2 3.4 collective-permute-start.11
  106.8 16.3 %collective-permute-done.8.refs_2_ = bf16[128,2560]{1,0:T(8,128)(2,1)S(1)} collective-permute-done((bf16[128,2560]{1,0:T(8,128)(2,1)S(1)}, bf16[128,2560]{1,0:T(8,128)(2,1)S(1)}, u32[]{:S(2)}, u32[]{:S(2)}) %collective-permute-start.8) | collective-permute-done | bytes 655392 | tf_op jit(solution)/shard_map/ppermute | solution.py:410
  127.1 4.0 reshape.359
  140.2 26.5 %collective-permute-done.11.refs_2_ = bf16[2,160,960]{2,1,0:T(8,128)(2,1)} collective-permute-done((bf16[2,160,960]{2,1,0:T(8,128)(2,1)}, bf16[2,160,960]{2,1,0:T(8,128)(2,1)}, u32[]{:S(2)}, u32[]{:S(2)}) %collective-permute-start.11) | collective-permute-done | bytes 614432 | tf_op jit(solution)/shard_map/ppermute | solution.py:413
  169.8 59.8 %all-gather.4.cloned.1.call-done = bf16[2560,1920]{1,0:T(8,128)(2,1)} async-done(((bf16[320,1920]{1,0:T(8,128)(2,1)}), bf16[2560,1920]{1,0:T(8,128)(2,1)}) %all-gather.4.cloned.1.call-update) | async-done | bytes 9830416 | tf_op jit(solution)/shard_map/all_gather | solution.py:508
  229.6 6.5 fusion.2
  243.0 7.6 collective-permute-done.13.refs_1_
  251.3 13.7 %collective-permute-done.10 = bf16[256,1280]{1,0:T(8,128)(2,1)S(1)} collective-permute-done((bf16[256,1280]{1,0:T(8,128)(2,1)S(1)}, bf16[256,1280]{1,0:T(8,128)(2,1)S(1)}, u32[]{:S(2)}, u32[]{:S(2)}) %collective-permute-start.10) | collective-permute-done | bytes 655392 | tf_op jit(solution)/shard_map/ppermute | solution.py:410
  267.2 6.0 shard_map.301
  281.0 9.2 collective-permute-done.16
  291.3 4.4 fusion.6
  300.3 25.0 %collective-permute-start.20 = (bf16[128,2560]{1,0:T(8,128)(2,1)}, bf16[128,2560]{1,0:T(8,128)(2,1)}, u32[]{:S(2)}, u32[]{:S(2)}) collective-permute-start(bf16[128,2560]{1,0:T(8,128)(2,1)} %shard_map.302), channel_id=1, source_target_pairs={{0,16},{2,18},{4,20},{6,22},{8,24},{10,26},{12,28},{14,30},{16,0},... | collective-permute-start | bytes 1966088 | tf_op jit(solution)/shard_map/ppermute | solution.py:413
  330.4 14.2 %all-gather.6.cloned.1.call-done.gate.up.refs_0_.refs_1_ = bf16[4,2,4,160,960]{4,3,2,1,0:T(8,128)(2,1)} async-done(((bf16[1,2,4,160,960]{4,3,2,1,0:T(8,128)(2,1)}), bf16[4,2,4,160,960]{4,3,2,1,0:T(8,128)(2,1)}) %all-gather.6.cloned.1.call-update) | async-done | bytes 9830416 | tf_op jit(solution)/shard_map/all_gather | solution.py:517
  351.0 14.3 %collective-permute-done.19 = bf16[128,2560]{1,0:T(8,128)(2,1)S(1)} collective-permute-done((bf16[128,2560]{1,0:T(8,128)(2,1)S(1)}, bf16[128,2560]{1,0:T(8,128)(2,1)S(1)}, u32[]{:S(2)}, u32[]{:S(2)}) %collective-permute-start.19) | collective-permute-done | bytes 655392 | tf_op jit(solution)/shard_map/ppermute | solution.py:410
  365.6 3.3 collective-permute-done.20
  369.6 13.4 %collective-permute-start.23 = (bf16[128,2560]{1,0:T(8,128)(2,1)S(1)}, bf16[128,2560]{1,0:T(8,128)(2,1)S(1)}, u32[]{:S(2)}, u32[]{:S(2)}) collective-permute-start(bf16[128,2560]{1,0:T(8,128)(2,1)S(1)} %shard_map.303), channel_id=1, source_target_pairs={{0,16},{2,18},{4,20},{6,22},{8,24},{10,26},{12,28},{14,30},{16,0},... | collective-permute-start | bytes 1966088 | tf_op jit(solution)/shard_map/ppermute | solution.py:413
  386.8 7.7 collective-permute-done.24
  394.5 42.0 %collective-permute-done.23 = bf16[128,2560]{1,0:T(8,128)(2,1)S(1)} collective-permute-done((bf16[128,2560]{1,0:T(8,128)(2,1)S(1)}, bf16[128,2560]{1,0:T(8,128)(2,1)S(1)}, u32[]{:S(2)}, u32[]{:S(2)}) %collective-permute-start.23) | collective-permute-done | bytes 655392 | tf_op jit(solution)/shard_map/ppermute | solution.py:413
  441.4 5.5 shard_map.308.grad
  448.3 11.9 %shard_map.309 = (bf16[512,960]{1,0:T(8,128)(2,1)}, bf16[2,512,960]{2,1,0:T(8,128)(2,1)}) custom-call(bf16[512,2560]{1,0:T(8,128)(2,1)} %collective-permute-done.25.act.refs_1_, f32[512,960]{1,0:T(8,128)} %copy-done.18, bf16[4,2,4,160,960]{4,3,2,1,0:T(8,128)(2,1)} %all-gather.6.cloned.1.call-done.gate.up.refs_0_.refs_1_, ...), custom_call_target="tpu_custom_call" | custom-call | tf_op jit(solution)/shard_map/pallas_call | solution.py:316
  460.2 7.1 shard_map.310
  467.8 5.5 shard_map.305.grad
  474.6 11.9 %shard_map.306 = (bf16[512,960]{1,0:T(8,128)(2,1)}, bf16[2,512,960]{2,1,0:T(8,128)(2,1)}) custom-call(bf16[512,2560]{1,0:T(8,128)(2,1)} %pad_maximum_fusion.1.act.refs_0_, f32[512,960]{1,0:T(8,128)} %copy-done.19, bf16[4,2,4,160,960]{4,3,2,1,0:T(8,128)(2,1)} %all-gather.6.cloned.1.call-done.gate.up.refs_0_.refs_1_, ...), custom_call_target="tpu_custom_call" | custom-call | tf_op jit(solution)/shard_map/pallas_call | solution.py:316
  486.5 7.4 shard_map.307
  493.9 4.1 convert_add_fusion.1
  502.9 15.9 %shard_map.312.refs_4_ = bf16[4,3,4,160,960]{4,3,2,1,0:T(8,128)(2,1)} custom-call(bf16[512,2560]{1,0:T(8,128)(2,1)} %pad_maximum_fusion.1.act.refs_0_, bf16[512,2560]{1,0:T(8,128)(2,1)} %collective-permute-done.25.act.refs_1_, bf16[2,512,960]{2,1,0:T(8,128)(2,1)S(1)} %copy-done.16, bf16[2,512,960]{2,1,0:T(8,128)(2,1)S(1)} %copy-done.17), custom_call_target="tpu_custom_call" | custom-call | tf_op jit(solution)/shard_map/pallas_call | solution.py:372
  518.8 8.6 shard_map.313
  527.5 17.0 %collective-permute-done.28 = bf16[128,2560]{1,0:T(8,128)(2,1)} collective-permute-done((bf16[128,2560]{1,0:T(8,128)(2,1)}, bf16[128,2560]{1,0:T(8,128)(2,1)}, u32[]{:S(2)}, u32[]{:S(2)}) %collective-permute-start.28) | collective-permute-done | bytes 655392 | tf_op jit(solution)/shard_map/ppermute | solution.py:413
  544.5 11.8 %shard_map.315 = bf16[512,2560]{1,0:T(8,128)(2,1)} custom-call(bf16[2,512,960]{2,1,0:T(8,128)(2,1)} %get-tuple-element.113.refs_3_.acts, bf16[4,2,4,160,960]{4,3,2,1,0:T(8,128)(2,1)} %all-gather.6.cloned.1.call-done.gate.up.refs_0_.refs_1_, bf16[4,2,4,160,960]{4,3,2,1,0:T(8,128)(2,1)} %all-gather.6.cloned.1.call-done.gate.up.refs_0_.refs_1_), custom_call_target="tpu_custom_call" | custom-call | tf_op jit(solution)/shard_map/pallas_call | solution.py:344
  558.9 12.2 %shard_map.314 = f32[512,2560]{1,0:T(8,128)} custom-call(bf16[2,512,960]{2,1,0:T(8,128)(2,1)} %get-tuple-element.112.refs_2_.acts, bf16[4,2,4,160,960]{4,3,2,1,0:T(8,128)(2,1)} %all-gather.6.cloned.1.call-done.gate.up.refs_0_.refs_1_, bf16[4,2,4,160,960]{4,3,2,1,0:T(8,128)(2,1)} %all-gather.6.cloned.1.call-done.gate.up.refs_0_.refs_1_), custom_call_target="tpu_custom_call" | custom-call | tf_op jit(solution)/shard_map/pallas_call | solution.py:344
  571.1 3.7 convert_add_fusion
  579.6 51.6 %collective-permute-done.29 = bf16[128,2560]{1,0:T(8,128)(2,1)S(1)} collective-permute-done((bf16[128,2560]{1,0:T(8,128)(2,1)}, bf16[128,2560]{1,0:T(8,128)(2,1)S(1)}, u32[]{:S(2)}, u32[]{:S(2)}) %collective-permute-start.29) | collective-permute-done | bytes 655392 | tf_op jit(solution)/shard_map/ppermute | solution.py:413
  631.2 14.0 %collective-permute-done.33 = bf16[128,2560]{1,0:T(8,128)(2,1)S(1)} collective-permute-done((bf16[128,2560]{1,0:T(8,128)(2,1)S(1)}, bf16[128,2560]{1,0:T(8,128)(2,1)S(1)}, u32[]{:S(2)}, u32[]{:S(2)}) %collective-permute-start.33) | collective-permute-done | bytes 655392 | tf_op jit(solution)/shard_map/ppermute | solution.py:413
  649.7 30.3 %collective-permute-done.35 = bf16[128,2560]{1,0:T(8,128)(2,1)S(1)} collective-permute-done((bf16[128,2560]{1,0:T(8,128)(2,1)S(1)}, bf16[128,2560]{1,0:T(8,128)(2,1)S(1)}, u32[]{:S(2)}, u32[]{:S(2)}) %collective-permute-start.35) | collective-permute-done | bytes 655392 | tf_op jit(solution)/shard_map/ppermute | solution.py:410
  681.7 3.4 collective-permute-done.36
  689.7 3.9 dynamic-slice_bitcast_fusion.2
  693.6 5.0 collective-permute-start.38
  698.6 4.1 fusion.4
  703.4 8.9 collective-permute-done.37
  712.5 10.0 %collective-permute-done.38.refs_4_ = bf16[3,160,960]{2,1,0:T(8,128)(2,1)S(1)} collective-permute-done((bf16[3,160,960]{2,1,0:T(8,128)(2,1)S(1)}, bf16[3,160,960]{2,1,0:T(8,128)(2,1)S(1)}, u32[]{:S(2)}, u32[]{:S(2)}) %collective-permute-start.38) | collective-permute-done | bytes 921632 | tf_op jit(solution)/shard_map/ppermute | solution.py:413
  724.6 4.2 shard_map.319.refs_2_
  728.8 4.0 collective-permute-done.40
  732.8 4.2 shard_map.320
  748.6 8.4 shard_map.317
  772.3 5.7 fusion
  778.0 13.3 %collective-permute-done.52 = bf16[4,2,48,1280]{3,2,1,0:T(8,128)(2,1)S(1)} collective-permute-done((bf16[4,2,48,1280]{3,2,1,0:T(8,128)(2,1)S(1)}, bf16[4,2,48,1280]{3,2,1,0:T(8,128)(2,1)S(1)}, u32[]{:S(2)}, u32[]{:S(2)}) %collective-permute-start.52) | collective-permute-done | bytes 983072 | tf_op jit(solution)/shard_map/ppermute | solution.py:410
  793.4 4.7 shard_map.318
  798.1 3.9 dynamic-slice_bitcast_fusion
  803.3 4.0 collective-permute-start.56
  807.3 3.3 fusion.10
  810.6 8.5 collective-permute-done.54
  819.3 4.2 collective-permute-done.56
  825.0 26.4 %collective-permute-done.55 = bf16[48,1280]{1,0:T(8,128)(2,1)S(1)} collective-permute-done((bf16[48,1280]{1,0:T(8,128)(2,1)S(1)}, bf16[48,1280]{1,0:T(8,128)(2,1)S(1)}, u32[]{:S(2)}, u32[]{:S(2)}) %collective-permute-start.55) | collective-permute-done | bytes 122912 | tf_op jit(solution)/shard_map/ppermute | solution.py:413
  858.2 13.6 %collective-permute-done.44.refs_5_ = bf16[3,160,960]{2,1,0:T(8,128)(2,1)S(1)} collective-permute-done((bf16[3,160,960]{2,1,0:T(8,128)(2,1)}, bf16[3,160,960]{2,1,0:T(8,128)(2,1)S(1)}, u32[]{:S(2)}, u32[]{:S(2)}) %collective-permute-start.44) | collective-permute-done | bytes 921632 | tf_op jit(solution)/shard_map/ppermute | solution.py:413
  880.9 3.4 fusion.19
  884.3 10.3 %collective-permute-done.48 = bf16[2,160,640]{2,1,0:T(8,128)(2,1)S(1)} collective-permute-done((bf16[2,160,640]{2,1,0:T(8,128)(2,1)S(1)}, bf16[2,160,640]{2,1,0:T(8,128)(2,1)S(1)}, u32[]{:S(2)}, u32[]{:S(2)}) %collective-permute-start.48) | collective-permute-done | bytes 409632 | tf_op jit(solution)/shard_map/ppermute | solution.py:413
  894.6 42.6 %collective-permute-done.47 = bf16[2,160,640]{2,1,0:T(8,128)(2,1)S(1)} collective-permute-done((bf16[2,160,640]{2,1,0:T(8,128)(2,1)S(1)}, bf16[2,160,640]{2,1,0:T(8,128)(2,1)S(1)}, u32[]{:S(2)}, u32[]{:S(2)}) %collective-permute-start.47) | collective-permute-done | bytes 409632 | tf_op jit(solution)/shard_map/ppermute | solution.py:413
  939.0 6.5 shard_map.321
  949.3 3.5 collective-permute-done.50
  (436 shorter events, 171.3 us)
Async XLA Ops:
  7.2 222.3 %all-gather.4.cloned.1.call-start = ((), (), s32[]{:S(2)}) async-start(), calls=%async_computation.2 | async-start | bytes 11059200 | tf_op jit(solution)/shard_map/all_gather | solution.py:508
  9.8 16.9 %collective-permute-start.7 = (bf16[160,1920]{1,0:T(8,128)(2,1)S(1)}, bf16[160,1920]{1,0:T(8,128)(2,1)S(1)}, u32[]{:S(2)}, u32[]{:S(2)}) collective-permute-start(bf16[160,1920]{1,0:T(8,128)(2,1)S(1)} %get-tuple-element.204), channel_id=1, source_target_pairs={{0,2},{2,0},{4,6},{6,4},{8,10},{10,8},{12,14},{14,12},{16,18},{18,... | collective-permute-start | bytes 1843208 | tf_op jit(solution)/shard_map/ppermute | solution.py:410
  30.2 314.4 %all-gather.6.cloned.1.call-start = ((), (), s32[]{:S(2)}) async-start(), calls=%async_computation.3 | async-start | bytes 13107200 | tf_op jit(solution)/shard_map/all_gather | solution.py:517
  32.7 24.4 %collective-permute-start = (bf16[2,160,960]{2,1,0:T(8,128)(2,1)S(1)}, bf16[2,160,960]{2,1,0:T(8,128)(2,1)S(1)}, u32[]{:S(2)}, u32[]{:S(2)}) collective-permute-start(bf16[2,160,960]{2,1,0:T(8,128)(2,1)S(1)} %get-tuple-element.79), channel_id=1, source_target_pairs={{0,8},{2,10},{4,12},{6,14},{8,16},{10,18},{12,20},{14,22},{16,24},... | collective-permute-start | bytes 1843208 | tf_op jit(solution)/shard_map/ppermute | solution.py:413
  34.8 67.5 %copy-start.13 = (bf16[128,2560]{1,0:T(8,128)(2,1)S(1)}, bf16[128,2560]{1,0:T(8,128)(2,1)}, u32[]{:S(2)}) copy-start(bf16[128,2560]{1,0:T(8,128)(2,1)} %refs_0_.4) | copy-start | bytes 1966084
  57.1 20.3 %collective-permute-start.3 = (bf16[1,48,1280]{2,1,0:T(8,128)(2,1)S(1)}, bf16[1,48,1280]{2,1,0:T(8,128)(2,1)S(1)}, u32[]{:S(2)}, u32[]{:S(2)}) collective-permute-start(bf16[1,48,1280]{2,1,0:T(8,128)(2,1)S(1)} %fusion.51.refs_0_), channel_id=1, source_target_pairs={{0,24},{2,26},{4,28},{6,30},{8,0},{10,2},{12,4},{14,6},{16,8},{18,... | collective-permute-start | bytes 368648 | tf_op jit(solution)/shard_map/ppermute | solution.py:413
  70.7 20.4 %collective-permute-start.2 = (bf16[1,48,1280]{2,1,0:T(8,128)(2,1)S(1)}, bf16[1,48,1280]{2,1,0:T(8,128)(2,1)S(1)}, u32[]{:S(2)}, u32[]{:S(2)}) collective-permute-start(bf16[1,48,1280]{2,1,0:T(8,128)(2,1)S(1)} %fusion.51.refs_0_), channel_id=1, source_target_pairs={{0,16},{2,18},{4,20},{6,22},{8,24},{10,26},{12,28},{14,30},{16,0},... | collective-permute-start | bytes 368648 | tf_op jit(solution)/shard_map/ppermute | solution.py:413
  72.2 18.9 %collective-permute-start.1 = (bf16[1,48,1280]{2,1,0:T(8,128)(2,1)S(1)}, bf16[1,48,1280]{2,1,0:T(8,128)(2,1)S(1)}, u32[]{:S(2)}, u32[]{:S(2)}) collective-permute-start(bf16[1,48,1280]{2,1,0:T(8,128)(2,1)S(1)} %fusion.51.refs_0_), channel_id=1, source_target_pairs={{0,8},{2,10},{4,12},{6,14},{8,16},{10,18},{12,20},{14,22},{16,24},... | collective-permute-start | bytes 368648 | tf_op jit(solution)/shard_map/ppermute | solution.py:413
  91.1 8.9 collective-permute-start.4
  101.1 22.0 %collective-permute-start.5 = (bf16[2,4,48,1280]{3,2,1,0:T(8,128)(2,1)}, bf16[2,4,48,1280]{3,2,1,0:T(8,128)(2,1)}, u32[]{:S(2)}, u32[]{:S(2)}) collective-permute-start(bf16[2,4,48,1280]{3,2,1,0:T(8,128)(2,1)} %maximum_select_fusion.7), channel_id=1, source_target_pairs={{0,2},{2,0},{4,6},{6,4},{8,10},{10,8},{12,14},{14,12},{16,18},{18,... | collective-permute-start | bytes 2949128 | tf_op jit(solution)/shard_map/ppermute | solution.py:410
  102.2 20.9 %collective-permute-start.8 = (bf16[128,2560]{1,0:T(8,128)(2,1)S(1)}, bf16[128,2560]{1,0:T(8,128)(2,1)S(1)}, u32[]{:S(2)}, u32[]{:S(2)}) collective-permute-start(bf16[128,2560]{1,0:T(8,128)(2,1)S(1)} %copy-done.13), channel_id=1, source_target_pairs={{0,2},{2,0},{4,6},{6,4},{8,10},{10,8},{12,14},{14,12},{16,18},{18,... | collective-permute-start | bytes 1966088 | tf_op jit(solution)/shard_map/ppermute | solution.py:410
  103.2 31.7 %collective-permute-start.6 = (bf16[128,2560]{1,0:T(8,128)(2,1)S(1)}, bf16[128,2560]{1,0:T(8,128)(2,1)S(1)}, u32[]{:S(2)}, u32[]{:S(2)}) collective-permute-start(bf16[128,2560]{1,0:T(8,128)(2,1)S(1)} %copy-done.13), channel_id=1, source_target_pairs={{0,1},{1,0},{2,3},{3,2},{4,5},{5,4},{6,7},{7,6},{8,9},{9,8},{10,11... | collective-permute-start | bytes 1966088 | tf_op jit(solution)/shard_map/ppermute | solution.py:408
  103.2 63.5 %collective-permute-start.11 = (bf16[2,160,960]{2,1,0:T(8,128)(2,1)}, bf16[2,160,960]{2,1,0:T(8,128)(2,1)}, u32[]{:S(2)}, u32[]{:S(2)}) collective-permute-start(bf16[2,160,960]{2,1,0:T(8,128)(2,1)} %get-tuple-element.87), channel_id=1, source_target_pairs={{0,16},{2,18},{4,20},{6,22},{8,24},{10,26},{12,28},{14,30},{16,0},... | collective-permute-start | bytes 1843208 | tf_op jit(solution)/shard_map/ppermute | solution.py:413
  106.5 60.2 %collective-permute-start.12 = (bf16[2,160,960]{2,1,0:T(8,128)(2,1)}, bf16[2,160,960]{2,1,0:T(8,128)(2,1)}, u32[]{:S(2)}, u32[]{:S(2)}) collective-permute-start(bf16[2,160,960]{2,1,0:T(8,128)(2,1)} %get-tuple-element.88), channel_id=1, source_target_pairs={{0,24},{2,26},{4,28},{6,30},{8,0},{10,2},{12,4},{14,6},{16,8},{18,... | collective-permute-start | bytes 1843208 | tf_op jit(solution)/shard_map/ppermute | solution.py:413
  123.2 12.5 %collective-permute-start.9 = (bf16[128,2560]{1,0:T(8,128)(2,1)S(1)}, bf16[128,2560]{1,0:T(8,128)(2,1)S(1)}, u32[]{:S(2)}, u32[]{:S(2)}) collective-permute-start(bf16[128,2560]{1,0:T(8,128)(2,1)S(1)} %collective-permute-done.8.refs_2_), channel_id=1, source_target_pairs={{0,1},{1,0},{2,3},{3,2},{4,5},{5,4},{6,7},{7,6},{8,9},{9,8},{10,11... | collective-permute-start | bytes 1966088 | tf_op jit(solution)/shard_map/ppermute | solution.py:408
  229.6 210.1 %all-gather.8.cloned.1.call-start = ((), (), s32[]{:S(2)}) async-start(), calls=%async_computation.4 | async-start | bytes 6553600 | tf_op jit(solution)/shard_map/all_gather | solution.py:517
  236.2 28.8 %collective-permute-start.10 = (bf16[256,1280]{1,0:T(8,128)(2,1)S(1)}, bf16[256,1280]{1,0:T(8,128)(2,1)S(1)}, u32[]{:S(2)}, u32[]{:S(2)}) collective-permute-start(bf16[256,1280]{1,0:T(8,128)(2,1)S(1)} %slice.394), channel_id=1, source_target_pairs={{0,2},{2,0},{4,6},{6,4},{8,10},{10,8},{12,14},{14,12},{16,18},{18,... | collective-permute-start | bytes 1966088 | tf_op jit(solution)/shard_map/ppermute | solution.py:410
  238.0 12.6 %collective-permute-start.13 = (bf16[1,160,960]{2,1,0:T(8,128)(2,1)S(1)}, bf16[1,160,960]{2,1,0:T(8,128)(2,1)S(1)}, u32[]{:S(2)}, u32[]{:S(2)}) collective-permute-start(bf16[1,160,960]{2,1,0:T(8,128)(2,1)S(1)} %get-tuple-element.93), channel_id=1, source_target_pairs={{0,8},{2,10},{4,12},{6,14},{8,16},{10,18},{12,20},{14,22},{16,24},... | collective-permute-start | bytes 921608 | tf_op jit(solution)/shard_map/ppermute | solution.py:413
  238.1 27.0 %collective-permute-start.14 = (bf16[1,160,960]{2,1,0:T(8,128)(2,1)S(1)}, bf16[1,160,960]{2,1,0:T(8,128)(2,1)S(1)}, u32[]{:S(2)}, u32[]{:S(2)}) collective-permute-start(bf16[1,160,960]{2,1,0:T(8,128)(2,1)S(1)} %get-tuple-element.94), channel_id=1, source_target_pairs={{0,16},{2,18},{4,20},{6,22},{8,24},{10,26},{12,28},{14,30},{16,0},... | collective-permute-start | bytes 921608 | tf_op jit(solution)/shard_map/ppermute | solution.py:413
  239.0 26.2 %collective-permute-start.15 = (bf16[1,160,960]{2,1,0:T(8,128)(2,1)S(1)}, bf16[1,160,960]{2,1,0:T(8,128)(2,1)S(1)}, u32[]{:S(2)}, u32[]{:S(2)}) collective-permute-start(bf16[1,160,960]{2,1,0:T(8,128)(2,1)S(1)} %get-tuple-element.95), channel_id=1, source_target_pairs={{0,24},{2,26},{4,28},{6,30},{8,0},{10,2},{12,4},{14,6},{16,8},{18,... | collective-permute-start | bytes 921608 | tf_op jit(solution)/shard_map/ppermute | solution.py:413
  250.6 40.7 %collective-permute-start.17 = (bf16[128,2560]{1,0:T(8,128)(2,1)}, bf16[128,2560]{1,0:T(8,128)(2,1)}, u32[]{:S(2)}, u32[]{:S(2)}) collective-permute-start(bf16[128,2560]{1,0:T(8,128)(2,1)} %shard_map.302), channel_id=1, source_target_pairs={{0,8},{2,10},{4,12},{6,14},{8,16},{10,18},{12,20},{14,22},{16,24},... | collective-permute-start | bytes 1966088 | tf_op jit(solution)/shard_map/ppermute | solution.py:413
  278.5 11.6 %collective-permute-start.16 = (bf16[256,640]{1,0:T(8,128)(2,1)}, bf16[256,640]{1,0:T(8,128)(2,1)}, u32[]{:S(2)}, u32[]{:S(2)}) collective-permute-start(bf16[256,640]{1,0:T(8,128)(2,1)} %get-tuple-element.215), channel_id=1, source_target_pairs={{0,2},{2,0},{4,6},{6,4},{8,10},{10,8},{12,14},{14,12},{16,18},{18,... | collective-permute-start | bytes 983048 | tf_op jit(solution)/shard_map/ppermute | solution.py:410
  299.3 45.4 %collective-permute-start.18 = (bf16[2,128,2560]{2,1,0:T(8,128)(2,1)}, bf16[2,128,2560]{2,1,0:T(8,128)(2,1)}, u32[]{:S(2)}, u32[]{:S(2)}) collective-permute-start(bf16[2,128,2560]{2,1,0:T(8,128)(2,1)} %fusion.22), channel_id=1, source_target_pairs={{0,1},{1,0},{2,3},{3,2},{4,5},{5,4},{6,7},{7,6},{8,9},{9,8},{10,11... | collective-permute-start | bytes 3932168 | tf_op jit(solution)/shard_map/ppermute | solution.py:408
  299.3 66.2 %collective-permute-start.21 = (bf16[128,2560]{1,0:T(8,128)(2,1)}, bf16[128,2560]{1,0:T(8,128)(2,1)}, u32[]{:S(2)}, u32[]{:S(2)}) collective-permute-start(bf16[128,2560]{1,0:T(8,128)(2,1)} %shard_map.302), channel_id=1, source_target_pairs={{0,24},{2,26},{4,28},{6,30},{8,0},{10,2},{12,4},{14,6},{16,8},{18,... | collective-permute-start | bytes 1966088 | tf_op jit(solution)/shard_map/ppermute | solution.py:413
  300.3 68.6 %collective-permute-start.20 = (bf16[128,2560]{1,0:T(8,128)(2,1)}, bf16[128,2560]{1,0:T(8,128)(2,1)}, u32[]{:S(2)}, u32[]{:S(2)}) collective-permute-start(bf16[128,2560]{1,0:T(8,128)(2,1)} %shard_map.302), channel_id=1, source_target_pairs={{0,16},{2,18},{4,20},{6,22},{8,24},{10,26},{12,28},{14,30},{16,0},... | collective-permute-start | bytes 1966088 | tf_op jit(solution)/shard_map/ppermute | solution.py:413
  344.6 345.1 %reduce-scatter.7.cloned.1.call-start = ((), (), s32[]{:S(2)}) async-start(), calls=%async_computation.6 | async-start | bytes 19660800
  347.2 18.1 %collective-permute-start.19 = (bf16[128,2560]{1,0:T(8,128)(2,1)S(1)}, bf16[128,2560]{1,0:T(8,128)(2,1)S(1)}, u32[]{:S(2)}, u32[]{:S(2)}) collective-permute-start(bf16[128,2560]{1,0:T(8,128)(2,1)S(1)} %fusion.41), channel_id=1, source_target_pairs={{0,2},{2,0},{4,6},{6,4},{8,10},{10,8},{12,14},{14,12},{16,18},{18,... | collective-permute-start | bytes 1966088 | tf_op jit(solution)/shard_map/ppermute | solution.py:410
  369.5 25.0 %collective-permute-start.24 = (bf16[128,2560]{1,0:T(8,128)(2,1)S(1)}, bf16[128,2560]{1,0:T(8,128)(2,1)S(1)}, u32[]{:S(2)}, u32[]{:S(2)}) collective-permute-start(bf16[128,2560]{1,0:T(8,128)(2,1)S(1)} %shard_map.303), channel_id=1, source_target_pairs={{0,24},{2,26},{4,28},{6,30},{8,0},{10,2},{12,4},{14,6},{16,8},{18,... | collective-permute-start | bytes 1966088 | tf_op jit(solution)/shard_map/ppermute | solution.py:413
  369.6 66.9 %collective-permute-start.23 = (bf16[128,2560]{1,0:T(8,128)(2,1)S(1)}, bf16[128,2560]{1,0:T(8,128)(2,1)S(1)}, u32[]{:S(2)}, u32[]{:S(2)}) collective-permute-start(bf16[128,2560]{1,0:T(8,128)(2,1)S(1)} %shard_map.303), channel_id=1, source_target_pairs={{0,16},{2,18},{4,20},{6,22},{8,24},{10,26},{12,28},{14,30},{16,0},... | collective-permute-start | bytes 1966088 | tf_op jit(solution)/shard_map/ppermute | solution.py:413
  383.0 53.5 %collective-permute-start.22 = (bf16[128,2560]{1,0:T(8,128)(2,1)S(1)}, bf16[128,2560]{1,0:T(8,128)(2,1)S(1)}, u32[]{:S(2)}, u32[]{:S(2)}) collective-permute-start(bf16[128,2560]{1,0:T(8,128)(2,1)S(1)} %shard_map.303), channel_id=1, source_target_pairs={{0,8},{2,10},{4,12},{6,14},{8,16},{10,18},{12,20},{14,22},{16,24},... | collective-permute-start | bytes 1966088 | tf_op jit(solution)/shard_map/ppermute | solution.py:413
  386.7 51.4 %collective-permute-start.26 = (bf16[512,2560]{1,0:T(8,128)(2,1)S(1)}, bf16[512,2560]{1,0:T(8,128)(2,1)S(1)}, u32[]{:S(2)}, u32[]{:S(2)}) collective-permute-start(bf16[512,2560]{1,0:T(8,128)(2,1)S(1)} %constant_dynamic-update-slice_fusion.act.refs_0_), channel_id=1, source_target_pairs={{0,1},{1,0},{2,3},{3,2},{4,5},{5,4},{6,7},{7,6},{8,9},{9,8},{10,11... | collective-permute-start | bytes 7864328 | tf_op jit(solution)/shard_map/ppermute | solution.py:408
  438.1 10.1 %collective-permute-start.25 = (bf16[512,2560]{1,0:T(8,128)(2,1)}, bf16[512,2560]{1,0:T(8,128)(2,1)}, u32[]{:S(2)}, u32[]{:S(2)}) collective-permute-start(bf16[512,2560]{1,0:T(8,128)(2,1)} %pad_maximum_fusion.1.act.refs_0_), channel_id=1, source_target_pairs={{0,1},{1,0},{2,3},{3,2},{4,5},{5,4},{6,7},{7,6},{8,9},{9,8},{10,11... | collective-permute-start | bytes 7864328 | tf_op jit(solution)/shard_map/ppermute | solution.py:408
  467.3 26.6 %collective-permute-start.27 = (bf16[512,2560]{1,0:T(8,128)(2,1)}, bf16[512,2560]{1,0:T(8,128)(2,1)}, u32[]{:S(2)}, u32[]{:S(2)}) collective-permute-start(bf16[512,2560]{1,0:T(8,128)(2,1)} %shard_map.310), channel_id=1, source_target_pairs={{0,1},{1,0},{2,3},{3,2},{4,5},{5,4},{6,7},{7,6},{8,9},{9,8},{10,11... | collective-permute-start | bytes 7864328 | tf_op jit(solution)/shard_map/ppermute | solution.py:408
  527.4 418.3 %reduce-scatter.5.cloned.1.call-start = ((), (), s32[]{:S(2)}) async-start(), calls=%async_computation.5 | async-start | bytes 7372800 | tf_op jit(solution)/shard_map/reduce_scatter | solution.py:628
  527.5 17.0 %collective-permute-start.28 = (bf16[128,2560]{1,0:T(8,128)(2,1)}, bf16[128,2560]{1,0:T(8,128)(2,1)}, u32[]{:S(2)}, u32[]{:S(2)}) collective-permute-start(bf16[128,2560]{1,0:T(8,128)(2,1)} %get-tuple-element.190), channel_id=1, source_target_pairs={{0,24},{2,26},{4,28},{6,30},{8,0},{10,2},{12,4},{14,6},{16,8},{18,... | collective-permute-start | bytes 1966088 | tf_op jit(solution)/shard_map/ppermute | solution.py:413
  556.3 14.8 %collective-permute-start.31 = (bf16[512,2560]{1,0:T(8,128)(2,1)}, bf16[512,2560]{1,0:T(8,128)(2,1)S(1)}, u32[]{:S(2)}, u32[]{:S(2)}) collective-permute-start(bf16[512,2560]{1,0:T(8,128)(2,1)} %shard_map.315), channel_id=1, source_target_pairs={{0,1},{1,0},{2,3},{3,2},{4,5},{5,4},{6,7},{7,6},{8,9},{9,8},{10,11... | collective-permute-start | bytes 7864328 | tf_op jit(solution)/shard_map/ppermute | solution.py:408
  556.3 23.3 %collective-permute-start.30 = (bf16[128,2560]{1,0:T(8,128)(2,1)}, bf16[128,2560]{1,0:T(8,128)(2,1)S(1)}, u32[]{:S(2)}, u32[]{:S(2)}) collective-permute-start(bf16[128,2560]{1,0:T(8,128)(2,1)} %get-tuple-element.191), channel_id=1, source_target_pairs={{0,8},{2,10},{4,12},{6,14},{8,16},{10,18},{12,20},{14,22},{16,24},... | collective-permute-start | bytes 1966088 | tf_op jit(solution)/shard_map/ppermute | solution.py:413
  556.3 74.9 %collective-permute-start.29 = (bf16[128,2560]{1,0:T(8,128)(2,1)}, bf16[128,2560]{1,0:T(8,128)(2,1)S(1)}, u32[]{:S(2)}, u32[]{:S(2)}) collective-permute-start(bf16[128,2560]{1,0:T(8,128)(2,1)} %get-tuple-element.192), channel_id=1, source_target_pairs={{0,16},{2,18},{4,20},{6,22},{8,24},{10,26},{12,28},{14,30},{16,0},... | collective-permute-start | bytes 1966088 | tf_op jit(solution)/shard_map/ppermute | solution.py:413
  575.3 55.9 %collective-permute-start.34 = (bf16[128,2560]{1,0:T(8,128)(2,1)S(1)}, bf16[128,2560]{1,0:T(8,128)(2,1)S(1)}, u32[]{:S(2)}, u32[]{:S(2)}) collective-permute-start(bf16[128,2560]{1,0:T(8,128)(2,1)S(1)} %get-tuple-element.187), channel_id=1, source_target_pairs={{0,8},{2,10},{4,12},{6,14},{8,16},{10,18},{12,20},{14,22},{16,24},... | collective-permute-start | bytes 1966088 | tf_op jit(solution)/shard_map/ppermute | solution.py:413
  577.1 68.2 %collective-permute-start.33 = (bf16[128,2560]{1,0:T(8,128)(2,1)S(1)}, bf16[128,2560]{1,0:T(8,128)(2,1)S(1)}, u32[]{:S(2)}, u32[]{:S(2)}) collective-permute-start(bf16[128,2560]{1,0:T(8,128)(2,1)S(1)} %get-tuple-element.188), channel_id=1, source_target_pairs={{0,16},{2,18},{4,20},{6,22},{8,24},{10,26},{12,28},{14,30},{16,0},... | collective-permute-start | bytes 1966088 | tf_op jit(solution)/shard_map/ppermute | solution.py:413
  577.1 68.2 %collective-permute-start.32 = (bf16[128,2560]{1,0:T(8,128)(2,1)S(1)}, bf16[128,2560]{1,0:T(8,128)(2,1)S(1)}, u32[]{:S(2)}, u32[]{:S(2)}) collective-permute-start(bf16[128,2560]{1,0:T(8,128)(2,1)S(1)} %get-tuple-element.189), channel_id=1, source_target_pairs={{0,24},{2,26},{4,28},{6,30},{8,0},{10,2},{12,4},{14,6},{16,8},{18,... | collective-permute-start | bytes 1966088 | tf_op jit(solution)/shard_map/ppermute | solution.py:413
  648.9 31.1 %collective-permute-start.35 = (bf16[128,2560]{1,0:T(8,128)(2,1)S(1)}, bf16[128,2560]{1,0:T(8,128)(2,1)S(1)}, u32[]{:S(2)}, u32[]{:S(2)}) collective-permute-start(bf16[128,2560]{1,0:T(8,128)(2,1)S(1)} %fusion.63), channel_id=1, source_target_pairs={{0,2},{2,0},{4,6},{6,4},{8,10},{10,8},{12,14},{14,12},{16,18},{18,... | collective-permute-start | bytes 1966088 | tf_op jit(solution)/shard_map/ppermute | solution.py:410
  681.7 3.4 collective-permute-start.36
  693.6 28.9 %collective-permute-start.38 = (bf16[3,160,960]{2,1,0:T(8,128)(2,1)S(1)}, bf16[3,160,960]{2,1,0:T(8,128)(2,1)S(1)}, u32[]{:S(2)}, u32[]{:S(2)}) collective-permute-start(bf16[3,160,960]{2,1,0:T(8,128)(2,1)S(1)} %get-tuple-element.183), channel_id=1, source_target_pairs={{0,8},{2,10},{4,12},{6,14},{8,16},{10,18},{12,20},{14,22},{16,24},... | collective-permute-start | bytes 2764808 | tf_op jit(solution)/shard_map/ppermute | solution.py:413
  702.7 9.5 collective-permute-start.37
  723.5 9.3 collective-permute-start.40
  761.6 10.7 %collective-permute-start.39 = (bf16[256,640]{1,0:T(8,128)(2,1)S(1)}, bf16[256,640]{1,0:T(8,128)(2,1)S(1)}, u32[]{:S(2)}, u32[]{:S(2)}) collective-permute-start(bf16[256,640]{1,0:T(8,128)(2,1)S(1)} %get-tuple-element.211), channel_id=1, source_target_pairs={{0,2},{2,0},{4,6},{6,4},{8,10},{10,8},{12,14},{14,12},{16,18},{18,... | collective-permute-start | bytes 983048 | tf_op jit(solution)/shard_map/ppermute | solution.py:410
  763.0 28.3 %collective-permute-start.52 = (bf16[4,2,48,1280]{3,2,1,0:T(8,128)(2,1)S(1)}, bf16[4,2,48,1280]{3,2,1,0:T(8,128)(2,1)S(1)}, u32[]{:S(2)}, u32[]{:S(2)}) collective-permute-start(bf16[4,2,48,1280]{3,2,1,0:T(8,128)(2,1)S(1)} %fusion.37), channel_id=1, source_target_pairs={{0,2},{2,0},{4,6},{6,4},{8,10},{10,8},{12,14},{14,12},{16,18},{18,... | collective-permute-start | bytes 2949128 | tf_op jit(solution)/shard_map/ppermute | solution.py:410
  767.7 90.5 %collective-permute-start.45 = (bf16[3,160,960]{2,1,0:T(8,128)(2,1)}, bf16[3,160,960]{2,1,0:T(8,128)(2,1)}, u32[]{:S(2)}, u32[]{:S(2)}) collective-permute-start(bf16[3,160,960]{2,1,0:T(8,128)(2,1)} %get-tuple-element.180), channel_id=1, source_target_pairs={{0,24},{2,26},{4,28},{6,30},{8,0},{10,2},{12,4},{14,6},{16,8},{18,... | collective-permute-start | bytes 2764808 | tf_op jit(solution)/shard_map/ppermute | solution.py:413
  791.6 11.4 %collective-permute-start.53 = (bf16[4,48,1280]{2,1,0:T(8,128)(2,1)S(1)}, bf16[4,48,1280]{2,1,0:T(8,128)(2,1)S(1)}, u32[]{:S(2)}, u32[]{:S(2)}) collective-permute-start(bf16[4,48,1280]{2,1,0:T(8,128)(2,1)S(1)} %fusion.43), channel_id=1, source_target_pairs={{0,4},{2,6},{4,0},{6,2},{8,12},{10,14},{12,8},{14,10},{16,20},{18,... | collective-permute-start | bytes 1474568 | tf_op jit(solution)/shard_map/ppermute | solution.py:410
  793.2 58.8 %collective-permute-start.41 = (bf16[2,128,2560]{2,1,0:T(8,128)(2,1)S(1)}, bf16[2,128,2560]{2,1,0:T(8,128)(2,1)S(1)}, u32[]{:S(2)}, u32[]{:S(2)}) collective-permute-start(bf16[2,128,2560]{2,1,0:T(8,128)(2,1)S(1)} %fusion.23), channel_id=1, source_target_pairs={{0,1},{1,0},{2,3},{3,2},{4,5},{5,4},{6,7},{7,6},{8,9},{9,8},{10,11... | collective-permute-start | bytes 3932168 | tf_op jit(solution)/shard_map/ppermute | solution.py:408
  803.2 15.9 %collective-permute-start.54 = (bf16[48,1280]{1,0:T(8,128)(2,1)S(1)}, bf16[48,1280]{1,0:T(8,128)(2,1)S(1)}, u32[]{:S(2)}, u32[]{:S(2)}) collective-permute-start(bf16[48,1280]{1,0:T(8,128)(2,1)S(1)} %get-tuple-element.205), channel_id=1, source_target_pairs={{0,8},{2,10},{4,12},{6,14},{8,16},{10,18},{12,20},{14,22},{16,24},... | collective-permute-start | bytes 368648 | tf_op jit(solution)/shard_map/ppermute | solution.py:413
  803.3 20.2 %collective-permute-start.56 = (bf16[48,1280]{1,0:T(8,128)(2,1)S(1)}, bf16[48,1280]{1,0:T(8,128)(2,1)S(1)}, u32[]{:S(2)}, u32[]{:S(2)}) collective-permute-start(bf16[48,1280]{1,0:T(8,128)(2,1)S(1)} %get-tuple-element.206), channel_id=1, source_target_pairs={{0,24},{2,26},{4,28},{6,30},{8,0},{10,2},{12,4},{14,6},{16,8},{18,... | collective-permute-start | bytes 368648 | tf_op jit(solution)/shard_map/ppermute | solution.py:413
  807.3 44.0 %collective-permute-start.55 = (bf16[48,1280]{1,0:T(8,128)(2,1)S(1)}, bf16[48,1280]{1,0:T(8,128)(2,1)S(1)}, u32[]{:S(2)}, u32[]{:S(2)}) collective-permute-start(bf16[48,1280]{1,0:T(8,128)(2,1)S(1)} %get-tuple-element.207), channel_id=1, source_target_pairs={{0,16},{2,18},{4,20},{6,22},{8,24},{10,26},{12,28},{14,30},{16,0},... | collective-permute-start | bytes 368648 | tf_op jit(solution)/shard_map/ppermute | solution.py:413
  819.1 52.8 %collective-permute-start.44 = (bf16[3,160,960]{2,1,0:T(8,128)(2,1)}, bf16[3,160,960]{2,1,0:T(8,128)(2,1)S(1)}, u32[]{:S(2)}, u32[]{:S(2)}) collective-permute-start(bf16[3,160,960]{2,1,0:T(8,128)(2,1)} %get-tuple-element.182), channel_id=1, source_target_pairs={{0,16},{2,18},{4,20},{6,22},{8,24},{10,26},{12,28},{14,30},{16,0},... | collective-permute-start | bytes 2764808 | tf_op jit(solution)/shard_map/ppermute | solution.py:413
  823.5 48.3 %collective-permute-start.43 = (bf16[4,2,160,640]{3,2,1,0:T(8,128)(2,1)}, bf16[4,2,160,640]{3,2,1,0:T(8,128)(2,1)}, u32[]{:S(2)}, u32[]{:S(2)}) collective-permute-start(bf16[4,2,160,640]{3,2,1,0:T(8,128)(2,1)} %fusion.10), channel_id=1, source_target_pairs={{0,4},{2,6},{4,0},{6,2},{8,12},{10,14},{12,8},{14,10},{16,20},{18,... | collective-permute-start | bytes 4915208 | tf_op jit(solution)/shard_map/ppermute | solution.py:410
  854.7 24.4 %collective-permute-start.42 = (bf16[128,2560]{1,0:T(8,128)(2,1)}, bf16[128,2560]{1,0:T(8,128)(2,1)}, u32[]{:S(2)}, u32[]{:S(2)}) collective-permute-start(bf16[128,2560]{1,0:T(8,128)(2,1)} %fusion.42), channel_id=1, source_target_pairs={{0,2},{2,0},{4,6},{6,4},{8,10},{10,8},{12,14},{14,12},{16,18},{18,... | collective-permute-start | bytes 1966088 | tf_op jit(solution)/shard_map/ppermute | solution.py:410
  875.1 19.5 %collective-permute-start.48 = (bf16[2,160,640]{2,1,0:T(8,128)(2,1)S(1)}, bf16[2,160,640]{2,1,0:T(8,128)(2,1)S(1)}, u32[]{:S(2)}, u32[]{:S(2)}) collective-permute-start(bf16[2,160,640]{2,1,0:T(8,128)(2,1)S(1)} %get-tuple-element.184), channel_id=1, source_target_pairs={{0,24},{2,26},{4,28},{6,30},{8,0},{10,2},{12,4},{14,6},{16,8},{18,... | collective-permute-start | bytes 1228808 | tf_op jit(solution)/shard_map/ppermute | solution.py:413
  876.7 60.5 %collective-permute-start.47 = (bf16[2,160,640]{2,1,0:T(8,128)(2,1)S(1)}, bf16[2,160,640]{2,1,0:T(8,128)(2,1)S(1)}, u32[]{:S(2)}, u32[]{:S(2)}) collective-permute-start(bf16[2,160,640]{2,1,0:T(8,128)(2,1)S(1)} %get-tuple-element.185), channel_id=1, source_target_pairs={{0,16},{2,18},{4,20},{6,22},{8,24},{10,26},{12,28},{14,30},{16,0},... | collective-permute-start | bytes 1228808 | tf_op jit(solution)/shard_map/ppermute | solution.py:413
  879.1 58.1 %collective-permute-start.46 = (bf16[2,160,640]{2,1,0:T(8,128)(2,1)S(1)}, bf16[2,160,640]{2,1,0:T(8,128)(2,1)S(1)}, u32[]{:S(2)}, u32[]{:S(2)}) collective-permute-start(bf16[2,160,640]{2,1,0:T(8,128)(2,1)S(1)} %get-tuple-element.186), channel_id=1, source_target_pairs={{0,8},{2,10},{4,12},{6,14},{8,16},{10,18},{12,20},{14,22},{16,24},... | collective-permute-start | bytes 1228808 | tf_op jit(solution)/shard_map/ppermute | solution.py:413
  937.4 8.2 collective-permute-start.49
  947.0 5.8 collective-permute-start.50
  948.4 6.6 collective-permute-start.57
  954.4 1.7 collective-permute-start.51
  (104 other events, 615.7 us)
Sparse Core Ops, SparseCore 0:
  30.2 199.2 all-gather.3
  231.4 113.1 all-gather.5
  347.0 72.5 all-gather.7
  527.6 157.6 reduce-scatter.6
  737.2 201.4 reduce-scatter.4

commit v4 on v3

--- a/solution.py
+++ b/solution.py
@@ -120,7 +120,7 @@
     gvec[...] = jnp.concatenate(sums, axis=0)
 
 
-def by_head(kernel, heads, length, block, kinds, outs):
+def by_head(kernel, heads, length, block, kinds, outs, flops=0):
     spec = {
         "r": pl.BlockSpec((length, block), lambda h: (0, h)),
         "g": pl.BlockSpec((1, block, block), lambda h: (h, 0, 0)),
@@ -134,6 +134,7 @@
         in_specs=[spec[k] for k in kinds],
         out_specs=[spec[k] for k, _ in outs],
         out_shape=[jax.ShapeDtypeStruct(sizes[k], d) for k, d in outs],
+        cost_estimate=pl.CostEstimate(flops=flops, bytes_accessed=0, transcendentals=0),
         compiler_params=pltpu.CompilerParams(vmem_limit_bytes=32 * 1024 * 1024),
     )
 
@@ -380,6 +381,7 @@
         ),
         out_shape=jax.ShapeDtypeStruct(full, dtype),
         input_output_aliases={} if into is None else {2 * p: 0},
+        cost_estimate=pl.CostEstimate(flops=20000000000, bytes_accessed=0, transcendentals=0),
         compiler_params=params(48),
     )(*acts, *grads, *([] if into is None else [into]))
 
@@ -545,7 +547,7 @@
         pre_x = whole_half(pre[0, :, :quarter], got[:, :quarter])
         pre_y = whole_half(pre[0, :, quarter:], got[:, quarter:])
         mixed, states, conv, rate, entry = by_head(
-            mixer_forward, heads, length, block, "rrggv", [("r", BF16)] + [("r", F32)] * 4
+            mixer_forward, heads, length, block, "rrggv", [("r", BF16)] + [("r", F32)] * 4, 30000000000
         )(pre_x, pre_y, full_gate_a, full_gate_in, per)
         mixed = after(to_rows(mixed), cot_line[1])
         branch_out = contract_last(mixed, full_out).reshape(2, 2, rows_each, width)
@@ -589,7 +591,7 @@
             return grid.shifts([take(k) for k in range(nz)])
 
         grad_ffn = lax.psum_scatter(
-            grad_ffn, "dp", scatter_dimension=0, tiled=True, axis_index_groups=grid.corners
+            after(grad_ffn, got_result[1]), "dp", scatter_dimension=0, tiled=True, axis_index_groups=grid.corners
         )
         grad_normed_two = total(after(got_two, *got_result[1:]))
         grad_ffn = ffn_send(grad_ffn[0], got_two[1])
@@ -639,6 +641,7 @@
             block,
             "rrrggvrrrr",
             [("r", BF16), ("w", F32), ("w", F32), ("v", F32)],
+            30000000000,
         )(grad_mixed, pre_x, pre_y, full_gate_a, full_gate_in, per, states, conv, rate, entry)
         grad_vec = jnp.concatenate([grad_vec[:7], grad_vec[7:] * jax.nn.sigmoid(decay_row)])
         grad_x_rows = to_rows(grad_pre_x)

time: 976 us -> 957 us (0.981)
  waiting for transfers between devices: 542 us -> 531 us
    ppermute x30, waiting for transfers between devices: 324 us -> 297 us  [shift(): lax.ppermute(value, 'dp', [(i, (i + 4 * by) % self.n) for i in range(self...]
    unnamed x6, waiting for transfers between devices: 0.08 us -> 10 us
    unnamed x216 -> x228, local copies, waits for them, and re-layouts: 54.7 us -> 49.7 us
  transfers between devices with their start and end apart: 63 -> 63, of which waited for: 35 -> 32; matrix products, arithmetic and copies ran while one was open for 9% -> 10% of each run, Pallas kernels for 9% -> 13%
where the time goes in v4:
time: 957 us; the launch traced here: 947 us
  waiting for transfers between devices  531 us (55%)
  Pallas kernels  141 us (15%)
  starting transfers between devices  107 us (11%)
  local copies, waits for them, and re-layouts  85.9 us (9%)
  other arithmetic  43.7 us (5%)
  matrix products  21.8 us (2%)
  between operations  15.8 us (2%)
    ppermute x30, waiting for transfers between devices, shift(): lax.ppermute(value, 'dp', [(i, (i + 4 * by) % self.n) for i in range(self...  297 us
    ppermute x18, waiting for transfers between devices, swap(): return lax.ppermute(value, 'dp', [(i, i ^ bit) for i in range(self.n)])  141 us
    ppermute x30, starting transfers between devices, shift(): lax.ppermute(value, 'dp', [(i, (i + 4 * by) % self.n) for i in range(self...  85.6 us
    all_gather x1, waiting for transfers between devices, run(): lax.all_gather(mine, 'dp', axis=0, tiled=True, axis_index_groups=grid.pla...  59.5 us
    unnamed x228, local copies, waits for them, and re-layouts  49.7 us
    pallas_call x4, Pallas kernels, ffn_collect(): pl.pallas_call(kernel, grid=(tokens // TILE,), in_specs=[pl.BlockSpec((n,...  38.4 us
    pallas_call x5, Pallas kernels, weight_grad(): pl.pallas_call(kernel, grid=(m, width // block // at_once), in_specs=[pl....  37.6 us
    pallas_call x2, Pallas kernels, ffn_middle(): pl.pallas_call(kernel, grid=(tokens // TILE,), in_specs=[rows_of(width),...  23.8 us
  transfers between devices with their start and end apart: 63, of which 32 were waited for; matrix products, arithmetic and copies ran while one was open for 10% of the time, Pallas kernels for 13%

profile of v4, /device:TPU:0, one launch (start us, length us, event | category | flops | bytes accessed | tf_op | source)
XLA Modules:
  0.0 946.7 jit_solution(13469620501843624018)
XLA Ops:
  12.8 13.9 %collective-permute-done.7 = bf16[160,1920]{1,0:T(8,128)(2,1)S(1)} collective-permute-done((bf16[160,1920]{1,0:T(8,128)(2,1)S(1)}, bf16[160,1920]{1,0:T(8,128)(2,1)S(1)}, u32[]{:S(2)}, u32[]{:S(2)}) %collective-permute-start.7) | collective-permute-done | bytes 614432 | tf_op jit(solution)/shard_map/ppermute | solution.py:412
  34.8 22.3 %collective-permute-done.refs_1_ = bf16[2,160,960]{2,1,0:T(8,128)(2,1)S(1)} collective-permute-done((bf16[2,160,960]{2,1,0:T(8,128)(2,1)S(1)}, bf16[2,160,960]{2,1,0:T(8,128)(2,1)S(1)}, u32[]{:S(2)}, u32[]{:S(2)}) %collective-permute-start) | collective-permute-done | bytes 614432 | tf_op jit(solution)/shard_map/ppermute | solution.py:415
  58.0 13.6 %collective-permute-start.3 = (bf16[1,48,1280]{2,1,0:T(8,128)(2,1)S(1)}, bf16[1,48,1280]{2,1,0:T(8,128)(2,1)S(1)}, u32[]{:S(2)}, u32[]{:S(2)}) collective-permute-start(bf16[1,48,1280]{2,1,0:T(8,128)(2,1)S(1)} %fusion.51.refs_0_), channel_id=1, source_target_pairs={{0,24},{2,26},{4,28},{6,30},{8,0},{10,2},{12,4},{14,6},{16,8},{18,... | collective-permute-start | bytes 368648 | tf_op jit(solution)/shard_map/ppermute | solution.py:415
  75.4 3.7 collective-permute-done.3.refs_3_
  79.1 14.0 %collective-permute-done.2.refs_2_ = bf16[1,48,1280]{2,1,0:T(8,128)(2,1)S(1)} collective-permute-done((bf16[1,48,1280]{2,1,0:T(8,128)(2,1)S(1)}, bf16[1,48,1280]{2,1,0:T(8,128)(2,1)S(1)}, u32[]{:S(2)}, u32[]{:S(2)}) %collective-permute-start.2) | collective-permute-done | bytes 122912 | tf_op jit(solution)/shard_map/ppermute | solution.py:415
  94.8 7.3 collective-permute-done.4
  107.9 16.7 %collective-permute-done.8.refs_2_ = bf16[128,2560]{1,0:T(8,128)(2,1)S(1)} collective-permute-done((bf16[128,2560]{1,0:T(8,128)(2,1)S(1)}, bf16[128,2560]{1,0:T(8,128)(2,1)S(1)}, u32[]{:S(2)}, u32[]{:S(2)}) %collective-permute-start.8) | collective-permute-done | bytes 655392 | tf_op jit(solution)/shard_map/ppermute | solution.py:412
  128.5 4.0 reshape.359
  141.6 26.0 %collective-permute-done.11.refs_2_ = bf16[2,160,960]{2,1,0:T(8,128)(2,1)} collective-permute-done((bf16[2,160,960]{2,1,0:T(8,128)(2,1)}, bf16[2,160,960]{2,1,0:T(8,128)(2,1)}, u32[]{:S(2)}, u32[]{:S(2)}) %collective-permute-start.11) | collective-permute-done | bytes 614432 | tf_op jit(solution)/shard_map/ppermute | solution.py:415
  167.6 3.0 shard_map.300
  170.6 59.5 %all-gather.4.cloned.1.call-done = bf16[2560,1920]{1,0:T(8,128)(2,1)} async-done(((bf16[320,1920]{1,0:T(8,128)(2,1)}), bf16[2560,1920]{1,0:T(8,128)(2,1)}) %all-gather.4.cloned.1.call-update) | async-done | bytes 9830416 | tf_op jit(solution)/shard_map/all_gather | solution.py:510
  230.2 6.5 fusion.2
  242.7 8.4 collective-permute-done.13.refs_1_
  251.9 13.1 %collective-permute-done.10 = bf16[256,1280]{1,0:T(8,128)(2,1)S(1)} collective-permute-done((bf16[256,1280]{1,0:T(8,128)(2,1)S(1)}, bf16[256,1280]{1,0:T(8,128)(2,1)S(1)}, u32[]{:S(2)}, u32[]{:S(2)}) %collective-permute-start.10) | collective-permute-done | bytes 655392 | tf_op jit(solution)/shard_map/ppermute | solution.py:412
  265.1 12.8 %collective-permute-done.14.refs_2_ = bf16[1,160,960]{2,1,0:T(8,128)(2,1)S(1)} collective-permute-done((bf16[1,160,960]{2,1,0:T(8,128)(2,1)S(1)}, bf16[1,160,960]{2,1,0:T(8,128)(2,1)S(1)}, u32[]{:S(2)}, u32[]{:S(2)}) %collective-permute-start.14) | collective-permute-done | bytes 307232 | tf_op jit(solution)/shard_map/ppermute | solution.py:415
  280.0 6.0 shard_map.301
  291.1 13.6 %collective-permute-done.16 = bf16[256,640]{1,0:T(8,128)(2,1)S(1)} collective-permute-done((bf16[256,640]{1,0:T(8,128)(2,1)}, bf16[256,640]{1,0:T(8,128)(2,1)S(1)}, u32[]{:S(2)}, u32[]{:S(2)}) %collective-permute-start.16) | collective-permute-done | bytes 327712 | tf_op jit(solution)/shard_map/ppermute | solution.py:412
  306.7 4.4 fusion.6
  314.7 10.8 %collective-permute-start.20 = (bf16[128,2560]{1,0:T(8,128)(2,1)S(1)}, bf16[128,2560]{1,0:T(8,128)(2,1)}, u32[]{:S(2)}, u32[]{:S(2)}) collective-permute-start(bf16[128,2560]{1,0:T(8,128)(2,1)S(1)} %shard_map.302), channel_id=1, source_target_pairs={{0,16},{2,18},{4,20},{6,22},{8,24},{10,26},{12,28},{14,30},{16,0},... | collective-permute-start | bytes 1966088 | tf_op jit(solution)/shard_map/ppermute | solution.py:415
  328.7 20.2 %all-gather.6.cloned.1.call-done.gate.up.refs_0_.refs_1_ = bf16[4,2,4,160,960]{4,3,2,1,0:T(8,128)(2,1)} async-done(((bf16[1,2,4,160,960]{4,3,2,1,0:T(8,128)(2,1)}), bf16[4,2,4,160,960]{4,3,2,1,0:T(8,128)(2,1)}) %all-gather.6.cloned.1.call-update) | async-done | bytes 9830416 | tf_op jit(solution)/shard_map/all_gather | solution.py:519
  353.1 19.3 %collective-permute-done.19 = bf16[128,2560]{1,0:T(8,128)(2,1)S(1)} collective-permute-done((bf16[128,2560]{1,0:T(8,128)(2,1)S(1)}, bf16[128,2560]{1,0:T(8,128)(2,1)S(1)}, u32[]{:S(2)}, u32[]{:S(2)}) %collective-permute-start.19) | collective-permute-done | bytes 655392 | tf_op jit(solution)/shard_map/ppermute | solution.py:412
  374.2 10.0 %collective-permute-start.23 = (bf16[128,2560]{1,0:T(8,128)(2,1)S(1)}, bf16[128,2560]{1,0:T(8,128)(2,1)S(1)}, u32[]{:S(2)}, u32[]{:S(2)}) collective-permute-start(bf16[128,2560]{1,0:T(8,128)(2,1)S(1)} %shard_map.303), channel_id=1, source_target_pairs={{0,16},{2,18},{4,20},{6,22},{8,24},{10,26},{12,28},{14,30},{16,0},... | collective-permute-start | bytes 1966088 | tf_op jit(solution)/shard_map/ppermute | solution.py:415
  388.0 7.7 collective-permute-done.24
  395.7 42.0 %collective-permute-done.23 = bf16[128,2560]{1,0:T(8,128)(2,1)S(1)} collective-permute-done((bf16[128,2560]{1,0:T(8,128)(2,1)S(1)}, bf16[128,2560]{1,0:T(8,128)(2,1)S(1)}, u32[]{:S(2)}, u32[]{:S(2)}) %collective-permute-start.23) | collective-permute-done | bytes 655392 | tf_op jit(solution)/shard_map/ppermute | solution.py:415
  442.6 5.5 shard_map.308.grad
  449.5 11.9 %shard_map.309 = (bf16[512,960]{1,0:T(8,128)(2,1)}, bf16[2,512,960]{2,1,0:T(8,128)(2,1)}) custom-call(bf16[512,2560]{1,0:T(8,128)(2,1)} %collective-permute-done.25.act.refs_1_, f32[512,960]{1,0:T(8,128)} %copy-done.2, bf16[4,2,4,160,960]{4,3,2,1,0:T(8,128)(2,1)} %all-gather.6.cloned.1.call-done.gate.up.refs_0_.refs_1_, ...), custom_call_target="tpu_custom_call" | custom-call | tf_op jit(solution)/shard_map/pallas_call | solution.py:317
  461.4 7.1 shard_map.310
  469.0 5.5 shard_map.305.grad
  475.8 11.9 %shard_map.306 = (bf16[512,960]{1,0:T(8,128)(2,1)}, bf16[2,512,960]{2,1,0:T(8,128)(2,1)}) custom-call(bf16[512,2560]{1,0:T(8,128)(2,1)} %pad_maximum_fusion.1.act.refs_0_, f32[512,960]{1,0:T(8,128)} %copy-done.3, bf16[4,2,4,160,960]{4,3,2,1,0:T(8,128)(2,1)} %all-gather.6.cloned.1.call-done.gate.up.refs_0_.refs_1_, ...), custom_call_target="tpu_custom_call" | custom-call | tf_op jit(solution)/shard_map/pallas_call | solution.py:317
  487.7 7.4 shard_map.307
  495.1 3.2 convert_add_fusion.1
  503.3 15.7 %shard_map.312.refs_4_ = bf16[4,3,4,160,960]{4,3,2,1,0:T(8,128)(2,1)} custom-call(bf16[512,2560]{1,0:T(8,128)(2,1)} %pad_maximum_fusion.1.act.refs_0_, bf16[512,2560]{1,0:T(8,128)(2,1)} %collective-permute-done.25.act.refs_1_, bf16[2,512,960]{2,1,0:T(8,128)(2,1)S(1)} %copy-done.24, bf16[2,512,960]{2,1,0:T(8,128)(2,1)S(1)} %copy-done.25), custom_call_target="tpu_custom_call" | custom-call | flops 20000000000 | tf_op jit(solution)/shard_map/pallas_call | solution.py:373
  519.1 8.6 shard_map.313
  528.5 12.0 %shard_map.315 = bf16[512,2560]{1,0:T(8,128)(2,1)} custom-call(bf16[2,512,960]{2,1,0:T(8,128)(2,1)} %get-tuple-element.114.refs_3_.acts, bf16[4,2,4,160,960]{4,3,2,1,0:T(8,128)(2,1)} %all-gather.6.cloned.1.call-done.gate.up.refs_0_.refs_1_, bf16[4,2,4,160,960]{4,3,2,1,0:T(8,128)(2,1)} %all-gather.6.cloned.1.call-done.gate.up.refs_0_.refs_1_), custom_call_target="tpu_custom_call" | custom-call | tf_op jit(solution)/shard_map/pallas_call | solution.py:345
  540.9 12.0 %shard_map.314 = f32[512,2560]{1,0:T(8,128)} custom-call(bf16[2,512,960]{2,1,0:T(8,128)(2,1)} %get-tuple-element.113.refs_2_.acts, bf16[4,2,4,160,960]{4,3,2,1,0:T(8,128)(2,1)} %all-gather.6.cloned.1.call-done.gate.up.refs_0_.refs_1_, bf16[4,2,4,160,960]{4,3,2,1,0:T(8,128)(2,1)} %all-gather.6.cloned.1.call-done.gate.up.refs_0_.refs_1_), custom_call_target="tpu_custom_call" | custom-call | tf_op jit(solution)/shard_map/pallas_call | solution.py:345
  552.9 3.2 convert_add_fusion
  556.6 4.6 collective-permute-start.34
  563.9 51.9 %collective-permute-done.29 = bf16[128,2560]{1,0:T(8,128)(2,1)S(1)} collective-permute-done((bf16[128,2560]{1,0:T(8,128)(2,1)}, bf16[128,2560]{1,0:T(8,128)(2,1)S(1)}, u32[]{:S(2)}, u32[]{:S(2)}) %collective-permute-start.29) | collective-permute-done | bytes 655392 | tf_op jit(solution)/shard_map/ppermute | solution.py:415
  615.8 14.0 %collective-permute-done.33 = bf16[128,2560]{1,0:T(8,128)(2,1)S(1)} collective-permute-done((bf16[128,2560]{1,0:T(8,128)(2,1)S(1)}, bf16[128,2560]{1,0:T(8,128)(2,1)S(1)}, u32[]{:S(2)}, u32[]{:S(2)}) %collective-permute-start.33) | collective-permute-done | bytes 655392 | tf_op jit(solution)/shard_map/ppermute | solution.py:415
  633.1 30.8 %collective-permute-done.35 = bf16[128,2560]{1,0:T(8,128)(2,1)S(1)} collective-permute-done((bf16[128,2560]{1,0:T(8,128)(2,1)S(1)}, bf16[128,2560]{1,0:T(8,128)(2,1)S(1)}, u32[]{:S(2)}, u32[]{:S(2)}) %collective-permute-start.35) | collective-permute-done | bytes 655392 | tf_op jit(solution)/shard_map/ppermute | solution.py:412
  665.7 3.3 collective-permute-done.36
  672.1 5.1 fusion.4
  678.8 9.9 %reduce-scatter.7.cloned.1.call-done = bf16[1,3,4,160,960]{4,3,2,1,0:T(8,128)(2,1)} async-done(((bf16[4,3,4,160,960]{4,3,2,1,0:T(8,128)(2,1)}), bf16[1,3,4,160,960]{4,3,2,1,0:T(8,128)(2,1)}) %reduce-scatter.7.cloned.1.call-update) | async-done | bytes 3686416
  688.7 3.9 dynamic-slice_bitcast_fusion.2
  692.6 4.6 collective-permute-start.38
  701.1 17.5 %collective-permute-done.38.refs_4_ = bf16[3,160,960]{2,1,0:T(8,128)(2,1)S(1)} collective-permute-done((bf16[3,160,960]{2,1,0:T(8,128)(2,1)S(1)}, bf16[3,160,960]{2,1,0:T(8,128)(2,1)S(1)}, u32[]{:S(2)}, u32[]{:S(2)}) %collective-permute-start.38) | collective-permute-done | bytes 921632 | tf_op jit(solution)/shard_map/ppermute | solution.py:415
  721.2 4.3 shard_map.319.refs_2_
  728.7 4.2 shard_map.320
  743.3 8.4 shard_map.317
  759.0 7.9 collective-permute-done.39
  766.9 5.8 fusion
  775.4 10.0 %collective-permute-done.52 = bf16[4,2,48,1280]{3,2,1,0:T(8,128)(2,1)S(1)} collective-permute-done((bf16[4,2,48,1280]{3,2,1,0:T(8,128)(2,1)S(1)}, bf16[4,2,48,1280]{3,2,1,0:T(8,128)(2,1)S(1)}, u32[]{:S(2)}, u32[]{:S(2)}) %collective-permute-start.52) | collective-permute-done | bytes 983072 | tf_op jit(solution)/shard_map/ppermute | solution.py:412
  787.1 4.7 shard_map.318
  791.8 4.0 dynamic-slice_bitcast_fusion
  797.4 3.2 collective-permute-start.56
  800.8 3.3 fusion.10
  804.0 3.5 collective-permute-done.54
  807.5 16.2 %collective-permute-start.44 = (bf16[3,160,960]{2,1,0:T(8,128)(2,1)}, bf16[3,160,960]{2,1,0:T(8,128)(2,1)S(1)}, u32[]{:S(2)}, u32[]{:S(2)}) collective-permute-start(bf16[3,160,960]{2,1,0:T(8,128)(2,1)} %get-tuple-element.184), channel_id=1, source_target_pairs={{0,16},{2,18},{4,20},{6,22},{8,24},{10,26},{12,28},{14,30},{16,0},... | collective-permute-start | bytes 2764808 | tf_op jit(solution)/shard_map/ppermute | solution.py:415
  833.3 43.6 %collective-permute-done.44.refs_5_ = bf16[3,160,960]{2,1,0:T(8,128)(2,1)S(1)} collective-permute-done((bf16[3,160,960]{2,1,0:T(8,128)(2,1)}, bf16[3,160,960]{2,1,0:T(8,128)(2,1)S(1)}, u32[]{:S(2)}, u32[]{:S(2)}) %collective-permute-start.44) | collective-permute-done | bytes 921632 | tf_op jit(solution)/shard_map/ppermute | solution.py:415
  884.3 3.3 fusion.19
  887.6 4.3 collective-permute-done.48
  891.9 25.6 %collective-permute-done.47 = bf16[2,160,640]{2,1,0:T(8,128)(2,1)S(1)} collective-permute-done((bf16[2,160,640]{2,1,0:T(8,128)(2,1)S(1)}, bf16[2,160,640]{2,1,0:T(8,128)(2,1)S(1)}, u32[]{:S(2)}, u32[]{:S(2)}) %collective-permute-start.47) | collective-permute-done | bytes 409632 | tf_op jit(solution)/shard_map/ppermute | solution.py:415
  919.4 6.8 shard_map.321
  930.0 5.8 collective-permute-done.50
  (450 shorter events, 157.4 us)
Async XLA Ops:
  7.2 222.9 %all-gather.4.cloned.1.call-start = ((), (), s32[]{:S(2)}) async-start(), calls=%async_computation.2 | async-start | bytes 11059200 | tf_op jit(solution)/shard_map/all_gather | solution.py:510
  9.8 16.9 %collective-permute-start.7 = (bf16[160,1920]{1,0:T(8,128)(2,1)S(1)}, bf16[160,1920]{1,0:T(8,128)(2,1)S(1)}, u32[]{:S(2)}, u32[]{:S(2)}) collective-permute-start(bf16[160,1920]{1,0:T(8,128)(2,1)S(1)} %get-tuple-element.206), channel_id=1, source_target_pairs={{0,2},{2,0},{4,6},{6,4},{8,10},{10,8},{12,14},{14,12},{16,18},{18,... | collective-permute-start | bytes 1843208 | tf_op jit(solution)/shard_map/ppermute | solution.py:412
  30.2 318.7 %all-gather.6.cloned.1.call-start = ((), (), s32[]{:S(2)}) async-start(), calls=%async_computation.3 | async-start | bytes 13107200 | tf_op jit(solution)/shard_map/all_gather | solution.py:519
  32.7 24.4 %collective-permute-start = (bf16[2,160,960]{2,1,0:T(8,128)(2,1)S(1)}, bf16[2,160,960]{2,1,0:T(8,128)(2,1)S(1)}, u32[]{:S(2)}, u32[]{:S(2)}) collective-permute-start(bf16[2,160,960]{2,1,0:T(8,128)(2,1)S(1)} %get-tuple-element.80), channel_id=1, source_target_pairs={{0,8},{2,10},{4,12},{6,14},{8,16},{10,18},{12,20},{14,22},{16,24},... | collective-permute-start | bytes 1843208 | tf_op jit(solution)/shard_map/ppermute | solution.py:415
  58.0 21.2 %collective-permute-start.3 = (bf16[1,48,1280]{2,1,0:T(8,128)(2,1)S(1)}, bf16[1,48,1280]{2,1,0:T(8,128)(2,1)S(1)}, u32[]{:S(2)}, u32[]{:S(2)}) collective-permute-start(bf16[1,48,1280]{2,1,0:T(8,128)(2,1)S(1)} %fusion.51.refs_0_), channel_id=1, source_target_pairs={{0,24},{2,26},{4,28},{6,30},{8,0},{10,2},{12,4},{14,6},{16,8},{18,... | collective-permute-start | bytes 368648 | tf_op jit(solution)/shard_map/ppermute | solution.py:415
  71.6 21.5 %collective-permute-start.2 = (bf16[1,48,1280]{2,1,0:T(8,128)(2,1)S(1)}, bf16[1,48,1280]{2,1,0:T(8,128)(2,1)S(1)}, u32[]{:S(2)}, u32[]{:S(2)}) collective-permute-start(bf16[1,48,1280]{2,1,0:T(8,128)(2,1)S(1)} %fusion.51.refs_0_), channel_id=1, source_target_pairs={{0,16},{2,18},{4,20},{6,22},{8,24},{10,26},{12,28},{14,30},{16,0},... | collective-permute-start | bytes 368648 | tf_op jit(solution)/shard_map/ppermute | solution.py:415
  73.4 19.8 %collective-permute-start.1 = (bf16[1,48,1280]{2,1,0:T(8,128)(2,1)S(1)}, bf16[1,48,1280]{2,1,0:T(8,128)(2,1)S(1)}, u32[]{:S(2)}, u32[]{:S(2)}) collective-permute-start(bf16[1,48,1280]{2,1,0:T(8,128)(2,1)S(1)} %fusion.51.refs_0_), channel_id=1, source_target_pairs={{0,8},{2,10},{4,12},{6,14},{8,16},{10,18},{12,20},{14,22},{16,24},... | collective-permute-start | bytes 368648 | tf_op jit(solution)/shard_map/ppermute | solution.py:415
  93.2 8.9 collective-permute-start.4
  103.2 21.3 %collective-permute-start.5 = (bf16[2,4,48,1280]{3,2,1,0:T(8,128)(2,1)}, bf16[2,4,48,1280]{3,2,1,0:T(8,128)(2,1)}, u32[]{:S(2)}, u32[]{:S(2)}) collective-permute-start(bf16[2,4,48,1280]{3,2,1,0:T(8,128)(2,1)} %maximum_select_fusion.7), channel_id=1, source_target_pairs={{0,2},{2,0},{4,6},{6,4},{8,10},{10,8},{12,14},{14,12},{16,18},{18,... | collective-permute-start | bytes 2949128 | tf_op jit(solution)/shard_map/ppermute | solution.py:412
  104.7 19.8 %collective-permute-start.8 = (bf16[128,2560]{1,0:T(8,128)(2,1)S(1)}, bf16[128,2560]{1,0:T(8,128)(2,1)S(1)}, u32[]{:S(2)}, u32[]{:S(2)}) collective-permute-start(bf16[128,2560]{1,0:T(8,128)(2,1)S(1)} %copy-done), channel_id=1, source_target_pairs={{0,2},{2,0},{4,6},{6,4},{8,10},{10,8},{12,14},{14,12},{16,18},{18,... | collective-permute-start | bytes 1966088 | tf_op jit(solution)/shard_map/ppermute | solution.py:412
  105.2 31.0 %collective-permute-start.6 = (bf16[128,2560]{1,0:T(8,128)(2,1)S(1)}, bf16[128,2560]{1,0:T(8,128)(2,1)S(1)}, u32[]{:S(2)}, u32[]{:S(2)}) collective-permute-start(bf16[128,2560]{1,0:T(8,128)(2,1)S(1)} %copy-done), channel_id=1, source_target_pairs={{0,1},{1,0},{2,3},{3,2},{4,5},{5,4},{6,7},{7,6},{8,9},{9,8},{10,11... | collective-permute-start | bytes 1966088 | tf_op jit(solution)/shard_map/ppermute | solution.py:410
  105.2 62.4 %collective-permute-start.11 = (bf16[2,160,960]{2,1,0:T(8,128)(2,1)}, bf16[2,160,960]{2,1,0:T(8,128)(2,1)}, u32[]{:S(2)}, u32[]{:S(2)}) collective-permute-start(bf16[2,160,960]{2,1,0:T(8,128)(2,1)} %get-tuple-element.88), channel_id=1, source_target_pairs={{0,16},{2,18},{4,20},{6,22},{8,24},{10,26},{12,28},{14,30},{16,0},... | collective-permute-start | bytes 1843208 | tf_op jit(solution)/shard_map/ppermute | solution.py:415
  107.2 60.3 %collective-permute-start.12 = (bf16[2,160,960]{2,1,0:T(8,128)(2,1)}, bf16[2,160,960]{2,1,0:T(8,128)(2,1)}, u32[]{:S(2)}, u32[]{:S(2)}) collective-permute-start(bf16[2,160,960]{2,1,0:T(8,128)(2,1)} %get-tuple-element.89), channel_id=1, source_target_pairs={{0,24},{2,26},{4,28},{6,30},{8,0},{10,2},{12,4},{14,6},{16,8},{18,... | collective-permute-start | bytes 1843208 | tf_op jit(solution)/shard_map/ppermute | solution.py:415
  124.5 12.6 %collective-permute-start.9 = (bf16[128,2560]{1,0:T(8,128)(2,1)S(1)}, bf16[128,2560]{1,0:T(8,128)(2,1)S(1)}, u32[]{:S(2)}, u32[]{:S(2)}) collective-permute-start(bf16[128,2560]{1,0:T(8,128)(2,1)S(1)} %collective-permute-done.8.refs_2_), channel_id=1, source_target_pairs={{0,1},{1,0},{2,3},{3,2},{4,5},{5,4},{6,7},{7,6},{8,9},{9,8},{10,11... | collective-permute-start | bytes 1966088 | tf_op jit(solution)/shard_map/ppermute | solution.py:410
  141.5 88.7 %copy-start.17 = (bf16[512,2560]{1,0:T(8,128)(2,1)}, bf16[512,2560]{1,0:T(8,128)(2,1)S(1)}, u32[]{:S(2)}) copy-start(bf16[512,2560]{1,0:T(8,128)(2,1)S(1)} %shard_map.298.refs_0_) | copy-start | bytes 7864324
  230.1 210.8 %all-gather.8.cloned.1.call-start = ((), (), s32[]{:S(2)}) async-start(), calls=%async_computation.4 | async-start | bytes 6553600 | tf_op jit(solution)/shard_map/all_gather | solution.py:519
  236.8 28.2 %collective-permute-start.10 = (bf16[256,1280]{1,0:T(8,128)(2,1)S(1)}, bf16[256,1280]{1,0:T(8,128)(2,1)S(1)}, u32[]{:S(2)}, u32[]{:S(2)}) collective-permute-start(bf16[256,1280]{1,0:T(8,128)(2,1)S(1)} %slice.394), channel_id=1, source_target_pairs={{0,2},{2,0},{4,6},{6,4},{8,10},{10,8},{12,14},{14,12},{16,18},{18,... | collective-permute-start | bytes 1966088 | tf_op jit(solution)/shard_map/ppermute | solution.py:412
  238.5 12.6 %collective-permute-start.13 = (bf16[1,160,960]{2,1,0:T(8,128)(2,1)S(1)}, bf16[1,160,960]{2,1,0:T(8,128)(2,1)S(1)}, u32[]{:S(2)}, u32[]{:S(2)}) collective-permute-start(bf16[1,160,960]{2,1,0:T(8,128)(2,1)S(1)} %get-tuple-element.94), channel_id=1, source_target_pairs={{0,8},{2,10},{4,12},{6,14},{8,16},{10,18},{12,20},{14,22},{16,24},... | collective-permute-start | bytes 921608 | tf_op jit(solution)/shard_map/ppermute | solution.py:415
  238.6 39.2 %collective-permute-start.14 = (bf16[1,160,960]{2,1,0:T(8,128)(2,1)S(1)}, bf16[1,160,960]{2,1,0:T(8,128)(2,1)S(1)}, u32[]{:S(2)}, u32[]{:S(2)}) collective-permute-start(bf16[1,160,960]{2,1,0:T(8,128)(2,1)S(1)} %get-tuple-element.95), channel_id=1, source_target_pairs={{0,16},{2,18},{4,20},{6,22},{8,24},{10,26},{12,28},{14,30},{16,0},... | collective-permute-start | bytes 921608 | tf_op jit(solution)/shard_map/ppermute | solution.py:415
  239.9 37.9 %collective-permute-start.15 = (bf16[1,160,960]{2,1,0:T(8,128)(2,1)S(1)}, bf16[1,160,960]{2,1,0:T(8,128)(2,1)S(1)}, u32[]{:S(2)}, u32[]{:S(2)}) collective-permute-start(bf16[1,160,960]{2,1,0:T(8,128)(2,1)S(1)} %get-tuple-element.96), channel_id=1, source_target_pairs={{0,24},{2,26},{4,28},{6,30},{8,0},{10,2},{12,4},{14,6},{16,8},{18,... | collective-permute-start | bytes 921608 | tf_op jit(solution)/shard_map/ppermute | solution.py:415
  251.1 55.5 %collective-permute-start.17 = (bf16[128,2560]{1,0:T(8,128)(2,1)S(1)}, bf16[128,2560]{1,0:T(8,128)(2,1)}, u32[]{:S(2)}, u32[]{:S(2)}) collective-permute-start(bf16[128,2560]{1,0:T(8,128)(2,1)S(1)} %shard_map.302), channel_id=1, source_target_pairs={{0,8},{2,10},{4,12},{6,14},{8,16},{10,18},{12,20},{14,22},{16,24},... | collective-permute-start | bytes 1966088 | tf_op jit(solution)/shard_map/ppermute | solution.py:415
  290.5 14.3 %collective-permute-start.16 = (bf16[256,640]{1,0:T(8,128)(2,1)}, bf16[256,640]{1,0:T(8,128)(2,1)S(1)}, u32[]{:S(2)}, u32[]{:S(2)}) collective-permute-start(bf16[256,640]{1,0:T(8,128)(2,1)} %get-tuple-element.217), channel_id=1, source_target_pairs={{0,2},{2,0},{4,6},{6,4},{8,10},{10,8},{12,14},{14,12},{16,18},{18,... | collective-permute-start | bytes 983048 | tf_op jit(solution)/shard_map/ppermute | solution.py:412
  314.6 34.3 %collective-permute-start.18 = (bf16[2,128,2560]{2,1,0:T(8,128)(2,1)}, bf16[2,128,2560]{2,1,0:T(8,128)(2,1)}, u32[]{:S(2)}, u32[]{:S(2)}) collective-permute-start(bf16[2,128,2560]{2,1,0:T(8,128)(2,1)} %fusion.22), channel_id=1, source_target_pairs={{0,1},{1,0},{2,3},{3,2},{4,5},{5,4},{6,7},{7,6},{8,9},{9,8},{10,11... | collective-permute-start | bytes 3932168 | tf_op jit(solution)/shard_map/ppermute | solution.py:410
  314.7 57.9 %collective-permute-start.21 = (bf16[128,2560]{1,0:T(8,128)(2,1)S(1)}, bf16[128,2560]{1,0:T(8,128)(2,1)}, u32[]{:S(2)}, u32[]{:S(2)}) collective-permute-start(bf16[128,2560]{1,0:T(8,128)(2,1)S(1)} %shard_map.302), channel_id=1, source_target_pairs={{0,24},{2,26},{4,28},{6,30},{8,0},{10,2},{12,4},{14,6},{16,8},{18,... | collective-permute-start | bytes 1966088 | tf_op jit(solution)/shard_map/ppermute | solution.py:415
  314.7 57.9 %collective-permute-start.20 = (bf16[128,2560]{1,0:T(8,128)(2,1)S(1)}, bf16[128,2560]{1,0:T(8,128)(2,1)}, u32[]{:S(2)}, u32[]{:S(2)}) collective-permute-start(bf16[128,2560]{1,0:T(8,128)(2,1)S(1)} %shard_map.302), channel_id=1, source_target_pairs={{0,16},{2,18},{4,20},{6,22},{8,24},{10,26},{12,28},{14,30},{16,0},... | collective-permute-start | bytes 1966088 | tf_op jit(solution)/shard_map/ppermute | solution.py:415
  348.9 339.8 %reduce-scatter.7.cloned.1.call-start = ((), (), s32[]{:S(2)}) async-start(), calls=%async_computation.6 | async-start | bytes 19660800
  351.5 20.9 %collective-permute-start.19 = (bf16[128,2560]{1,0:T(8,128)(2,1)S(1)}, bf16[128,2560]{1,0:T(8,128)(2,1)S(1)}, u32[]{:S(2)}, u32[]{:S(2)}) collective-permute-start(bf16[128,2560]{1,0:T(8,128)(2,1)S(1)} %fusion.41), channel_id=1, source_target_pairs={{0,2},{2,0},{4,6},{6,4},{8,10},{10,8},{12,14},{14,12},{16,18},{18,... | collective-permute-start | bytes 1966088 | tf_op jit(solution)/shard_map/ppermute | solution.py:412
  374.1 21.6 %collective-permute-start.24 = (bf16[128,2560]{1,0:T(8,128)(2,1)S(1)}, bf16[128,2560]{1,0:T(8,128)(2,1)S(1)}, u32[]{:S(2)}, u32[]{:S(2)}) collective-permute-start(bf16[128,2560]{1,0:T(8,128)(2,1)S(1)} %shard_map.303), channel_id=1, source_target_pairs={{0,24},{2,26},{4,28},{6,30},{8,0},{10,2},{12,4},{14,6},{16,8},{18,... | collective-permute-start | bytes 1966088 | tf_op jit(solution)/shard_map/ppermute | solution.py:415
  374.2 63.5 %collective-permute-start.23 = (bf16[128,2560]{1,0:T(8,128)(2,1)S(1)}, bf16[128,2560]{1,0:T(8,128)(2,1)S(1)}, u32[]{:S(2)}, u32[]{:S(2)}) collective-permute-start(bf16[128,2560]{1,0:T(8,128)(2,1)S(1)} %shard_map.303), channel_id=1, source_target_pairs={{0,16},{2,18},{4,20},{6,22},{8,24},{10,26},{12,28},{14,30},{16,0},... | collective-permute-start | bytes 1966088 | tf_op jit(solution)/shard_map/ppermute | solution.py:415
  384.2 53.5 %collective-permute-start.22 = (bf16[128,2560]{1,0:T(8,128)(2,1)S(1)}, bf16[128,2560]{1,0:T(8,128)(2,1)S(1)}, u32[]{:S(2)}, u32[]{:S(2)}) collective-permute-start(bf16[128,2560]{1,0:T(8,128)(2,1)S(1)} %shard_map.303), channel_id=1, source_target_pairs={{0,8},{2,10},{4,12},{6,14},{8,16},{10,18},{12,20},{14,22},{16,24},... | collective-permute-start | bytes 1966088 | tf_op jit(solution)/shard_map/ppermute | solution.py:415
  387.9 51.4 %collective-permute-start.26 = (bf16[512,2560]{1,0:T(8,128)(2,1)S(1)}, bf16[512,2560]{1,0:T(8,128)(2,1)S(1)}, u32[]{:S(2)}, u32[]{:S(2)}) collective-permute-start(bf16[512,2560]{1,0:T(8,128)(2,1)S(1)} %constant_dynamic-update-slice_fusion.act.refs_0_), channel_id=1, source_target_pairs={{0,1},{1,0},{2,3},{3,2},{4,5},{5,4},{6,7},{7,6},{8,9},{9,8},{10,11... | collective-permute-start | bytes 7864328 | tf_op jit(solution)/shard_map/ppermute | solution.py:410
  439.3 10.2 %collective-permute-start.25 = (bf16[512,2560]{1,0:T(8,128)(2,1)}, bf16[512,2560]{1,0:T(8,128)(2,1)}, u32[]{:S(2)}, u32[]{:S(2)}) collective-permute-start(bf16[512,2560]{1,0:T(8,128)(2,1)} %pad_maximum_fusion.1.act.refs_0_), channel_id=1, source_target_pairs={{0,1},{1,0},{2,3},{3,2},{4,5},{5,4},{6,7},{7,6},{8,9},{9,8},{10,11... | collective-permute-start | bytes 7864328 | tf_op jit(solution)/shard_map/ppermute | solution.py:410
  468.5 26.6 %collective-permute-start.27 = (bf16[512,2560]{1,0:T(8,128)(2,1)}, bf16[512,2560]{1,0:T(8,128)(2,1)S(1)}, u32[]{:S(2)}, u32[]{:S(2)}) collective-permute-start(bf16[512,2560]{1,0:T(8,128)(2,1)} %shard_map.310), channel_id=1, source_target_pairs={{0,1},{1,0},{2,3},{3,2},{4,5},{5,4},{6,7},{7,6},{8,9},{9,8},{10,11... | collective-permute-start | bytes 7864328 | tf_op jit(solution)/shard_map/ppermute | solution.py:410
  502.2 25.5 %collective-permute-start.28 = (bf16[128,2560]{1,0:T(8,128)(2,1)}, bf16[128,2560]{1,0:T(8,128)(2,1)S(1)}, u32[]{:S(2)}, u32[]{:S(2)}) collective-permute-start(bf16[128,2560]{1,0:T(8,128)(2,1)} %get-tuple-element.192), channel_id=1, source_target_pairs={{0,24},{2,26},{4,28},{6,30},{8,0},{10,2},{12,4},{14,6},{16,8},{18,... | collective-permute-start | bytes 1966088 | tf_op jit(solution)/shard_map/ppermute | solution.py:415
  528.5 397.9 %reduce-scatter.5.cloned.1.call-start = ((), (), s32[]{:S(2)}) async-start(), calls=%async_computation.5 | async-start | bytes 7372800 | tf_op jit(solution)/shard_map/reduce_scatter | solution.py:630
  540.5 12.4 %collective-permute-start.31 = (bf16[512,2560]{1,0:T(8,128)(2,1)}, bf16[512,2560]{1,0:T(8,128)(2,1)S(1)}, u32[]{:S(2)}, u32[]{:S(2)}) collective-permute-start(bf16[512,2560]{1,0:T(8,128)(2,1)} %shard_map.315), channel_id=1, source_target_pairs={{0,1},{1,0},{2,3},{3,2},{4,5},{5,4},{6,7},{7,6},{8,9},{9,8},{10,11... | collective-permute-start | bytes 7864328 | tf_op jit(solution)/shard_map/ppermute | solution.py:410
  540.5 23.4 %collective-permute-start.30 = (bf16[128,2560]{1,0:T(8,128)(2,1)}, bf16[128,2560]{1,0:T(8,128)(2,1)S(1)}, u32[]{:S(2)}, u32[]{:S(2)}) collective-permute-start(bf16[128,2560]{1,0:T(8,128)(2,1)} %get-tuple-element.193), channel_id=1, source_target_pairs={{0,8},{2,10},{4,12},{6,14},{8,16},{10,18},{12,20},{14,22},{16,24},... | collective-permute-start | bytes 1966088 | tf_op jit(solution)/shard_map/ppermute | solution.py:415
  540.9 74.9 %collective-permute-start.29 = (bf16[128,2560]{1,0:T(8,128)(2,1)}, bf16[128,2560]{1,0:T(8,128)(2,1)S(1)}, u32[]{:S(2)}, u32[]{:S(2)}) collective-permute-start(bf16[128,2560]{1,0:T(8,128)(2,1)} %get-tuple-element.194), channel_id=1, source_target_pairs={{0,16},{2,18},{4,20},{6,22},{8,24},{10,26},{12,28},{14,30},{16,0},... | collective-permute-start | bytes 1966088 | tf_op jit(solution)/shard_map/ppermute | solution.py:415
  556.6 59.2 %collective-permute-start.34 = (bf16[128,2560]{1,0:T(8,128)(2,1)S(1)}, bf16[128,2560]{1,0:T(8,128)(2,1)S(1)}, u32[]{:S(2)}, u32[]{:S(2)}) collective-permute-start(bf16[128,2560]{1,0:T(8,128)(2,1)S(1)} %get-tuple-element.189), channel_id=1, source_target_pairs={{0,8},{2,10},{4,12},{6,14},{8,16},{10,18},{12,20},{14,22},{16,24},... | collective-permute-start | bytes 1966088 | tf_op jit(solution)/shard_map/ppermute | solution.py:415
  561.2 68.6 %collective-permute-start.33 = (bf16[128,2560]{1,0:T(8,128)(2,1)S(1)}, bf16[128,2560]{1,0:T(8,128)(2,1)S(1)}, u32[]{:S(2)}, u32[]{:S(2)}) collective-permute-start(bf16[128,2560]{1,0:T(8,128)(2,1)S(1)} %get-tuple-element.190), channel_id=1, source_target_pairs={{0,16},{2,18},{4,20},{6,22},{8,24},{10,26},{12,28},{14,30},{16,0},... | collective-permute-start | bytes 1966088 | tf_op jit(solution)/shard_map/ppermute | solution.py:415
  561.2 68.6 %collective-permute-start.32 = (bf16[128,2560]{1,0:T(8,128)(2,1)S(1)}, bf16[128,2560]{1,0:T(8,128)(2,1)S(1)}, u32[]{:S(2)}, u32[]{:S(2)}) collective-permute-start(bf16[128,2560]{1,0:T(8,128)(2,1)S(1)} %get-tuple-element.191), channel_id=1, source_target_pairs={{0,24},{2,26},{4,28},{6,30},{8,0},{10,2},{12,4},{14,6},{16,8},{18,... | collective-permute-start | bytes 1966088 | tf_op jit(solution)/shard_map/ppermute | solution.py:415
  633.0 30.9 %collective-permute-start.35 = (bf16[128,2560]{1,0:T(8,128)(2,1)S(1)}, bf16[128,2560]{1,0:T(8,128)(2,1)S(1)}, u32[]{:S(2)}, u32[]{:S(2)}) collective-permute-start(bf16[128,2560]{1,0:T(8,128)(2,1)S(1)} %fusion.63), channel_id=1, source_target_pairs={{0,2},{2,0},{4,6},{6,4},{8,10},{10,8},{12,14},{14,12},{16,18},{18,... | collective-permute-start | bytes 1966088 | tf_op jit(solution)/shard_map/ppermute | solution.py:412
  665.6 3.4 collective-permute-start.36
  678.4 21.0 %collective-permute-start.37 = (bf16[256,640]{1,0:T(8,128)(2,1)}, bf16[256,640]{1,0:T(8,128)(2,1)}, u32[]{:S(2)}, u32[]{:S(2)}) collective-permute-start(bf16[256,640]{1,0:T(8,128)(2,1)} %slice.395), channel_id=1, source_target_pairs={{0,2},{2,0},{4,6},{6,4},{8,10},{10,8},{12,14},{14,12},{16,18},{18,... | collective-permute-start | bytes 983048 | tf_op jit(solution)/shard_map/ppermute | solution.py:412
  692.6 26.0 %collective-permute-start.38 = (bf16[3,160,960]{2,1,0:T(8,128)(2,1)S(1)}, bf16[3,160,960]{2,1,0:T(8,128)(2,1)S(1)}, u32[]{:S(2)}, u32[]{:S(2)}) collective-permute-start(bf16[3,160,960]{2,1,0:T(8,128)(2,1)S(1)} %get-tuple-element.185), channel_id=1, source_target_pairs={{0,8},{2,10},{4,12},{6,14},{8,16},{10,18},{12,20},{14,22},{16,24},... | collective-permute-start | bytes 2764808 | tf_op jit(solution)/shard_map/ppermute | solution.py:415
  719.6 9.0 collective-permute-start.40
  725.5 107.8 %collective-permute-start.45 = (bf16[3,160,960]{2,1,0:T(8,128)(2,1)}, bf16[3,160,960]{2,1,0:T(8,128)(2,1)}, u32[]{:S(2)}, u32[]{:S(2)}) collective-permute-start(bf16[3,160,960]{2,1,0:T(8,128)(2,1)} %get-tuple-element.182), channel_id=1, source_target_pairs={{0,24},{2,26},{4,28},{6,30},{8,0},{10,2},{12,4},{14,6},{16,8},{18,... | collective-permute-start | bytes 2764808 | tf_op jit(solution)/shard_map/ppermute | solution.py:415
  756.2 10.7 %collective-permute-start.39 = (bf16[256,640]{1,0:T(8,128)(2,1)S(1)}, bf16[256,640]{1,0:T(8,128)(2,1)S(1)}, u32[]{:S(2)}, u32[]{:S(2)}) collective-permute-start(bf16[256,640]{1,0:T(8,128)(2,1)S(1)} %get-tuple-element.213), channel_id=1, source_target_pairs={{0,2},{2,0},{4,6},{6,4},{8,10},{10,8},{12,14},{14,12},{16,18},{18,... | collective-permute-start | bytes 983048 | tf_op jit(solution)/shard_map/ppermute | solution.py:412
  758.6 26.8 %collective-permute-start.52 = (bf16[4,2,48,1280]{3,2,1,0:T(8,128)(2,1)S(1)}, bf16[4,2,48,1280]{3,2,1,0:T(8,128)(2,1)S(1)}, u32[]{:S(2)}, u32[]{:S(2)}) collective-permute-start(bf16[4,2,48,1280]{3,2,1,0:T(8,128)(2,1)S(1)} %fusion.37), channel_id=1, source_target_pairs={{0,2},{2,0},{4,6},{6,4},{8,10},{10,8},{12,14},{14,12},{16,18},{18,... | collective-permute-start | bytes 2949128 | tf_op jit(solution)/shard_map/ppermute | solution.py:412
  774.0 51.8 %collective-permute-start.41 = (bf16[2,128,2560]{2,1,0:T(8,128)(2,1)}, bf16[2,128,2560]{2,1,0:T(8,128)(2,1)}, u32[]{:S(2)}, u32[]{:S(2)}) collective-permute-start(bf16[2,128,2560]{2,1,0:T(8,128)(2,1)} %fusion.23), channel_id=1, source_target_pairs={{0,1},{1,0},{2,3},{3,2},{4,5},{5,4},{6,7},{7,6},{8,9},{9,8},{10,11... | collective-permute-start | bytes 3932168 | tf_op jit(solution)/shard_map/ppermute | solution.py:410
  785.7 10.8 %collective-permute-start.53 = (bf16[4,48,1280]{2,1,0:T(8,128)(2,1)S(1)}, bf16[4,48,1280]{2,1,0:T(8,128)(2,1)S(1)}, u32[]{:S(2)}, u32[]{:S(2)}) collective-permute-start(bf16[4,48,1280]{2,1,0:T(8,128)(2,1)S(1)} %fusion.43), channel_id=1, source_target_pairs={{0,4},{2,6},{4,0},{6,2},{8,12},{10,14},{12,8},{14,10},{16,20},{18,... | collective-permute-start | bytes 1474568 | tf_op jit(solution)/shard_map/ppermute | solution.py:412
  796.7 10.9 %collective-permute-start.54 = (bf16[48,1280]{1,0:T(8,128)(2,1)S(1)}, bf16[48,1280]{1,0:T(8,128)(2,1)S(1)}, u32[]{:S(2)}, u32[]{:S(2)}) collective-permute-start(bf16[48,1280]{1,0:T(8,128)(2,1)S(1)} %get-tuple-element.207), channel_id=1, source_target_pairs={{0,8},{2,10},{4,12},{6,14},{8,16},{10,18},{12,20},{14,22},{16,24},... | collective-permute-start | bytes 368648 | tf_op jit(solution)/shard_map/ppermute | solution.py:415
  797.4 26.3 %collective-permute-start.56 = (bf16[48,1280]{1,0:T(8,128)(2,1)S(1)}, bf16[48,1280]{1,0:T(8,128)(2,1)S(1)}, u32[]{:S(2)}, u32[]{:S(2)}) collective-permute-start(bf16[48,1280]{1,0:T(8,128)(2,1)S(1)} %get-tuple-element.208), channel_id=1, source_target_pairs={{0,24},{2,26},{4,28},{6,30},{8,0},{10,2},{12,4},{14,6},{16,8},{18,... | collective-permute-start | bytes 368648 | tf_op jit(solution)/shard_map/ppermute | solution.py:415
  800.5 24.6 %collective-permute-start.55 = (bf16[48,1280]{1,0:T(8,128)(2,1)S(1)}, bf16[48,1280]{1,0:T(8,128)(2,1)S(1)}, u32[]{:S(2)}, u32[]{:S(2)}) collective-permute-start(bf16[48,1280]{1,0:T(8,128)(2,1)S(1)} %get-tuple-element.209), channel_id=1, source_target_pairs={{0,16},{2,18},{4,20},{6,22},{8,24},{10,26},{12,28},{14,30},{16,0},... | collective-permute-start | bytes 368648 | tf_op jit(solution)/shard_map/ppermute | solution.py:415
  807.5 69.4 %collective-permute-start.44 = (bf16[3,160,960]{2,1,0:T(8,128)(2,1)}, bf16[3,160,960]{2,1,0:T(8,128)(2,1)S(1)}, u32[]{:S(2)}, u32[]{:S(2)}) collective-permute-start(bf16[3,160,960]{2,1,0:T(8,128)(2,1)} %get-tuple-element.184), channel_id=1, source_target_pairs={{0,16},{2,18},{4,20},{6,22},{8,24},{10,26},{12,28},{14,30},{16,0},... | collective-permute-start | bytes 2764808 | tf_op jit(solution)/shard_map/ppermute | solution.py:415
  823.7 53.2 %collective-permute-start.43 = (bf16[4,2,160,640]{3,2,1,0:T(8,128)(2,1)}, bf16[4,2,160,640]{3,2,1,0:T(8,128)(2,1)}, u32[]{:S(2)}, u32[]{:S(2)}) collective-permute-start(bf16[4,2,160,640]{3,2,1,0:T(8,128)(2,1)} %fusion.10), channel_id=1, source_target_pairs={{0,4},{2,6},{4,0},{6,2},{8,12},{10,14},{12,8},{14,10},{16,20},{18,... | collective-permute-start | bytes 4915208 | tf_op jit(solution)/shard_map/ppermute | solution.py:412
  829.9 52.7 %collective-permute-start.42 = (bf16[128,2560]{1,0:T(8,128)(2,1)}, bf16[128,2560]{1,0:T(8,128)(2,1)}, u32[]{:S(2)}, u32[]{:S(2)}) collective-permute-start(bf16[128,2560]{1,0:T(8,128)(2,1)} %fusion.42), channel_id=1, source_target_pairs={{0,2},{2,0},{4,6},{6,4},{8,10},{10,8},{12,14},{14,12},{16,18},{18,... | collective-permute-start | bytes 1966088 | tf_op jit(solution)/shard_map/ppermute | solution.py:412
  879.9 11.9 %collective-permute-start.48 = (bf16[2,160,640]{2,1,0:T(8,128)(2,1)S(1)}, bf16[2,160,640]{2,1,0:T(8,128)(2,1)S(1)}, u32[]{:S(2)}, u32[]{:S(2)}) collective-permute-start(bf16[2,160,640]{2,1,0:T(8,128)(2,1)S(1)} %get-tuple-element.186), channel_id=1, source_target_pairs={{0,24},{2,26},{4,28},{6,30},{8,0},{10,2},{12,4},{14,6},{16,8},{18,... | collective-permute-start | bytes 1228808 | tf_op jit(solution)/shard_map/ppermute | solution.py:415
  882.0 35.5 %collective-permute-start.47 = (bf16[2,160,640]{2,1,0:T(8,128)(2,1)S(1)}, bf16[2,160,640]{2,1,0:T(8,128)(2,1)S(1)}, u32[]{:S(2)}, u32[]{:S(2)}) collective-permute-start(bf16[2,160,640]{2,1,0:T(8,128)(2,1)S(1)} %get-tuple-element.187), channel_id=1, source_target_pairs={{0,16},{2,18},{4,20},{6,22},{8,24},{10,26},{12,28},{14,30},{16,0},... | collective-permute-start | bytes 1228808 | tf_op jit(solution)/shard_map/ppermute | solution.py:415
  882.0 35.5 %collective-permute-start.46 = (bf16[2,160,640]{2,1,0:T(8,128)(2,1)S(1)}, bf16[2,160,640]{2,1,0:T(8,128)(2,1)S(1)}, u32[]{:S(2)}, u32[]{:S(2)}) collective-permute-start(bf16[2,160,640]{2,1,0:T(8,128)(2,1)S(1)} %get-tuple-element.188), channel_id=1, source_target_pairs={{0,8},{2,10},{4,12},{6,14},{8,16},{10,18},{12,20},{14,22},{16,24},... | collective-permute-start | bytes 1228808 | tf_op jit(solution)/shard_map/ppermute | solution.py:415
  917.8 8.5 collective-permute-start.49
  927.7 8.1 collective-permute-start.50
  929.2 8.9 collective-permute-start.57
  937.3 1.7 collective-permute-start.51
  (111 other events, 738.3 us)
Sparse Core Ops, SparseCore 0:
  30.2 199.8 all-gather.3
  231.9 116.8 all-gather.5
  351.3 69.4 all-gather.7
  527.8 160.8 reduce-scatter.6
  733.1 152.8 reduce-scatter.4

commit v5 on v4

--- a/solution.py
+++ b/solution.py
@@ -284,44 +284,29 @@
     return ref[...].reshape(-1, ref.shape[-1])
 
 
-def ffn_down_back(act, weights):
+def ffn_middle(act, weights, upstream):
     tokens, width = act.shape
     units = weights[0].shape[-1]
 
-    def kernel(act, down, out):
-        out[...] = matmul(act[...], flat(down))
-
-    return pl.pallas_call(
-        kernel,
-        grid=(tokens // TILE,),
-        in_specs=[rows_of(width), weight_of(weights, DOWN)],
-        out_specs=rows_of(units),
-        out_shape=jax.ShapeDtypeStruct((tokens, units), F32),
-        compiler_params=params(48),
-    )(act, weights[1])
-
-
-def ffn_middle(act, weights, grad_hidden):
-    tokens, width = act.shape
-    units = weights[0].shape[-1]
-
-    def kernel(act, grad, gate, up, hidden, grads):
+    def kernel(act, upstream, gate, up, down, hidden, grads):
         value = act[...]
+        grad = matmul(upstream[...], flat(down))
         gate_pre = matmul(value, flat(gate))
         up_pre = matmul(value, flat(up))
         active, slope = gelu_parts(gate_pre)
         hidden[...] = (active * up_pre).astype(BF16)
-        grads[0] = (slope * (grad[...] * up_pre)).astype(BF16)
-        grads[1] = (grad[...] * active).astype(BF16)
+        grads[0] = (slope * (grad * up_pre)).astype(BF16)
+        grads[1] = (grad * active).astype(BF16)
 
     return pl.pallas_call(
         kernel,
         grid=(tokens // TILE,),
         in_specs=[
             rows_of(width),
-            rows_of(units),
+            rows_of(width),
             weight_of(weights, GATE),
             weight_of(weights, UP),
+            weight_of(weights, DOWN),
         ],
         out_specs=[rows_of(units), pl.BlockSpec((2, TILE, units), lambda i: (0, i, 0))],
         out_shape=[
@@ -329,7 +314,7 @@
             jax.ShapeDtypeStruct((2, tokens, units), BF16),
         ],
         compiler_params=params(56),
-    )(act, grad_hidden, weights[0], weights[0])
+    )(act, upstream, weights[0], weights[0], weights[1])
 
 
 def ffn_collect(acts, weights, which, dtype):
@@ -572,10 +557,9 @@
             return rows, grid.swap(rows, "t")
 
         upstream = both_t(cot_line)
-        grad_hidden = [ffn_down_back(u, weights) for u in upstream]
         normed_two = both_t(to_line(normed_two_rows.astype(BF16)))
         hidden, grad_pre = zip(
-            *[ffn_middle(a, weights, g) for a, g in zip(normed_two, grad_hidden)]
+            *[ffn_middle(a, weights, u) for a, u in zip(normed_two, upstream)]
         )
         hidden = [h[None] for h in hidden]
         sent, got_result = from_line(hidden, (DOWN,))

time: 957 us -> 951 us (level)
    pallas_call x2 -> x0, Pallas kernels: 11.1 us -> none  [ffn_down_back(): pl.pallas_call(kernel, grid=(tokens // TILE,), in_specs=[rows_of(width),...]
    unnamed x228 -> x220, local copies, waits for them, and re-layouts: 49.7 us -> 47.7 us
  transfers between devices with their start and end apart: 63 -> 63, of which waited for: 32 -> 33; matrix products, arithmetic and copies ran while one was open for 10% -> 10% of each run, Pallas kernels for 13% -> 12%
where the time goes in v5:
time: 951 us; the launch traced here: 941 us
  waiting for transfers between devices  532 us (56%)
  Pallas kernels  138 us (15%)
  starting transfers between devices  107 us (11%)
  local copies, waits for them, and re-layouts  83.7 us (9%)
  other arithmetic  42.3 us (4%)
  matrix products  21.7 us (2%)
  between operations  15.8 us (2%)
    ppermute x30, waiting for transfers between devices, shift(): lax.ppermute(value, 'dp', [(i, (i + 4 * by) % self.n) for i in range(self...  296 us
    ppermute x18, waiting for transfers between devices, swap(): return lax.ppermute(value, 'dp', [(i, i ^ bit) for i in range(self.n)])  140 us
    ppermute x30, starting transfers between devices, shift(): lax.ppermute(value, 'dp', [(i, (i + 4 * by) % self.n) for i in range(self...  86.1 us
    all_gather x1, waiting for transfers between devices, run(): lax.all_gather(mine, 'dp', axis=0, tiled=True, axis_index_groups=grid.pla...  59.5 us
    unnamed x220, local copies, waits for them, and re-layouts  47.7 us
    pallas_call x4, Pallas kernels, ffn_collect(): pl.pallas_call(kernel, grid=(tokens // TILE,), in_specs=[pl.BlockSpec((n,...  38.1 us
    pallas_call x5, Pallas kernels, weight_grad(): pl.pallas_call(kernel, grid=(m, width // block // at_once), in_specs=[pl....  37.6 us
    pallas_call x2, Pallas kernels, ffn_middle(): pl.pallas_call(kernel, grid=(tokens // TILE,), in_specs=[rows_of(width),...  32.5 us
  transfers between devices with their start and end apart: 63, of which 33 were waited for; matrix products, arithmetic and copies ran while one was open for 10% of the time, Pallas kernels for 12%

profile of v5, /device:TPU:0, one launch (start us, length us, event | category | flops | bytes accessed | tf_op | source)
XLA Modules:
  0.0 940.8 jit_solution(4739896824760883915)
XLA Ops:
  9.8 3.0 collective-permute-start.7
  12.8 13.9 %collective-permute-done.7 = bf16[160,1920]{1,0:T(8,128)(2,1)S(1)} collective-permute-done((bf16[160,1920]{1,0:T(8,128)(2,1)S(1)}, bf16[160,1920]{1,0:T(8,128)(2,1)S(1)}, u32[]{:S(2)}, u32[]{:S(2)}) %collective-permute-start.7) | collective-permute-done | bytes 614432 | tf_op jit(solution)/shard_map/ppermute | solution.py:397
  27.4 2.6 maximum_select_fusion.5
  34.8 22.3 %collective-permute-done.refs_1_ = bf16[2,160,960]{2,1,0:T(8,128)(2,1)S(1)} collective-permute-done((bf16[2,160,960]{2,1,0:T(8,128)(2,1)S(1)}, bf16[2,160,960]{2,1,0:T(8,128)(2,1)S(1)}, u32[]{:S(2)}, u32[]{:S(2)}) %collective-permute-start) | collective-permute-done | bytes 614432 | tf_op jit(solution)/shard_map/ppermute | solution.py:400
  58.0 13.6 %collective-permute-start.3 = (bf16[1,48,1280]{2,1,0:T(8,128)(2,1)S(1)}, bf16[1,48,1280]{2,1,0:T(8,128)(2,1)S(1)}, u32[]{:S(2)}, u32[]{:S(2)}) collective-permute-start(bf16[1,48,1280]{2,1,0:T(8,128)(2,1)S(1)} %fusion.51.refs_0_), channel_id=1, source_target_pairs={{0,24},{2,26},{4,28},{6,30},{8,0},{10,2},{12,4},{14,6},{16,8},{18,... | collective-permute-start | bytes 368648 | tf_op jit(solution)/shard_map/ppermute | solution.py:400
  75.4 3.8 collective-permute-done.3.refs_3_
  79.2 14.0 %collective-permute-done.2.refs_2_ = bf16[1,48,1280]{2,1,0:T(8,128)(2,1)S(1)} collective-permute-done((bf16[1,48,1280]{2,1,0:T(8,128)(2,1)S(1)}, bf16[1,48,1280]{2,1,0:T(8,128)(2,1)S(1)}, u32[]{:S(2)}, u32[]{:S(2)}) %collective-permute-start.2) | collective-permute-done | bytes 122912 | tf_op jit(solution)/shard_map/ppermute | solution.py:400
  94.8 7.3 collective-permute-done.4
  107.9 16.7 %collective-permute-done.8.refs_2_ = bf16[128,2560]{1,0:T(8,128)(2,1)S(1)} collective-permute-done((bf16[128,2560]{1,0:T(8,128)(2,1)S(1)}, bf16[128,2560]{1,0:T(8,128)(2,1)S(1)}, u32[]{:S(2)}, u32[]{:S(2)}) %collective-permute-start.8) | collective-permute-done | bytes 655392 | tf_op jit(solution)/shard_map/ppermute | solution.py:397
  128.5 4.0 reshape.359
  141.6 26.0 %collective-permute-done.11.refs_2_ = bf16[2,160,960]{2,1,0:T(8,128)(2,1)} collective-permute-done((bf16[2,160,960]{2,1,0:T(8,128)(2,1)}, bf16[2,160,960]{2,1,0:T(8,128)(2,1)}, u32[]{:S(2)}, u32[]{:S(2)}) %collective-permute-start.11) | collective-permute-done | bytes 614432 | tf_op jit(solution)/shard_map/ppermute | solution.py:400
  167.6 3.0 shard_map.300
  170.6 59.5 %all-gather.4.cloned.1.call-done = bf16[2560,1920]{1,0:T(8,128)(2,1)} async-done(((bf16[320,1920]{1,0:T(8,128)(2,1)}), bf16[2560,1920]{1,0:T(8,128)(2,1)}) %all-gather.4.cloned.1.call-update) | async-done | bytes 9830416 | tf_op jit(solution)/shard_map/all_gather | solution.py:495
  230.2 6.5 fusion.2
  242.7 8.4 collective-permute-done.13.refs_1_
  251.9 13.2 %collective-permute-done.10 = bf16[256,1280]{1,0:T(8,128)(2,1)S(1)} collective-permute-done((bf16[256,1280]{1,0:T(8,128)(2,1)S(1)}, bf16[256,1280]{1,0:T(8,128)(2,1)S(1)}, u32[]{:S(2)}, u32[]{:S(2)}) %collective-permute-start.10) | collective-permute-done | bytes 655392 | tf_op jit(solution)/shard_map/ppermute | solution.py:397
  265.1 12.7 %collective-permute-done.14.refs_2_ = bf16[1,160,960]{2,1,0:T(8,128)(2,1)S(1)} collective-permute-done((bf16[1,160,960]{2,1,0:T(8,128)(2,1)S(1)}, bf16[1,160,960]{2,1,0:T(8,128)(2,1)S(1)}, u32[]{:S(2)}, u32[]{:S(2)}) %collective-permute-start.14) | collective-permute-done | bytes 307232 | tf_op jit(solution)/shard_map/ppermute | solution.py:400
  280.0 6.0 shard_map.301
  291.1 13.7 %collective-permute-done.16 = bf16[256,640]{1,0:T(8,128)(2,1)} collective-permute-done((bf16[256,640]{1,0:T(8,128)(2,1)}, bf16[256,640]{1,0:T(8,128)(2,1)}, u32[]{:S(2)}, u32[]{:S(2)}) %collective-permute-start.16) | collective-permute-done | bytes 327712 | tf_op jit(solution)/shard_map/ppermute | solution.py:397
  306.0 4.4 fusion.6
  314.1 10.9 %collective-permute-start.20 = (bf16[128,2560]{1,0:T(8,128)(2,1)S(1)}, bf16[128,2560]{1,0:T(8,128)(2,1)}, u32[]{:S(2)}, u32[]{:S(2)}) collective-permute-start(bf16[128,2560]{1,0:T(8,128)(2,1)S(1)} %shard_map.302), channel_id=1, source_target_pairs={{0,16},{2,18},{4,20},{6,22},{8,24},{10,26},{12,28},{14,30},{16,0},... | collective-permute-start | bytes 1966088 | tf_op jit(solution)/shard_map/ppermute | solution.py:400
  330.0 18.9 %all-gather.6.cloned.1.call-done.gate.up.refs_0_.refs_1_ = bf16[4,2,4,160,960]{4,3,2,1,0:T(8,128)(2,1)} async-done(((bf16[1,2,4,160,960]{4,3,2,1,0:T(8,128)(2,1)}), bf16[4,2,4,160,960]{4,3,2,1,0:T(8,128)(2,1)}) %all-gather.6.cloned.1.call-update) | async-done | bytes 9830416 | tf_op jit(solution)/shard_map/all_gather | solution.py:504
  353.1 19.3 %collective-permute-done.19 = bf16[128,2560]{1,0:T(8,128)(2,1)S(1)} collective-permute-done((bf16[128,2560]{1,0:T(8,128)(2,1)S(1)}, bf16[128,2560]{1,0:T(8,128)(2,1)S(1)}, u32[]{:S(2)}, u32[]{:S(2)}) %collective-permute-start.19) | collective-permute-done | bytes 655392 | tf_op jit(solution)/shard_map/ppermute | solution.py:397
  374.2 10.0 %collective-permute-start.23 = (bf16[128,2560]{1,0:T(8,128)(2,1)S(1)}, bf16[128,2560]{1,0:T(8,128)(2,1)S(1)}, u32[]{:S(2)}, u32[]{:S(2)}) collective-permute-start(bf16[128,2560]{1,0:T(8,128)(2,1)S(1)} %shard_map.303), channel_id=1, source_target_pairs={{0,16},{2,18},{4,20},{6,22},{8,24},{10,26},{12,28},{14,30},{16,0},... | collective-permute-start | bytes 1966088 | tf_op jit(solution)/shard_map/ppermute | solution.py:400
  388.0 7.7 collective-permute-done.24
  395.7 42.0 %collective-permute-done.23 = bf16[128,2560]{1,0:T(8,128)(2,1)S(1)} collective-permute-done((bf16[128,2560]{1,0:T(8,128)(2,1)S(1)}, bf16[128,2560]{1,0:T(8,128)(2,1)S(1)}, u32[]{:S(2)}, u32[]{:S(2)}) %collective-permute-start.23) | collective-permute-done | bytes 655392 | tf_op jit(solution)/shard_map/ppermute | solution.py:400
  443.0 16.3 %shard_map.307 = (bf16[512,960]{1,0:T(8,128)(2,1)}, bf16[2,512,960]{2,1,0:T(8,128)(2,1)}) custom-call(bf16[512,2560]{1,0:T(8,128)(2,1)} %collective-permute-done.25.act.refs_1_, bf16[512,2560]{1,0:T(8,128)(2,1)} %copy-done.75, bf16[4,2,4,160,960]{4,3,2,1,0:T(8,128)(2,1)} %all-gather.6.cloned.1.call-done.gate.up.refs_0_.refs_1_, ...), custom_call_target="tpu_custom_call" | custom-call | tf_op jit(solution)/shard_map/pallas_call | solution.py:301
  459.3 6.9 shard_map.308
  466.3 16.2 %shard_map.305 = (bf16[512,960]{1,0:T(8,128)(2,1)}, bf16[2,512,960]{2,1,0:T(8,128)(2,1)}) custom-call(bf16[512,2560]{1,0:T(8,128)(2,1)} %copy-done.71, bf16[512,2560]{1,0:T(8,128)(2,1)} %copy-done.11, bf16[4,2,4,160,960]{4,3,2,1,0:T(8,128)(2,1)} %all-gather.6.cloned.1.call-done.gate.up.refs_0_.refs_1_, ...), custom_call_target="tpu_custom_call" | custom-call | tf_op jit(solution)/shard_map/pallas_call | solution.py:301
  482.5 7.4 shard_map.306
  489.9 3.2 convert_add_fusion.1
  497.9 15.7 %shard_map.310.refs_4_ = bf16[4,3,4,160,960]{4,3,2,1,0:T(8,128)(2,1)} custom-call(bf16[512,2560]{1,0:T(8,128)(2,1)} %copy-done.71, bf16[512,2560]{1,0:T(8,128)(2,1)} %collective-permute-done.25.act.refs_1_, bf16[2,512,960]{2,1,0:T(8,128)(2,1)S(1)} %copy-done.19, bf16[2,512,960]{2,1,0:T(8,128)(2,1)S(1)} %copy-done.20), custom_call_target="tpu_custom_call" | custom-call | flops 20000000000 | tf_op jit(solution)/shard_map/pallas_call | solution.py:358
  513.6 8.6 shard_map.311
  523.1 11.9 %shard_map.313 = bf16[512,2560]{1,0:T(8,128)(2,1)} custom-call(bf16[2,512,960]{2,1,0:T(8,128)(2,1)} %get-tuple-element.114.refs_3_.acts, bf16[4,2,4,160,960]{4,3,2,1,0:T(8,128)(2,1)} %all-gather.6.cloned.1.call-done.gate.up.refs_0_.refs_1_, bf16[4,2,4,160,960]{4,3,2,1,0:T(8,128)(2,1)} %all-gather.6.cloned.1.call-done.gate.up.refs_0_.refs_1_), custom_call_target="tpu_custom_call" | custom-call | tf_op jit(solution)/shard_map/pallas_call | solution.py:330
  535.6 12.0 %shard_map.312 = f32[512,2560]{1,0:T(8,128)} custom-call(bf16[2,512,960]{2,1,0:T(8,128)(2,1)} %get-tuple-element.113.refs_2_.acts, bf16[4,2,4,160,960]{4,3,2,1,0:T(8,128)(2,1)} %all-gather.6.cloned.1.call-done.gate.up.refs_0_.refs_1_, bf16[4,2,4,160,960]{4,3,2,1,0:T(8,128)(2,1)} %all-gather.6.cloned.1.call-done.gate.up.refs_0_.refs_1_), custom_call_target="tpu_custom_call" | custom-call | tf_op jit(solution)/shard_map/pallas_call | solution.py:330
  547.6 3.2 convert_add_fusion
  551.3 4.8 collective-permute-start.34
  558.9 51.5 %collective-permute-done.29 = bf16[128,2560]{1,0:T(8,128)(2,1)S(1)} collective-permute-done((bf16[128,2560]{1,0:T(8,128)(2,1)}, bf16[128,2560]{1,0:T(8,128)(2,1)S(1)}, u32[]{:S(2)}, u32[]{:S(2)}) %collective-permute-start.29) | collective-permute-done | bytes 655392 | tf_op jit(solution)/shard_map/ppermute | solution.py:400
  610.4 14.0 %collective-permute-done.33 = bf16[128,2560]{1,0:T(8,128)(2,1)S(1)} collective-permute-done((bf16[128,2560]{1,0:T(8,128)(2,1)S(1)}, bf16[128,2560]{1,0:T(8,128)(2,1)S(1)}, u32[]{:S(2)}, u32[]{:S(2)}) %collective-permute-start.33) | collective-permute-done | bytes 655392 | tf_op jit(solution)/shard_map/ppermute | solution.py:400
  626.8 30.9 %collective-permute-done.35 = bf16[128,2560]{1,0:T(8,128)(2,1)S(1)} collective-permute-done((bf16[128,2560]{1,0:T(8,128)(2,1)S(1)}, bf16[128,2560]{1,0:T(8,128)(2,1)S(1)}, u32[]{:S(2)}, u32[]{:S(2)}) %collective-permute-start.35) | collective-permute-done | bytes 655392 | tf_op jit(solution)/shard_map/ppermute | solution.py:397
  659.5 3.3 collective-permute-done.36
  662.8 3.0 fusion.8
  665.9 5.1 fusion.4
  672.6 11.7 %reduce-scatter.7.cloned.1.call-done = bf16[1,3,4,160,960]{4,3,2,1,0:T(8,128)(2,1)} async-done(((bf16[4,3,4,160,960]{4,3,2,1,0:T(8,128)(2,1)}), bf16[1,3,4,160,960]{4,3,2,1,0:T(8,128)(2,1)}) %reduce-scatter.7.cloned.1.call-update) | async-done | bytes 3686416
  684.3 3.9 dynamic-slice_bitcast_fusion.2
  688.1 2.9 collective-permute-start.38
  695.0 18.0 %collective-permute-done.38.refs_4_ = bf16[3,160,960]{2,1,0:T(8,128)(2,1)S(1)} collective-permute-done((bf16[3,160,960]{2,1,0:T(8,128)(2,1)S(1)}, bf16[3,160,960]{2,1,0:T(8,128)(2,1)S(1)}, u32[]{:S(2)}, u32[]{:S(2)}) %collective-permute-start.38) | collective-permute-done | bytes 921632 | tf_op jit(solution)/shard_map/ppermute | solution.py:400
  715.5 4.3 shard_map.317.refs_2_
  722.2 4.2 shard_map.318
  736.9 8.4 shard_map.315
  752.7 7.9 collective-permute-done.39
  760.6 5.8 fusion
  769.1 9.5 %collective-permute-done.52 = bf16[4,2,48,1280]{3,2,1,0:T(8,128)(2,1)S(1)} collective-permute-done((bf16[4,2,48,1280]{3,2,1,0:T(8,128)(2,1)S(1)}, bf16[4,2,48,1280]{3,2,1,0:T(8,128)(2,1)S(1)}, u32[]{:S(2)}, u32[]{:S(2)}) %collective-permute-start.52) | collective-permute-done | bytes 983072 | tf_op jit(solution)/shard_map/ppermute | solution.py:397
  780.0 4.7 shard_map.316
  784.8 4.0 dynamic-slice_bitcast_fusion
  794.5 3.4 fusion.10
  800.1 17.2 %collective-permute-start.44 = (bf16[3,160,960]{2,1,0:T(8,128)(2,1)}, bf16[3,160,960]{2,1,0:T(8,128)(2,1)S(1)}, u32[]{:S(2)}, u32[]{:S(2)}) collective-permute-start(bf16[3,160,960]{2,1,0:T(8,128)(2,1)} %get-tuple-element.184), channel_id=1, source_target_pairs={{0,16},{2,18},{4,20},{6,22},{8,24},{10,26},{12,28},{14,30},{16,0},... | collective-permute-start | bytes 2764808 | tf_op jit(solution)/shard_map/ppermute | solution.py:400
  827.0 42.5 %collective-permute-done.44.refs_5_ = bf16[3,160,960]{2,1,0:T(8,128)(2,1)S(1)} collective-permute-done((bf16[3,160,960]{2,1,0:T(8,128)(2,1)}, bf16[3,160,960]{2,1,0:T(8,128)(2,1)S(1)}, u32[]{:S(2)}, u32[]{:S(2)}) %collective-permute-start.44) | collective-permute-done | bytes 921632 | tf_op jit(solution)/shard_map/ppermute | solution.py:400
  869.5 2.9 convert_add_fusion.2
  877.4 3.3 fusion.19
  880.7 4.2 collective-permute-done.48
  885.0 26.3 %collective-permute-done.47 = bf16[2,160,640]{2,1,0:T(8,128)(2,1)S(1)} collective-permute-done((bf16[2,160,640]{2,1,0:T(8,128)(2,1)S(1)}, bf16[2,160,640]{2,1,0:T(8,128)(2,1)S(1)}, u32[]{:S(2)}, u32[]{:S(2)}) %collective-permute-start.47) | collective-permute-done | bytes 409632 | tf_op jit(solution)/shard_map/ppermute | solution.py:400
  913.1 6.8 shard_map.319
  923.7 5.8 collective-permute-done.50
  (440 shorter events, 150.0 us)
Async XLA Ops:
  7.2 222.9 %all-gather.4.cloned.1.call-start = ((), (), s32[]{:S(2)}) async-start(), calls=%async_computation.2 | async-start | bytes 11059200 | tf_op jit(solution)/shard_map/all_gather | solution.py:495
  9.8 16.9 %collective-permute-start.7 = (bf16[160,1920]{1,0:T(8,128)(2,1)S(1)}, bf16[160,1920]{1,0:T(8,128)(2,1)S(1)}, u32[]{:S(2)}, u32[]{:S(2)}) collective-permute-start(bf16[160,1920]{1,0:T(8,128)(2,1)S(1)} %get-tuple-element.206), channel_id=1, source_target_pairs={{0,2},{2,0},{4,6},{6,4},{8,10},{10,8},{12,14},{14,12},{16,18},{18,... | collective-permute-start | bytes 1843208 | tf_op jit(solution)/shard_map/ppermute | solution.py:397
  30.2 318.7 %all-gather.6.cloned.1.call-start = ((), (), s32[]{:S(2)}) async-start(), calls=%async_computation.3 | async-start | bytes 13107200 | tf_op jit(solution)/shard_map/all_gather | solution.py:504
  32.7 24.4 %collective-permute-start = (bf16[2,160,960]{2,1,0:T(8,128)(2,1)S(1)}, bf16[2,160,960]{2,1,0:T(8,128)(2,1)S(1)}, u32[]{:S(2)}, u32[]{:S(2)}) collective-permute-start(bf16[2,160,960]{2,1,0:T(8,128)(2,1)S(1)} %get-tuple-element.80), channel_id=1, source_target_pairs={{0,8},{2,10},{4,12},{6,14},{8,16},{10,18},{12,20},{14,22},{16,24},... | collective-permute-start | bytes 1843208 | tf_op jit(solution)/shard_map/ppermute | solution.py:400
  58.0 21.2 %collective-permute-start.3 = (bf16[1,48,1280]{2,1,0:T(8,128)(2,1)S(1)}, bf16[1,48,1280]{2,1,0:T(8,128)(2,1)S(1)}, u32[]{:S(2)}, u32[]{:S(2)}) collective-permute-start(bf16[1,48,1280]{2,1,0:T(8,128)(2,1)S(1)} %fusion.51.refs_0_), channel_id=1, source_target_pairs={{0,24},{2,26},{4,28},{6,30},{8,0},{10,2},{12,4},{14,6},{16,8},{18,... | collective-permute-start | bytes 368648 | tf_op jit(solution)/shard_map/ppermute | solution.py:400
  71.6 21.5 %collective-permute-start.2 = (bf16[1,48,1280]{2,1,0:T(8,128)(2,1)S(1)}, bf16[1,48,1280]{2,1,0:T(8,128)(2,1)S(1)}, u32[]{:S(2)}, u32[]{:S(2)}) collective-permute-start(bf16[1,48,1280]{2,1,0:T(8,128)(2,1)S(1)} %fusion.51.refs_0_), channel_id=1, source_target_pairs={{0,16},{2,18},{4,20},{6,22},{8,24},{10,26},{12,28},{14,30},{16,0},... | collective-permute-start | bytes 368648 | tf_op jit(solution)/shard_map/ppermute | solution.py:400
  73.4 19.8 %collective-permute-start.1 = (bf16[1,48,1280]{2,1,0:T(8,128)(2,1)S(1)}, bf16[1,48,1280]{2,1,0:T(8,128)(2,1)S(1)}, u32[]{:S(2)}, u32[]{:S(2)}) collective-permute-start(bf16[1,48,1280]{2,1,0:T(8,128)(2,1)S(1)} %fusion.51.refs_0_), channel_id=1, source_target_pairs={{0,8},{2,10},{4,12},{6,14},{8,16},{10,18},{12,20},{14,22},{16,24},... | collective-permute-start | bytes 368648 | tf_op jit(solution)/shard_map/ppermute | solution.py:400
  93.2 8.9 collective-permute-start.4
  103.2 21.3 %collective-permute-start.5 = (bf16[2,4,48,1280]{3,2,1,0:T(8,128)(2,1)}, bf16[2,4,48,1280]{3,2,1,0:T(8,128)(2,1)}, u32[]{:S(2)}, u32[]{:S(2)}) collective-permute-start(bf16[2,4,48,1280]{3,2,1,0:T(8,128)(2,1)} %maximum_select_fusion.7), channel_id=1, source_target_pairs={{0,2},{2,0},{4,6},{6,4},{8,10},{10,8},{12,14},{14,12},{16,18},{18,... | collective-permute-start | bytes 2949128 | tf_op jit(solution)/shard_map/ppermute | solution.py:397
  104.7 19.8 %collective-permute-start.8 = (bf16[128,2560]{1,0:T(8,128)(2,1)S(1)}, bf16[128,2560]{1,0:T(8,128)(2,1)S(1)}, u32[]{:S(2)}, u32[]{:S(2)}) collective-permute-start(bf16[128,2560]{1,0:T(8,128)(2,1)S(1)} %copy-done), channel_id=1, source_target_pairs={{0,2},{2,0},{4,6},{6,4},{8,10},{10,8},{12,14},{14,12},{16,18},{18,... | collective-permute-start | bytes 1966088 | tf_op jit(solution)/shard_map/ppermute | solution.py:397
  105.2 31.0 %collective-permute-start.6 = (bf16[128,2560]{1,0:T(8,128)(2,1)S(1)}, bf16[128,2560]{1,0:T(8,128)(2,1)S(1)}, u32[]{:S(2)}, u32[]{:S(2)}) collective-permute-start(bf16[128,2560]{1,0:T(8,128)(2,1)S(1)} %copy-done), channel_id=1, source_target_pairs={{0,1},{1,0},{2,3},{3,2},{4,5},{5,4},{6,7},{7,6},{8,9},{9,8},{10,11... | collective-permute-start | bytes 1966088 | tf_op jit(solution)/shard_map/ppermute | solution.py:395
  105.2 62.4 %collective-permute-start.11 = (bf16[2,160,960]{2,1,0:T(8,128)(2,1)}, bf16[2,160,960]{2,1,0:T(8,128)(2,1)}, u32[]{:S(2)}, u32[]{:S(2)}) collective-permute-start(bf16[2,160,960]{2,1,0:T(8,128)(2,1)} %get-tuple-element.88), channel_id=1, source_target_pairs={{0,16},{2,18},{4,20},{6,22},{8,24},{10,26},{12,28},{14,30},{16,0},... | collective-permute-start | bytes 1843208 | tf_op jit(solution)/shard_map/ppermute | solution.py:400
  107.2 60.3 %collective-permute-start.12 = (bf16[2,160,960]{2,1,0:T(8,128)(2,1)}, bf16[2,160,960]{2,1,0:T(8,128)(2,1)}, u32[]{:S(2)}, u32[]{:S(2)}) collective-permute-start(bf16[2,160,960]{2,1,0:T(8,128)(2,1)} %get-tuple-element.89), channel_id=1, source_target_pairs={{0,24},{2,26},{4,28},{6,30},{8,0},{10,2},{12,4},{14,6},{16,8},{18,... | collective-permute-start | bytes 1843208 | tf_op jit(solution)/shard_map/ppermute | solution.py:400
  124.5 12.5 %collective-permute-start.9 = (bf16[128,2560]{1,0:T(8,128)(2,1)S(1)}, bf16[128,2560]{1,0:T(8,128)(2,1)S(1)}, u32[]{:S(2)}, u32[]{:S(2)}) collective-permute-start(bf16[128,2560]{1,0:T(8,128)(2,1)S(1)} %collective-permute-done.8.refs_2_), channel_id=1, source_target_pairs={{0,1},{1,0},{2,3},{3,2},{4,5},{5,4},{6,7},{7,6},{8,9},{9,8},{10,11... | collective-permute-start | bytes 1966088 | tf_op jit(solution)/shard_map/ppermute | solution.py:395
  141.5 88.7 %copy-start.14 = (bf16[512,2560]{1,0:T(8,128)(2,1)}, bf16[512,2560]{1,0:T(8,128)(2,1)S(1)}, u32[]{:S(2)}) copy-start(bf16[512,2560]{1,0:T(8,128)(2,1)S(1)} %shard_map.298.refs_0_) | copy-start | bytes 7864324
  230.1 212.9 %all-gather.8.cloned.1.call-start = ((), (), s32[]{:S(2)}) async-start(), calls=%async_computation.4 | async-start | bytes 6553600 | tf_op jit(solution)/shard_map/all_gather | solution.py:504
  236.8 28.2 %collective-permute-start.10 = (bf16[256,1280]{1,0:T(8,128)(2,1)S(1)}, bf16[256,1280]{1,0:T(8,128)(2,1)S(1)}, u32[]{:S(2)}, u32[]{:S(2)}) collective-permute-start(bf16[256,1280]{1,0:T(8,128)(2,1)S(1)} %slice.394), channel_id=1, source_target_pairs={{0,2},{2,0},{4,6},{6,4},{8,10},{10,8},{12,14},{14,12},{16,18},{18,... | collective-permute-start | bytes 1966088 | tf_op jit(solution)/shard_map/ppermute | solution.py:397
  238.6 12.6 %collective-permute-start.13 = (bf16[1,160,960]{2,1,0:T(8,128)(2,1)S(1)}, bf16[1,160,960]{2,1,0:T(8,128)(2,1)S(1)}, u32[]{:S(2)}, u32[]{:S(2)}) collective-permute-start(bf16[1,160,960]{2,1,0:T(8,128)(2,1)S(1)} %get-tuple-element.94), channel_id=1, source_target_pairs={{0,8},{2,10},{4,12},{6,14},{8,16},{10,18},{12,20},{14,22},{16,24},... | collective-permute-start | bytes 921608 | tf_op jit(solution)/shard_map/ppermute | solution.py:400
  238.6 39.2 %collective-permute-start.14 = (bf16[1,160,960]{2,1,0:T(8,128)(2,1)S(1)}, bf16[1,160,960]{2,1,0:T(8,128)(2,1)S(1)}, u32[]{:S(2)}, u32[]{:S(2)}) collective-permute-start(bf16[1,160,960]{2,1,0:T(8,128)(2,1)S(1)} %get-tuple-element.95), channel_id=1, source_target_pairs={{0,16},{2,18},{4,20},{6,22},{8,24},{10,26},{12,28},{14,30},{16,0},... | collective-permute-start | bytes 921608 | tf_op jit(solution)/shard_map/ppermute | solution.py:400
  240.0 37.9 %collective-permute-start.15 = (bf16[1,160,960]{2,1,0:T(8,128)(2,1)S(1)}, bf16[1,160,960]{2,1,0:T(8,128)(2,1)S(1)}, u32[]{:S(2)}, u32[]{:S(2)}) collective-permute-start(bf16[1,160,960]{2,1,0:T(8,128)(2,1)S(1)} %get-tuple-element.96), channel_id=1, source_target_pairs={{0,24},{2,26},{4,28},{6,30},{8,0},{10,2},{12,4},{14,6},{16,8},{18,... | collective-permute-start | bytes 921608 | tf_op jit(solution)/shard_map/ppermute | solution.py:400
  251.1 54.9 %collective-permute-start.17 = (bf16[128,2560]{1,0:T(8,128)(2,1)S(1)}, bf16[128,2560]{1,0:T(8,128)(2,1)}, u32[]{:S(2)}, u32[]{:S(2)}) collective-permute-start(bf16[128,2560]{1,0:T(8,128)(2,1)S(1)} %shard_map.302), channel_id=1, source_target_pairs={{0,8},{2,10},{4,12},{6,14},{8,16},{10,18},{12,20},{14,22},{16,24},... | collective-permute-start | bytes 1966088 | tf_op jit(solution)/shard_map/ppermute | solution.py:400
  290.5 14.4 %collective-permute-start.16 = (bf16[256,640]{1,0:T(8,128)(2,1)}, bf16[256,640]{1,0:T(8,128)(2,1)}, u32[]{:S(2)}, u32[]{:S(2)}) collective-permute-start(bf16[256,640]{1,0:T(8,128)(2,1)} %get-tuple-element.217), channel_id=1, source_target_pairs={{0,2},{2,0},{4,6},{6,4},{8,10},{10,8},{12,14},{14,12},{16,18},{18,... | collective-permute-start | bytes 983048 | tf_op jit(solution)/shard_map/ppermute | solution.py:397
  314.0 34.9 %collective-permute-start.18 = (bf16[2,128,2560]{2,1,0:T(8,128)(2,1)}, bf16[2,128,2560]{2,1,0:T(8,128)(2,1)}, u32[]{:S(2)}, u32[]{:S(2)}) collective-permute-start(bf16[2,128,2560]{2,1,0:T(8,128)(2,1)} %fusion.22), channel_id=1, source_target_pairs={{0,1},{1,0},{2,3},{3,2},{4,5},{5,4},{6,7},{7,6},{8,9},{9,8},{10,11... | collective-permute-start | bytes 3932168 | tf_op jit(solution)/shard_map/ppermute | solution.py:395
  314.1 58.5 %collective-permute-start.21 = (bf16[128,2560]{1,0:T(8,128)(2,1)S(1)}, bf16[128,2560]{1,0:T(8,128)(2,1)}, u32[]{:S(2)}, u32[]{:S(2)}) collective-permute-start(bf16[128,2560]{1,0:T(8,128)(2,1)S(1)} %shard_map.302), channel_id=1, source_target_pairs={{0,24},{2,26},{4,28},{6,30},{8,0},{10,2},{12,4},{14,6},{16,8},{18,... | collective-permute-start | bytes 1966088 | tf_op jit(solution)/shard_map/ppermute | solution.py:400
  314.1 58.5 %collective-permute-start.20 = (bf16[128,2560]{1,0:T(8,128)(2,1)S(1)}, bf16[128,2560]{1,0:T(8,128)(2,1)}, u32[]{:S(2)}, u32[]{:S(2)}) collective-permute-start(bf16[128,2560]{1,0:T(8,128)(2,1)S(1)} %shard_map.302), channel_id=1, source_target_pairs={{0,16},{2,18},{4,20},{6,22},{8,24},{10,26},{12,28},{14,30},{16,0},... | collective-permute-start | bytes 1966088 | tf_op jit(solution)/shard_map/ppermute | solution.py:400
  348.9 335.4 %reduce-scatter.7.cloned.1.call-start = ((), (), s32[]{:S(2)}) async-start(), calls=%async_computation.6 | async-start | bytes 19660800
  351.5 20.9 %collective-permute-start.19 = (bf16[128,2560]{1,0:T(8,128)(2,1)S(1)}, bf16[128,2560]{1,0:T(8,128)(2,1)S(1)}, u32[]{:S(2)}, u32[]{:S(2)}) collective-permute-start(bf16[128,2560]{1,0:T(8,128)(2,1)S(1)} %fusion.41), channel_id=1, source_target_pairs={{0,2},{2,0},{4,6},{6,4},{8,10},{10,8},{12,14},{14,12},{16,18},{18,... | collective-permute-start | bytes 1966088 | tf_op jit(solution)/shard_map/ppermute | solution.py:397
  374.1 21.6 %collective-permute-start.24 = (bf16[128,2560]{1,0:T(8,128)(2,1)S(1)}, bf16[128,2560]{1,0:T(8,128)(2,1)S(1)}, u32[]{:S(2)}, u32[]{:S(2)}) collective-permute-start(bf16[128,2560]{1,0:T(8,128)(2,1)S(1)} %shard_map.303), channel_id=1, source_target_pairs={{0,24},{2,26},{4,28},{6,30},{8,0},{10,2},{12,4},{14,6},{16,8},{18,... | collective-permute-start | bytes 1966088 | tf_op jit(solution)/shard_map/ppermute | solution.py:400
  374.2 63.5 %collective-permute-start.23 = (bf16[128,2560]{1,0:T(8,128)(2,1)S(1)}, bf16[128,2560]{1,0:T(8,128)(2,1)S(1)}, u32[]{:S(2)}, u32[]{:S(2)}) collective-permute-start(bf16[128,2560]{1,0:T(8,128)(2,1)S(1)} %shard_map.303), channel_id=1, source_target_pairs={{0,16},{2,18},{4,20},{6,22},{8,24},{10,26},{12,28},{14,30},{16,0},... | collective-permute-start | bytes 1966088 | tf_op jit(solution)/shard_map/ppermute | solution.py:400
  384.2 53.5 %collective-permute-start.22 = (bf16[128,2560]{1,0:T(8,128)(2,1)S(1)}, bf16[128,2560]{1,0:T(8,128)(2,1)S(1)}, u32[]{:S(2)}, u32[]{:S(2)}) collective-permute-start(bf16[128,2560]{1,0:T(8,128)(2,1)S(1)} %shard_map.303), channel_id=1, source_target_pairs={{0,8},{2,10},{4,12},{6,14},{8,16},{10,18},{12,20},{14,22},{16,24},... | collective-permute-start | bytes 1966088 | tf_op jit(solution)/shard_map/ppermute | solution.py:400
  387.9 50.1 %collective-permute-start.26 = (bf16[512,2560]{1,0:T(8,128)(2,1)S(1)}, bf16[512,2560]{1,0:T(8,128)(2,1)S(1)}, u32[]{:S(2)}, u32[]{:S(2)}) collective-permute-start(bf16[512,2560]{1,0:T(8,128)(2,1)S(1)} %constant_dynamic-update-slice_fusion.upstream.refs_0_), channel_id=1, source_target_pairs={{0,1},{1,0},{2,3},{3,2},{4,5},{5,4},{6,7},{7,6},{8,9},{9,8},{10,11... | collective-permute-start | bytes 7864328 | tf_op jit(solution)/shard_map/ppermute | solution.py:395
  437.9 5.1 collective-permute-start.25
  466.2 23.7 %collective-permute-start.27 = (bf16[512,2560]{1,0:T(8,128)(2,1)}, bf16[512,2560]{1,0:T(8,128)(2,1)S(1)}, u32[]{:S(2)}, u32[]{:S(2)}) collective-permute-start(bf16[512,2560]{1,0:T(8,128)(2,1)} %shard_map.308), channel_id=1, source_target_pairs={{0,1},{1,0},{2,3},{3,2},{4,5},{5,4},{6,7},{7,6},{8,9},{9,8},{10,11... | collective-permute-start | bytes 7864328 | tf_op jit(solution)/shard_map/ppermute | solution.py:395
  496.8 25.4 %collective-permute-start.28 = (bf16[128,2560]{1,0:T(8,128)(2,1)S(1)}, bf16[128,2560]{1,0:T(8,128)(2,1)S(1)}, u32[]{:S(2)}, u32[]{:S(2)}) collective-permute-start(bf16[128,2560]{1,0:T(8,128)(2,1)S(1)} %get-tuple-element.192), channel_id=1, source_target_pairs={{0,24},{2,26},{4,28},{6,30},{8,0},{10,2},{12,4},{14,6},{16,8},{18,... | collective-permute-start | bytes 1966088 | tf_op jit(solution)/shard_map/ppermute | solution.py:400
  523.1 397.1 %reduce-scatter.5.cloned.1.call-start = ((), (), s32[]{:S(2)}) async-start(), calls=%async_computation.5 | async-start | bytes 7372800 | tf_op jit(solution)/shard_map/reduce_scatter | solution.py:614
  534.9 12.7 %collective-permute-start.31 = (bf16[512,2560]{1,0:T(8,128)(2,1)}, bf16[512,2560]{1,0:T(8,128)(2,1)S(1)}, u32[]{:S(2)}, u32[]{:S(2)}) collective-permute-start(bf16[512,2560]{1,0:T(8,128)(2,1)} %shard_map.313), channel_id=1, source_target_pairs={{0,1},{1,0},{2,3},{3,2},{4,5},{5,4},{6,7},{7,6},{8,9},{9,8},{10,11... | collective-permute-start | bytes 7864328 | tf_op jit(solution)/shard_map/ppermute | solution.py:395
  535.4 23.5 %collective-permute-start.30 = (bf16[128,2560]{1,0:T(8,128)(2,1)}, bf16[128,2560]{1,0:T(8,128)(2,1)S(1)}, u32[]{:S(2)}, u32[]{:S(2)}) collective-permute-start(bf16[128,2560]{1,0:T(8,128)(2,1)} %get-tuple-element.193), channel_id=1, source_target_pairs={{0,8},{2,10},{4,12},{6,14},{8,16},{10,18},{12,20},{14,22},{16,24},... | collective-permute-start | bytes 1966088 | tf_op jit(solution)/shard_map/ppermute | solution.py:400
  535.6 74.8 %collective-permute-start.29 = (bf16[128,2560]{1,0:T(8,128)(2,1)}, bf16[128,2560]{1,0:T(8,128)(2,1)S(1)}, u32[]{:S(2)}, u32[]{:S(2)}) collective-permute-start(bf16[128,2560]{1,0:T(8,128)(2,1)} %get-tuple-element.194), channel_id=1, source_target_pairs={{0,16},{2,18},{4,20},{6,22},{8,24},{10,26},{12,28},{14,30},{16,0},... | collective-permute-start | bytes 1966088 | tf_op jit(solution)/shard_map/ppermute | solution.py:400
  551.3 59.1 %collective-permute-start.34 = (bf16[128,2560]{1,0:T(8,128)(2,1)S(1)}, bf16[128,2560]{1,0:T(8,128)(2,1)S(1)}, u32[]{:S(2)}, u32[]{:S(2)}) collective-permute-start(bf16[128,2560]{1,0:T(8,128)(2,1)S(1)} %get-tuple-element.189), channel_id=1, source_target_pairs={{0,8},{2,10},{4,12},{6,14},{8,16},{10,18},{12,20},{14,22},{16,24},... | collective-permute-start | bytes 1966088 | tf_op jit(solution)/shard_map/ppermute | solution.py:400
  556.1 68.3 %collective-permute-start.33 = (bf16[128,2560]{1,0:T(8,128)(2,1)S(1)}, bf16[128,2560]{1,0:T(8,128)(2,1)S(1)}, u32[]{:S(2)}, u32[]{:S(2)}) collective-permute-start(bf16[128,2560]{1,0:T(8,128)(2,1)S(1)} %get-tuple-element.190), channel_id=1, source_target_pairs={{0,16},{2,18},{4,20},{6,22},{8,24},{10,26},{12,28},{14,30},{16,0},... | collective-permute-start | bytes 1966088 | tf_op jit(solution)/shard_map/ppermute | solution.py:400
  556.1 68.3 %collective-permute-start.32 = (bf16[128,2560]{1,0:T(8,128)(2,1)S(1)}, bf16[128,2560]{1,0:T(8,128)(2,1)S(1)}, u32[]{:S(2)}, u32[]{:S(2)}) collective-permute-start(bf16[128,2560]{1,0:T(8,128)(2,1)S(1)} %get-tuple-element.191), channel_id=1, source_target_pairs={{0,24},{2,26},{4,28},{6,30},{8,0},{10,2},{12,4},{14,6},{16,8},{18,... | collective-permute-start | bytes 1966088 | tf_op jit(solution)/shard_map/ppermute | solution.py:400
  626.8 31.0 %collective-permute-start.35 = (bf16[128,2560]{1,0:T(8,128)(2,1)S(1)}, bf16[128,2560]{1,0:T(8,128)(2,1)S(1)}, u32[]{:S(2)}, u32[]{:S(2)}) collective-permute-start(bf16[128,2560]{1,0:T(8,128)(2,1)S(1)} %fusion.63), channel_id=1, source_target_pairs={{0,2},{2,0},{4,6},{6,4},{8,10},{10,8},{12,14},{14,12},{16,18},{18,... | collective-permute-start | bytes 1966088 | tf_op jit(solution)/shard_map/ppermute | solution.py:397
  659.4 3.4 collective-permute-start.36
  672.2 21.0 %collective-permute-start.37 = (bf16[256,640]{1,0:T(8,128)(2,1)}, bf16[256,640]{1,0:T(8,128)(2,1)}, u32[]{:S(2)}, u32[]{:S(2)}) collective-permute-start(bf16[256,640]{1,0:T(8,128)(2,1)} %slice.395), channel_id=1, source_target_pairs={{0,2},{2,0},{4,6},{6,4},{8,10},{10,8},{12,14},{14,12},{16,18},{18,... | collective-permute-start | bytes 983048 | tf_op jit(solution)/shard_map/ppermute | solution.py:397
  688.1 24.9 %collective-permute-start.38 = (bf16[3,160,960]{2,1,0:T(8,128)(2,1)S(1)}, bf16[3,160,960]{2,1,0:T(8,128)(2,1)S(1)}, u32[]{:S(2)}, u32[]{:S(2)}) collective-permute-start(bf16[3,160,960]{2,1,0:T(8,128)(2,1)S(1)} %get-tuple-element.185), channel_id=1, source_target_pairs={{0,8},{2,10},{4,12},{6,14},{8,16},{10,18},{12,20},{14,22},{16,24},... | collective-permute-start | bytes 2764808 | tf_op jit(solution)/shard_map/ppermute | solution.py:400
  714.0 8.2 collective-permute-start.40
  719.7 107.3 %collective-permute-start.45 = (bf16[3,160,960]{2,1,0:T(8,128)(2,1)}, bf16[3,160,960]{2,1,0:T(8,128)(2,1)}, u32[]{:S(2)}, u32[]{:S(2)}) collective-permute-start(bf16[3,160,960]{2,1,0:T(8,128)(2,1)} %get-tuple-element.182), channel_id=1, source_target_pairs={{0,24},{2,26},{4,28},{6,30},{8,0},{10,2},{12,4},{14,6},{16,8},{18,... | collective-permute-start | bytes 2764808 | tf_op jit(solution)/shard_map/ppermute | solution.py:400
  749.9 10.7 %collective-permute-start.39 = (bf16[256,640]{1,0:T(8,128)(2,1)S(1)}, bf16[256,640]{1,0:T(8,128)(2,1)S(1)}, u32[]{:S(2)}, u32[]{:S(2)}) collective-permute-start(bf16[256,640]{1,0:T(8,128)(2,1)S(1)} %get-tuple-element.213), channel_id=1, source_target_pairs={{0,2},{2,0},{4,6},{6,4},{8,10},{10,8},{12,14},{14,12},{16,18},{18,... | collective-permute-start | bytes 983048 | tf_op jit(solution)/shard_map/ppermute | solution.py:397
  752.1 26.4 %collective-permute-start.52 = (bf16[4,2,48,1280]{3,2,1,0:T(8,128)(2,1)S(1)}, bf16[4,2,48,1280]{3,2,1,0:T(8,128)(2,1)S(1)}, u32[]{:S(2)}, u32[]{:S(2)}) collective-permute-start(bf16[4,2,48,1280]{3,2,1,0:T(8,128)(2,1)S(1)} %fusion.37), channel_id=1, source_target_pairs={{0,2},{2,0},{4,6},{6,4},{8,10},{10,8},{12,14},{14,12},{16,18},{18,... | collective-permute-start | bytes 2949128 | tf_op jit(solution)/shard_map/ppermute | solution.py:397
  767.7 51.8 %collective-permute-start.41 = (bf16[2,128,2560]{2,1,0:T(8,128)(2,1)}, bf16[2,128,2560]{2,1,0:T(8,128)(2,1)}, u32[]{:S(2)}, u32[]{:S(2)}) collective-permute-start(bf16[2,128,2560]{2,1,0:T(8,128)(2,1)} %fusion.23), channel_id=1, source_target_pairs={{0,1},{1,0},{2,3},{3,2},{4,5},{5,4},{6,7},{7,6},{8,9},{9,8},{10,11... | collective-permute-start | bytes 3932168 | tf_op jit(solution)/shard_map/ppermute | solution.py:395
  778.8 10.3 %collective-permute-start.53 = (bf16[4,48,1280]{2,1,0:T(8,128)(2,1)S(1)}, bf16[4,48,1280]{2,1,0:T(8,128)(2,1)S(1)}, u32[]{:S(2)}, u32[]{:S(2)}) collective-permute-start(bf16[4,48,1280]{2,1,0:T(8,128)(2,1)S(1)} %fusion.43), channel_id=1, source_target_pairs={{0,4},{2,6},{4,0},{6,2},{8,12},{10,14},{12,8},{14,10},{16,20},{18,... | collective-permute-start | bytes 1474568 | tf_op jit(solution)/shard_map/ppermute | solution.py:397
  789.2 10.9 %collective-permute-start.54 = (bf16[48,1280]{1,0:T(8,128)(2,1)S(1)}, bf16[48,1280]{1,0:T(8,128)(2,1)S(1)}, u32[]{:S(2)}, u32[]{:S(2)}) collective-permute-start(bf16[48,1280]{1,0:T(8,128)(2,1)S(1)} %get-tuple-element.207), channel_id=1, source_target_pairs={{0,8},{2,10},{4,12},{6,14},{8,16},{10,18},{12,20},{14,22},{16,24},... | collective-permute-start | bytes 368648 | tf_op jit(solution)/shard_map/ppermute | solution.py:400
  791.2 26.1 %collective-permute-start.56 = (bf16[48,1280]{1,0:T(8,128)(2,1)S(1)}, bf16[48,1280]{1,0:T(8,128)(2,1)S(1)}, u32[]{:S(2)}, u32[]{:S(2)}) collective-permute-start(bf16[48,1280]{1,0:T(8,128)(2,1)S(1)} %get-tuple-element.208), channel_id=1, source_target_pairs={{0,24},{2,26},{4,28},{6,30},{8,0},{10,2},{12,4},{14,6},{16,8},{18,... | collective-permute-start | bytes 368648 | tf_op jit(solution)/shard_map/ppermute | solution.py:400
  793.1 25.7 %collective-permute-start.55 = (bf16[48,1280]{1,0:T(8,128)(2,1)S(1)}, bf16[48,1280]{1,0:T(8,128)(2,1)S(1)}, u32[]{:S(2)}, u32[]{:S(2)}) collective-permute-start(bf16[48,1280]{1,0:T(8,128)(2,1)S(1)} %get-tuple-element.209), channel_id=1, source_target_pairs={{0,16},{2,18},{4,20},{6,22},{8,24},{10,26},{12,28},{14,30},{16,0},... | collective-permute-start | bytes 368648 | tf_op jit(solution)/shard_map/ppermute | solution.py:400
  800.1 69.4 %collective-permute-start.44 = (bf16[3,160,960]{2,1,0:T(8,128)(2,1)}, bf16[3,160,960]{2,1,0:T(8,128)(2,1)S(1)}, u32[]{:S(2)}, u32[]{:S(2)}) collective-permute-start(bf16[3,160,960]{2,1,0:T(8,128)(2,1)} %get-tuple-element.184), channel_id=1, source_target_pairs={{0,16},{2,18},{4,20},{6,22},{8,24},{10,26},{12,28},{14,30},{16,0},... | collective-permute-start | bytes 2764808 | tf_op jit(solution)/shard_map/ppermute | solution.py:400
  817.3 52.2 %collective-permute-start.43 = (bf16[4,2,160,640]{3,2,1,0:T(8,128)(2,1)}, bf16[4,2,160,640]{3,2,1,0:T(8,128)(2,1)}, u32[]{:S(2)}, u32[]{:S(2)}) collective-permute-start(bf16[4,2,160,640]{3,2,1,0:T(8,128)(2,1)} %fusion.10), channel_id=1, source_target_pairs={{0,4},{2,6},{4,0},{6,2},{8,12},{10,14},{12,8},{14,10},{16,20},{18,... | collective-permute-start | bytes 4915208 | tf_op jit(solution)/shard_map/ppermute | solution.py:397
  823.5 52.1 %collective-permute-start.42 = (bf16[128,2560]{1,0:T(8,128)(2,1)}, bf16[128,2560]{1,0:T(8,128)(2,1)}, u32[]{:S(2)}, u32[]{:S(2)}) collective-permute-start(bf16[128,2560]{1,0:T(8,128)(2,1)} %fusion.42), channel_id=1, source_target_pairs={{0,2},{2,0},{4,6},{6,4},{8,10},{10,8},{12,14},{14,12},{16,18},{18,... | collective-permute-start | bytes 1966088 | tf_op jit(solution)/shard_map/ppermute | solution.py:397
  872.5 12.4 %collective-permute-start.48 = (bf16[2,160,640]{2,1,0:T(8,128)(2,1)S(1)}, bf16[2,160,640]{2,1,0:T(8,128)(2,1)S(1)}, u32[]{:S(2)}, u32[]{:S(2)}) collective-permute-start(bf16[2,160,640]{2,1,0:T(8,128)(2,1)S(1)} %get-tuple-element.186), channel_id=1, source_target_pairs={{0,24},{2,26},{4,28},{6,30},{8,0},{10,2},{12,4},{14,6},{16,8},{18,... | collective-permute-start | bytes 1228808 | tf_op jit(solution)/shard_map/ppermute | solution.py:400
  875.0 36.2 %collective-permute-start.47 = (bf16[2,160,640]{2,1,0:T(8,128)(2,1)S(1)}, bf16[2,160,640]{2,1,0:T(8,128)(2,1)S(1)}, u32[]{:S(2)}, u32[]{:S(2)}) collective-permute-start(bf16[2,160,640]{2,1,0:T(8,128)(2,1)S(1)} %get-tuple-element.187), channel_id=1, source_target_pairs={{0,16},{2,18},{4,20},{6,22},{8,24},{10,26},{12,28},{14,30},{16,0},... | collective-permute-start | bytes 1228808 | tf_op jit(solution)/shard_map/ppermute | solution.py:400
  875.0 36.2 %collective-permute-start.46 = (bf16[2,160,640]{2,1,0:T(8,128)(2,1)S(1)}, bf16[2,160,640]{2,1,0:T(8,128)(2,1)S(1)}, u32[]{:S(2)}, u32[]{:S(2)}) collective-permute-start(bf16[2,160,640]{2,1,0:T(8,128)(2,1)S(1)} %get-tuple-element.188), channel_id=1, source_target_pairs={{0,8},{2,10},{4,12},{6,14},{8,16},{10,18},{12,20},{14,22},{16,24},... | collective-permute-start | bytes 1228808 | tf_op jit(solution)/shard_map/ppermute | solution.py:400
  911.5 8.5 collective-permute-start.49
  921.5 8.1 collective-permute-start.50
  922.9 9.2 collective-permute-start.57
  931.1 2.1 collective-permute-start.51
  (107 other events, 713.1 us)
Sparse Core Ops, SparseCore 0:
  30.2 199.8 all-gather.3
  231.9 116.8 all-gather.5
  351.3 69.4 all-gather.7
  522.4 161.8 reduce-scatter.6
  726.6 153.8 reduce-scatter.4
